TPU v7x, 128 devices: a whole 4x4x4 slice. The times are simulated.
128 devices in a mesh: tile: 32 (over x, z_hi, y), sub: 4 (over z_lo, core).
Axes of the slice: x: 4, y: 4, z: 4 (z_hi: 2, z_lo: 2; z = z_hi * 2 + z_lo), core: 2. Of those that a mesh axis runs over, the one named last changes fastest.
Arguments:
- field_in: bfloat16 [12, 64, 64, 128], P('sub', 'tile'), may hold values from -6 to 6
- grad_out: bfloat16 [12, 64, 64, 128], P('sub', 'tile'), may hold values from -6 to 6
- first_weight: bfloat16 [3, 3, 128, 128], replicated, may hold values from -0.1875 to 0.1875
- second_weight: bfloat16 [3, 3, 128, 128], replicated, may hold values from -0.1875 to 0.1875
- face_neighbour: int32 [12, 4], replicated, may hold values from 0 to 11, as said below
- seam_rotation: int32 [12, 4], replicated, may hold values from 0 to 7, as said below
- corner_fill: int32 [12, 4], replicated, may hold values from 0 to 47
Outputs:
- grad_in: bfloat16 [12, 64, 64, 128], P('sub', 'tile')
- first_grad: float32 [3, 3, 128, 128], replicated
- second_grad: float32 [3, 3, 128, 128], replicated
Inputs may be any that keep to these rules, and one draw needn't show every extreme that they name: With seam_rotation: side s of face f borders side seam_rotation[f,s] % 4 of face face_neighbour[f,s], read in reverse when seam_rotation[f,s] // 4 = 1. The pairing is symmetric: that side names side s of face f back, with the same reversal; no side names itself. `seam_rotation`: see face_neighbour.
All inputs are finite; a program needn't handle non-finite values.
Results may differ from a plain program's by a relative error of at most 0.007.
Values may be sent and summed in bfloat16 or wider, within the bound.
No kernel may reach another device: no remote copies, remote signals or barrier semaphores. Data moves between devices by JAX's collectives and lax.ppermute only.
A program may use at most 64 MiB of HBM per device.

v0:
```python
import jax
import jax.numpy as jnp
from jax import lax
from jax.sharding import PartitionSpec as P


def extended(value, sides, width):
    for axis, dim in sides:
        count, length = (lax.axis_size(axis), value.shape[dim])
        up = [(i, (i + 1) % count) for i in range(count - 1)]
        down = [(j, i) for i, j in up]
        last = lax.slice_in_dim(value, length - width, length, axis=dim)
        initial = lax.slice_in_dim(value, 0, width, axis=dim)
        before = lax.ppermute(last, axis, up)
        after = lax.ppermute(initial, axis, down)
        value = jnp.concatenate([before, value, after], axis=dim)
    return value


def spread_2(value, axis, root):
    mine = lax.axis_index(axis) == root
    return lax.psum(jnp.where(mine, value, jnp.zeros_like(value)), axis)


def unfold(padded):
    height = padded.shape[0] - 2
    breadth = padded.shape[1] - 2
    pieces = [
        padded[row_shift : row_shift + height, col_shift : col_shift + breadth]
        for row_shift in range(3)
        for col_shift in range(3)
    ]
    return jnp.concatenate(pieces, axis=-1).reshape(height * breadth, -1)


def apply_taps(padded, weight):
    height = padded.shape[0] - 2
    breadth = padded.shape[1] - 2
    matrix = weight.reshape(-1, weight.shape[3])
    return jnp.dot(unfold(padded), matrix, preferred_element_type=jnp.float32).reshape(
        height, breadth, -1
    )


def weight_taps(padded, gradient):
    channels = gradient.shape[-1]
    product = lax.dot_general(
        unfold(padded),
        gradient.reshape(-1, channels),
        (((0,), (0,)), ((), ())),
        preferred_element_type=jnp.float32,
    )
    return product.reshape(3, 3, padded.shape[-1], channels)


def transpose_taps(gradient, weight):
    widened = jnp.pad(gradient, ((2, 2), (2, 2), (0, 0)))
    return apply_taps(widened, jnp.transpose(weight[::-1, ::-1], (0, 1, 3, 2)))


def sigmoid_slope(pre_act):
    logistic = jax.nn.sigmoid(pre_act)
    return logistic * (1.0 + pre_act * (1.0 - logistic))


def one_hot(indices, slot_total, value_type):
    return (indices[:, None] == jnp.arange(slot_total, dtype=jnp.int32)[None, :]).astype(value_type)


def own_rows(lookup, group_index, faces_dev):
    return lax.dynamic_slice_in_dim(lookup, group_index * faces_dev, faces_dev, 0)


def assemble(field_data, face_neighbour, seam_rotation, corner_fill):
    faces_dev, row_count, line_length, channels = field_data.shape
    band_count = lax.axis_size("tile")
    band_index = lax.axis_index("tile")
    group_index = lax.axis_index("sub")
    edge_rows = jnp.stack([field_data[:, 0], field_data[:, -1]], axis=0)
    beside = extended(edge_rows, (("tile", 0),), 1)
    row_above = beside[0]
    row_below = beside[3]
    edge_cols = jnp.stack([field_data[:, :, 0], field_data[:, :, -1]], axis=1)
    edge_full = lax.all_gather(edge_cols, "tile", axis=2, tiled=True)
    top_lines = spread_2(field_data[:, 0], "tile", 0)
    bottom_lines = spread_2(field_data[:, -1], "tile", band_count - 1)
    own_lines = jnp.stack([top_lines, bottom_lines, edge_full[:, 0], edge_full[:, 1]], axis=1)
    lines_all = lax.all_gather(own_lines, "sub", axis=0, tiled=True)
    slot_total = lines_all.shape[0] * 4
    neighbours = own_rows(face_neighbour, group_index, faces_dev)
    rotations = own_rows(seam_rotation, group_index, faces_dev)
    fills = own_rows(corner_fill, group_index, faces_dev)
    source = (neighbours * 4 + rotations % 4).reshape(-1)
    picked = jnp.dot(
        one_hot(source, slot_total, jnp.bfloat16),
        lines_all.reshape(slot_total, -1),
        preferred_element_type=jnp.float32,
    )
    picked = picked.astype(jnp.bfloat16).reshape(faces_dev, 4, line_length, channels)
    flipped = (rotations // 4 == 1)[:, :, None, None]
    picked = jnp.where(flipped, picked[:, :, ::-1], picked)
    corners = jnp.stack(
        [lines_all[:, 0, 0], lines_all[:, 0, -1], lines_all[:, 1, 0], lines_all[:, 1, -1]], axis=1
    ).reshape(slot_total, channels)
    filled = jnp.dot(
        one_hot(fills.reshape(-1), slot_total, jnp.bfloat16),
        corners,
        preferred_element_type=jnp.float32,
    )
    filled = filled.astype(jnp.bfloat16).reshape(faces_dev, 4, channels)
    left_ext = jnp.concatenate([filled[:, 0:1], picked[:, 2], filled[:, 2:3]], axis=1)
    right_ext = jnp.concatenate([filled[:, 1:2], picked[:, 3], filled[:, 3:4]], axis=1)
    row_start = band_index * row_count
    left_side = lax.dynamic_slice_in_dim(left_ext, row_start, row_count + 2, 1)
    right_side = lax.dynamic_slice_in_dim(right_ext, row_start, row_count + 2, 1)
    first_row = jnp.where(band_index == 0, picked[:, 0], row_above)
    last_row = jnp.where(band_index == band_count - 1, picked[:, 1], row_below)
    middle = jnp.concatenate([first_row[:, None], field_data, last_row[:, None]], axis=1)
    return jnp.concatenate([left_side[:, :, None], middle, right_side[:, :, None]], axis=2)


def scatter_back(full_grad, face_neighbour, seam_rotation, corner_fill):
    faces_dev = full_grad.shape[0]
    row_count = full_grad.shape[1] - 2
    line_length = full_grad.shape[2] - 2
    channels = full_grad.shape[3]
    faces_all = faces_dev * lax.axis_size("sub")
    slot_total = faces_all * 4
    band_count = lax.axis_size("tile")
    band_index = lax.axis_index("tile")
    group_index = lax.axis_index("sub")
    first_band = band_index == 0
    last_band = band_index == band_count - 1
    interior = full_grad[:, 1:-1, 1:-1]
    zeros_line = jnp.zeros_like(full_grad[:, 0, 1:-1])
    upper_grad = jnp.where(first_band, zeros_line, full_grad[:, 0, 1:-1])
    lower_grad = jnp.where(last_band, zeros_line, full_grad[:, -1, 1:-1])
    beside = extended(jnp.stack([upper_grad, lower_grad], axis=0), (("tile", 0),), 1)
    interior = interior.at[:, 0].add(beside[0]).at[:, -1].add(beside[3])
    row_start = band_index * row_count
    empty_ext = jnp.zeros((faces_dev, line_length + 2, channels), jnp.float32)
    left_part = lax.dynamic_update_slice_in_dim(empty_ext, full_grad[:, :, 0], row_start, 1)
    right_part = lax.dynamic_update_slice_in_dim(empty_ext, full_grad[:, :, -1], row_start, 1)
    top_part = jnp.where(first_band, full_grad[:, 0, 1:-1], zeros_line)
    bottom_part = jnp.where(last_band, full_grad[:, -1, 1:-1], zeros_line)
    neighbours = own_rows(face_neighbour, group_index, faces_dev)
    rotations = own_rows(seam_rotation, group_index, faces_dev)
    fills = own_rows(corner_fill, group_index, faces_dev)
    flipped = (rotations // 4 == 1)[:, :, None, None]
    source = (neighbours * 4 + rotations % 4).reshape(-1)
    left_sum, right_sum, top_sum, bottom_sum = (
        lax.psum(left_part.astype(jnp.bfloat16), "tile").astype(jnp.float32),
        lax.psum(right_part.astype(jnp.bfloat16), "tile").astype(jnp.float32),
        lax.psum(top_part.astype(jnp.bfloat16), "tile").astype(jnp.float32),
        lax.psum(bottom_part.astype(jnp.bfloat16), "tile").astype(jnp.float32),
    )
    line_grads = jnp.stack([top_sum, bottom_sum, left_sum[:, 1:-1], right_sum[:, 1:-1]], axis=1)
    corner_grads = jnp.stack(
        [left_sum[:, 0], right_sum[:, 0], left_sum[:, -1], right_sum[:, -1]], axis=1
    )
    line_grads = jnp.where(flipped, line_grads[:, :, ::-1], line_grads)
    spread = jnp.dot(
        one_hot(source, slot_total, jnp.float32).T,
        line_grads.reshape(faces_dev * 4, -1),
        precision=lax.Precision.HIGHEST,
        preferred_element_type=jnp.float32,
    )
    corner_spread = jnp.dot(
        one_hot(fills.reshape(-1), slot_total, jnp.float32).T,
        corner_grads.reshape(faces_dev * 4, channels),
        precision=lax.Precision.HIGHEST,
        preferred_element_type=jnp.float32,
    )
    owned, corner_owned = (
        lax.psum_scatter(
            spread.astype(jnp.bfloat16), "sub", scatter_dimension=0, tiled=True
        ).astype(jnp.float32),
        lax.psum_scatter(
            corner_spread.astype(jnp.bfloat16), "sub", scatter_dimension=0, tiled=True
        ).astype(jnp.float32),
    )
    owned = owned.reshape(faces_dev, 4, line_length, channels)
    corner_owned = corner_owned.reshape(faces_dev, 4, channels)
    interior = interior.at[:, 0].add(jnp.where(first_band, owned[:, 0], 0.0))
    interior = interior.at[:, -1].add(jnp.where(last_band, owned[:, 1], 0.0))
    interior = interior.at[:, :, 0].add(
        lax.dynamic_slice_in_dim(owned[:, 2], row_start, row_count, 1)
    )
    interior = interior.at[:, :, -1].add(
        lax.dynamic_slice_in_dim(owned[:, 3], row_start, row_count, 1)
    )
    interior = interior.at[:, 0, 0].add(jnp.where(first_band, corner_owned[:, 0], 0.0))
    interior = interior.at[:, 0, -1].add(jnp.where(first_band, corner_owned[:, 1], 0.0))
    interior = interior.at[:, -1, 0].add(jnp.where(last_band, corner_owned[:, 2], 0.0))
    return interior.at[:, -1, -1].add(jnp.where(last_band, corner_owned[:, 3], 0.0))


def body(
    field_in, grad_out, first_weight, second_weight, face_neighbour, seam_rotation, corner_fill
):
    faces_all = field_in.shape[0] * lax.axis_size("sub")
    line_length = field_in.shape[2]
    factor = (1.0 * faces_all * line_length * line_length) ** (-0.5)
    padded_in = assemble(field_in, face_neighbour, seam_rotation, corner_fill)
    pre_act = lax.map(lambda one_face: apply_taps(one_face, first_weight), padded_in)
    hidden = jax.nn.silu(pre_act).astype(jnp.bfloat16)
    padded_hidden = assemble(hidden, face_neighbour, seam_rotation, corner_fill)
    second_local = jnp.sum(
        lax.map(
            lambda item_pair: weight_taps(item_pair[0], item_pair[1]), (padded_hidden, grad_out)
        ),
        axis=0,
    )
    back_hidden = lax.map(lambda one_face: transpose_taps(one_face, second_weight), grad_out)
    grad_hidden = scatter_back(back_hidden, face_neighbour, seam_rotation, corner_fill)
    grad_pre = (grad_hidden * sigmoid_slope(pre_act)).astype(jnp.bfloat16)
    first_local = jnp.sum(
        lax.map(lambda item_pair: weight_taps(item_pair[0], item_pair[1]), (padded_in, grad_pre)),
        axis=0,
    )
    back_in = lax.map(lambda one_face: transpose_taps(one_face, first_weight), grad_pre)
    grad_in = (
        grad_out.astype(jnp.float32)
        + scatter_back(back_in, face_neighbour, seam_rotation, corner_fill)
    ).astype(jnp.bfloat16)
    first_total, second_total = lax.psum((first_local, second_local), ("tile", "sub"))
    return (grad_in, first_total * factor, second_total * factor)


def solution(mesh):
    return jax.shard_map(
        body,
        mesh=mesh,
        in_specs=(
            P("sub", "tile", None, None),
            P("sub", "tile", None, None),
            P(),
            P(),
            P(),
            P(),
            P(),
        ),
        out_specs=(P("sub", "tile", None, None), P(), P()),
        check_vma=False,
    )
```

profile of v0, /device:TPU:1, one launch (start us, length us, event | category | flops | bytes accessed | tf_op | source)
XLA Modules:
  0.0 1070.2 jit_solution(9784375088118563498)
XLA Ops:
  7.2 1.2 copy.798
  8.5 4.4 while.74
  8.5 0.8 dynamic-slice_bitcast_fusion.10
  9.9 0.8 dynamic-slice_bitcast_fusion.10
  11.4 0.8 dynamic-slice_bitcast_fusion.10
  13.0 4.2 collective-permute-start
  17.4 1.3 collective-permute-start.1
  18.7 1.3 collective-permute-start.3
  20.0 4.6 collective-permute-start.2
  25.4 0.7 fusion.31
  28.6 81.2 %all_gather.12 = bf16[3,2,64,128]{3,1,0,2:T(2,128)(2,1)S(1)} all-gather(bf16[3,2,2,128]{3,1,0,2:T(2,128)(2,1)S(1)} %copy.823), channel_id=1, replica_groups=mesh['tile'=32,'sub'=4] {'tile'}, dimensions={2}, use_global_device_ids=true | all-gather | bytes 101376 | tf_op jit(solution)/shard_map/all_gather | solution.py:84
  111.3 0.7 and_reduce_fusion
  112.7 2.0 scatter-add.66
  114.8 2.0 scatter-add.69
  116.8 236.7 %all-reduce.23.cloned.1.call-done = (bf16[3,66,128]{2,1,0:T(8,128)(2,1)}, bf16[3,66,128]{2,1,0:T(8,128)(2,1)}, bf16[3,1,64,128]{3,2,0,1:T(8,128)(2,1)}, bf16[3,1...) async-done(((bf16[3,66,128]{2,1,0:T(8,128)(2,1)}, bf16[3,66,128]{2,1,0:T(8,128)(2,1)}, bf16[3,1,64,128]{3,2,0,1:T(8,128)(2,1)}, ...) | async-done | bytes 298000 | tf_op jit(solution)/shard_map/psum | solution.py:153
  353.5 0.9 copy.825
  354.4 0.9 copy.824
  355.6 26.6 %all_gather.13 = bf16[12,4,64,128]{3,2,1,0:T(8,128)(2,1)S(1)} all-gather(bf16[3,4,64,128]{3,2,1,0:T(8,128)(2,1)S(1)} %copy.826), channel_id=1, replica_groups=mesh['tile'=32,'sub'=4] {'sub'}, dimensions={0}, use_global_device_ids=true | all-gather | bytes 983040 | tf_op jit(solution)/shard_map/all_gather | solution.py:88
  383.7 1.6 while.75
  387.1 0.9 convolution_convert_fusion.1
  388.3 12.9 %fusion.95 = (bf16[16,8192]{1,0:T(8,128)(2,1)S(1)}, bf16[16,128]{1,0:T(8,128)(2,1)S(1)}) fusion(bf16[48,8192]{1,0:T(8,128)(2,1)S(1)} %convolution_convert_fusion.1, bf16[48,128]{1,0:T(8,128)(2,1)S(1)} %convolution_convert_fusion.5), kind=kCustom, calls=%all-reduce-scatter.5 | all-reduce-scatter fusion | flops 532481 | bytes 1065472
  401.3 4.3 collective-permute-start.8
  405.6 1.9 collective-permute-start.9
  407.6 82.4 %all_gather.14 = bf16[3,2,64,128]{3,1,0,2:T(2,128)(2,1)} all-gather(bf16[3,2,2,128]{3,1,0,2:T(2,128)(2,1)S(1)} %copy.874), channel_id=1, replica_groups=mesh['tile'=32,'sub'=4] {'tile'}, dimensions={2}, use_global_device_ids=true | all-gather | bytes 101376 | tf_op jit(solution)/shard_map/all_gather | solution.py:84
  490.0 1.3 collective-permute-start.7
  491.3 4.6 collective-permute-start.6
  497.2 2.0 scatter-add.70
  499.4 2.0 scatter-add.71
  501.5 1.9 broadcast_select_fusion.19
  503.4 1.3 scatter-add.79
  505.3 2.1 while.76
  507.6 0.8 copy.850
  508.4 0.9 broadcast_select_fusion.5
  509.2 0.9 fusion.32
  510.1 1.3 collective-permute-start.4
  511.4 1.3 collective-permute-start.5
  512.9 7.0 while.77
  512.9 0.9 dynamic-slice_bitcast_fusion.13
  514.3 0.8 constant_dynamic-slice_fusion.15
  515.3 0.9 dynamic-slice_bitcast_fusion.13
  516.6 0.8 constant_dynamic-slice_fusion.15
  517.6 0.9 dynamic-slice_bitcast_fusion.13
  519.0 0.8 constant_dynamic-slice_fusion.15
  521.0 1.0 reduce_sum.18
  522.1 331.2 %all-reduce.21.cloned.1.call-done = (bf16[3,66,128]{2,1,0:T(8,128)(2,1)}, bf16[3,66,128]{2,1,0:T(8,128)(2,1)}, bf16[3,1,64,128]{3,1,2,0:T(2,128)(2,1)}, bf16[3,1...) async-done(((bf16[3,66,128]{2,1,0:T(8,128)(2,1)}, bf16[3,66,128]{2,1,0:T(8,128)(2,1)}, bf16[3,1,64,128]{3,1,2,0:T(2,128)(2,1)}, ...) | async-done | bytes 298000 | tf_op jit(solution)/shard_map/psum | solution.py:152
  853.3 0.8 slice.1141
  854.1 0.7 fusion.103
  854.9 0.8 slice.1139
  855.7 0.7 fusion.102
  856.4 1.0 stack.100
  857.4 1.0 stack.98
  859.4 0.9 convolution_convert_fusion
  860.6 31.3 %fusion.94 = (bf16[16,8192]{1,0:T(8,128)(2,1)S(1)}, bf16[16,128]{1,0:T(8,128)(2,1)S(1)}) fusion(bf16[48,8192]{1,0:T(8,128)(2,1)S(1)} %convolution_convert_fusion, bf16[48,128]{1,0:T(8,128)(2,1)S(1)} %convolution_convert_fusion.4), kind=kCustom, calls=%all-reduce-scatter.4 | all-reduce-scatter fusion | flops 532481 | bytes 1065472
  892.0 4.3 collective-permute-start.10
  896.3 1.9 collective-permute-start.11
  898.8 8.7 all_gather.15
  908.7 0.8 slice_bitcast_fusion.4
  910.0 2.1 while.78
  912.1 1.0 reduce_sum.19
  915.5 1.9 fusion.92
  917.4 1.3 scatter-add.95
  919.5 140.2 %all-reduce.19.cloned.1.call-done = (f32[3,3,128,128]{3,2,1,0:T(8,128)}, f32[3,3,128,128]{3,2,1,0:T(8,128)}) async-done(((f32[3,3,128,128]{3,2,1,0:T(8,128)}, f32[3,3,128,128]{3,2,1,0:T(8,128)}), (f32[3,3,128,128]{3,2,1,0:T(8,128)}, f32[3,3,128,128]{3,2,1,0:T(8,128)})) %all-reduce.19.cloned.1.call-update) | async-done | bytes 1179664 | tf_op jit(solution)/shard_map/psum | solution.py:226
  1059.8 1.9 broadcast_multiply_fusion.1
  1061.7 1.9 broadcast_multiply_fusion
  (426 shorter events, 27.5 us)
Async XLA Ops:
  7.2 21.1 %copy-start = (s32[12,4]{0,1:T(4,128)S(1)}, s32[12,4]{0,1:T(4,128)}, u32[]{:S(2)}) copy-start(s32[12,4]{0,1:T(4,128)} %param.63) | copy-start | bytes 580
  7.2 346.3 %all-reduce.23.cloned.1.call-start = ((), (), s32[]{:S(2)}) async-start(), calls=%async_computation.2 | async-start | bytes 712704 | tf_op jit(solution)/shard_map/psum | solution.py:153
  8.4 10.2 copy-start.9
  12.9 15.0 %copy-start.7 = (f32[3,1,64,128]{3,1,2,0:T(1,128)}, f32[3,1,64,128]{3,1,2,0:T(1,128)S(1)}, u32[]{:S(2)}) copy-start(f32[3,1,64,128]{3,1,2,0:T(1,128)S(1)} %broadcast.529) | copy-start | bytes 294916
  12.9 15.0 %copy-start.23 = (s32[12,4]{0,1:T(4,128)S(1)}, s32[12,4]{0,1:T(4,128)}, u32[]{:S(2)}) copy-start(s32[12,4]{0,1:T(4,128)} %param.62) | copy-start | bytes 580
  12.9 15.1 %copy-start.24 = (s32[12,4]{0,1:T(4,128)S(1)}, s32[12,4]{0,1:T(4,128)}, u32[]{:S(2)}) copy-start(s32[12,4]{0,1:T(4,128)} %param.61) | copy-start | bytes 580
  13.0 96.8 %copy-start.1 = (bf16[3,3,128,128]{3,2,1,0:T(8,128)(2,1)S(1)}, bf16[3,3,128,128]{3,2,1,0:T(8,128)(2,1)}, u32[]{:S(2)}) copy-start(bf16[3,3,128,128]{3,2,1,0:T(8,128)(2,1)} %param.59) | copy-start | bytes 884740
  13.0 99.7 %collective-permute-start = (f32[1,3,64,128]{3,2,1,0:T(8,128)S(1)}, f32[1,3,64,128]{3,2,1,0:T(8,128)S(1)}, u32[]{:S(2)}, u32[]{:S(2)}) collective-permute-start(f32[1,3,64,128]{3,2,1,0:T(8,128)S(1)} %select_bitcast_fusion), channel_id=1, source_target_pairs={{0,4},{4,8},{8,12},{12,16},{16,20},{20,24},{24,28},{28,32},{32,36}... | collective-permute-start | bytes 294920 | tf_op jit(solution)/shard_map/ppermute | solution.py:14
  17.3 92.9 %copy-start.25 = (u32[128]{0:T(128)S(1)}, u32[128]{0:T(128)}, u32[]{:S(2)}) copy-start(u32[128]{0:T(128)} %constant.627) | copy-start | bytes 1540
  17.3 94.0 %copy-start.26 = (s32[4]{0:T(128)S(1)}, s32[4]{0:T(128)}, u32[]{:S(2)}) copy-start(s32[4]{0:T(128)} %constant.614.clone.1) | copy-start | bytes 52
  17.4 97.2 %collective-permute-start.1 = (f32[1,3,64,128]{3,2,1,0:T(8,128)S(1)}, f32[1,3,64,128]{3,2,1,0:T(8,128)S(1)}, u32[]{:S(2)}, u32[]{:S(2)}) collective-permute-start(f32[1,3,64,128]{3,2,1,0:T(8,128)S(1)} %bitcast.435), channel_id=1, source_target_pairs={{4,0},{8,4},{12,8},{16,12},{20,16},{24,20},{28,24},{32,28},{36,32}... | collective-permute-start | bytes 294920 | tf_op jit(solution)/shard_map/ppermute | solution.py:15
  18.7 364.8 %collective-permute-start.3 = (bf16[1,3,64,128]{3,2,1,0:T(8,128)(2,1)S(1)}, bf16[1,3,64,128]{3,2,1,0:T(8,128)(2,1)S(1)}, u32[]{:S(2)}, u32[]{:S(2)}) collective-permute-start(bf16[1,3,64,128]{3,2,1,0:T(8,128)(2,1)S(1)} %get-tuple-element.711), channel_id=1, source_target_pairs={{4,0},{8,4},{12,8},{16,12},{20,16},{24,20},{28,24},{32,28},{36,32}... | collective-permute-start | bytes 147464 | tf_op jit(solution)/shard_map/ppermute | solution.py:15
  20.0 363.5 %collective-permute-start.2 = (bf16[1,3,64,128]{3,2,1,0:T(8,128)(2,1)S(1)}, bf16[1,3,64,128]{3,2,1,0:T(8,128)(2,1)S(1)}, u32[]{:S(2)}, u32[]{:S(2)}) collective-permute-start(bf16[1,3,64,128]{3,2,1,0:T(8,128)(2,1)S(1)} %get-tuple-element.710), channel_id=1, source_target_pairs={{0,4},{4,8},{8,12},{12,16},{16,20},{20,24},{24,28},{28,32},{32,36}... | collective-permute-start | bytes 147464 | tf_op jit(solution)/shard_map/ppermute | solution.py:14
  26.9 0.6 copy-start.15
  27.1 0.6 copy-start.16
  27.7 825.6 %all-reduce.21.cloned.1.call-start = ((), (), s32[]{:S(2)}) async-start(), calls=%async_computation.1 | async-start | bytes 811008 | tf_op jit(solution)/shard_map/psum | solution.py:152
  382.3 1.1 copy-start.18
  382.3 1.1 copy-start.19
  383.7 2.6 copy-start.20
  383.7 2.6 copy-start.17
  385.4 1.3 copy-start.2
  385.6 0.9 copy-start.10
  401.3 94.8 %collective-permute-start.8 = (bf16[12,8192]{1,0:T(8,128)(2,1)S(1)}, bf16[12,8192]{1,0:T(8,128)(2,1)S(1)}, u32[]{:S(2)}, u32[]{:S(2)}) collective-permute-start(bf16[12,8192]{1,0:T(8,128)(2,1)S(1)} %slice.1176), channel_id=1, source_target_pairs={{0,1},{1,2},{2,3},{4,5},{5,6},{6,7},{8,9},{9,10},{10,11},{12,13},{... | collective-permute-start | bytes 589832
  405.6 90.3 %collective-permute-start.9 = (bf16[12,128]{1,0:T(8,128)(2,1)S(1)}, bf16[12,128]{1,0:T(8,128)(2,1)S(1)}, u32[]{:S(2)}, u32[]{:S(2)}) collective-permute-start(bf16[12,128]{1,0:T(8,128)(2,1)S(1)} %slice.1177), channel_id=1, source_target_pairs={{0,1},{1,2},{2,3},{4,5},{5,6},{6,7},{8,9},{9,10},{10,11},{12,13},{... | collective-permute-start | bytes 9224
  490.0 418.7 %collective-permute-start.7 = (bf16[1,3,64,128]{3,2,1,0:T(8,128)(2,1)}, bf16[1,3,64,128]{3,2,1,0:T(8,128)(2,1)}, u32[]{:S(2)}, u32[]{:S(2)}) collective-permute-start(bf16[1,3,64,128]{3,2,1,0:T(8,128)(2,1)} %get-tuple-element.705), channel_id=1, source_target_pairs={{4,0},{8,4},{12,8},{16,12},{20,16},{24,20},{28,24},{32,28},{36,32}... | collective-permute-start | bytes 147464 | tf_op jit(solution)/shard_map/ppermute | solution.py:15
  491.3 417.4 %collective-permute-start.6 = (bf16[1,3,64,128]{3,2,1,0:T(8,128)(2,1)S(1)}, bf16[1,3,64,128]{3,2,1,0:T(8,128)(2,1)}, u32[]{:S(2)}, u32[]{:S(2)}) collective-permute-start(bf16[1,3,64,128]{3,2,1,0:T(8,128)(2,1)S(1)} %get-tuple-element.704), channel_id=1, source_target_pairs={{0,4},{4,8},{8,12},{12,16},{16,20},{20,24},{24,28},{28,32},{32,36}... | collective-permute-start | bytes 147464 | tf_op jit(solution)/shard_map/ppermute | solution.py:14
  507.4 2.7 copy-start.5
  510.1 12.0 %collective-permute-start.4 = (f32[1,3,64,128]{3,2,1,0:T(8,128)}, f32[1,3,64,128]{3,2,1,0:T(8,128)S(1)}, u32[]{:S(2)}, u32[]{:S(2)}) collective-permute-start(f32[1,3,64,128]{3,2,1,0:T(8,128)} %bitcast.68), channel_id=1, source_target_pairs={{0,4},{4,8},{8,12},{12,16},{16,20},{20,24},{24,28},{28,32},{32,36}... | collective-permute-start | bytes 294920 | tf_op jit(solution)/shard_map/ppermute | solution.py:14
  511.4 10.7 collective-permute-start.5
  520.8 1.2 copy-start.13
  521.0 1.0 copy-start.14
  522.0 537.8 %all-reduce.19.cloned.1.call-start = ((), (), s32[]{:S(2)}) async-start(), calls=%async_computation | async-start | bytes 2359296 | tf_op jit(solution)/shard_map/psum | solution.py:226
  522.1 336.9 %copy-start.3 = (f32[3,2,64,128]{3,2,0,1:T(8,128)}, f32[3,2,64,128]{3,2,0,1:T(8,128)S(1)}, u32[]{:S(2)}) copy-start(f32[3,2,64,128]{3,2,0,1:T(8,128)S(1)} %fusion.39) | copy-start | bytes 589828
  859.0 39.2 %copy-start.22 = (bf16[3,1,64,128]{3,2,0,1:T(8,128)(2,1)S(1)}, bf16[3,1,64,128]{3,2,0,1:T(8,128)(2,1)}, u32[]{:S(2)}) copy-start(bf16[3,1,64,128]{3,2,0,1:T(8,128)(2,1)} %get-tuple-element.657) | copy-start | bytes 147460
  859.4 39.0 %copy-start.21 = (bf16[3,1,64,128]{3,2,0,1:T(8,128)(2,1)S(1)}, bf16[3,1,64,128]{3,2,0,1:T(8,128)(2,1)}, u32[]{:S(2)}) copy-start(bf16[3,1,64,128]{3,2,0,1:T(8,128)(2,1)} %get-tuple-element.658) | copy-start | bytes 147460
  859.4 39.1 %copy-start.12 = (bf16[3,2,64,128]{3,1,0,2:T(2,128)(2,1)S(1)}, bf16[3,2,64,128]{3,1,0,2:T(2,128)(2,1)}, u32[]{:S(2)}) copy-start(bf16[3,2,64,128]{3,1,0,2:T(2,128)(2,1)} %all_gather.14) | copy-start | bytes 294916
  892.0 21.4 %collective-permute-start.10 = (bf16[12,8192]{1,0:T(8,128)(2,1)S(1)}, bf16[12,8192]{1,0:T(8,128)(2,1)S(1)}, u32[]{:S(2)}, u32[]{:S(2)}) collective-permute-start(bf16[12,8192]{1,0:T(8,128)(2,1)S(1)} %slice.1178), channel_id=1, source_target_pairs={{0,1},{1,2},{2,3},{4,5},{5,6},{6,7},{8,9},{9,10},{10,11},{12,13},{... | collective-permute-start | bytes 589832
  896.3 16.8 %collective-permute-start.11 = (bf16[12,128]{1,0:T(8,128)(2,1)S(1)}, bf16[12,128]{1,0:T(8,128)(2,1)S(1)}, u32[]{:S(2)}, u32[]{:S(2)}) collective-permute-start(bf16[12,128]{1,0:T(8,128)(2,1)S(1)} %slice.1179), channel_id=1, source_target_pairs={{0,1},{1,2},{2,3},{4,5},{5,6},{6,7},{8,9},{9,10},{10,11},{12,13},{... | collective-permute-start | bytes 9224
  907.9 1.8 copy-start.11
  908.6 1.4 copy-start.6
  914.1 0.9 copy-start.4
  914.1 1.0 copy-start.8
Sparse Core Ops, SparseCore 0:
  27.9 325.5 all-reduce.22
  522.1 331.1 all-reduce.20
  913.3 146.4 all-reduce.18
where the time goes:
time: 1070 us
  waiting for transfers between devices  708 us (66%)
  blocking collectives  243 us (23%)
  local copies, waits for them, and re-layouts  40 us (4%)
  starting transfers between devices  32.5 us (3%)
  other arithmetic  21.3 us (2%)
  between operations  16.1 us (2%)
    psum x1, waiting for transfers between devices, scatter_back(): lax.psum(left_part.astype(jnp.bfloat16), 'tile').astype(jnp.float32)  331 us
    psum x1, waiting for transfers between devices, scatter_back(): lax.psum(right_part.astype(jnp.bfloat16), 'tile').astype(jnp.float32)  237 us
    all_gather x2, blocking collectives, assemble(): edge_full = lax.all_gather(edge_cols, 'tile', axis=2, tiled=True)  164 us
    psum x1, waiting for transfers between devices, body(): lax.psum((first_local, second_local), ('tile', 'sub'))  140 us
    unnamed x2, blocking collectives  44.1 us
    all_gather x2, blocking collectives, assemble(): lines_all = lax.all_gather(own_lines, 'sub', axis=0, tiled=True)  35.3 us
  transfers between devices with their start and end apart: 15, of which 3 were waited for; matrix products, arithmetic and copies ran while one was open for 8% of the time, Pallas kernels for 0%

commit v1 on v0

v1 whole, which is shorter than its diff:
```python
import jax
import jax.numpy as jnp
import numpy as np
from jax import lax
from jax.experimental import pallas as pl
from jax.experimental.pallas import tpu as pltpu
from jax.sharding import PartitionSpec as P

BF = jnp.bfloat16
F32 = jnp.float32
I32 = jnp.int32
BOTH = ("tile", "sub")
BANDS = 32
GROUPS = 4
SPAN = 64
CH = 128
TAPS = [(a, b) for a in range(3) for b in range(3)]
POSITIONS = 10
ROWS_BLOCK = POSITIONS * 16
SLOT_ONE = ROWS_BLOCK + 48
CHUNK = 18
SLOT_TWO = 24
VMEM_BYTES = 48 * 1024 * 1024


def mm(left, right):
    return jnp.dot(left, right, preferred_element_type=F32)


def mm_t(left, right):
    return lax.dot_general(left, right, (((0,), (0,)), ((), ())), preferred_element_type=F32)


def call(kernel, outs, scratch, operands, smem_first=False):
    specs = [pl.BlockSpec(memory_space=pltpu.VMEM) for _ in operands]
    if smem_first:
        specs[0] = pl.BlockSpec(memory_space=pltpu.SMEM)
    many = isinstance(outs, (list, tuple))
    out_specs = [pl.BlockSpec(memory_space=pltpu.VMEM) for _ in outs] if many else pl.BlockSpec(memory_space=pltpu.VMEM)
    return pl.pallas_call(
        kernel,
        out_shape=outs,
        in_specs=specs,
        out_specs=out_specs,
        scratch_shapes=scratch,
        compiler_params=pltpu.CompilerParams(vmem_limit_bytes=VMEM_BYTES),
    )(*operands)


def pack_lines(f_ref, g_ref, out_ref, wide, ends):
    wide[...] = jnp.zeros_like(wide)
    for fld, ref in enumerate((f_ref, g_ref)):
        for row in range(2):
            for face in range(3):
                block = ref[face, row].astype(F32)
                wide[pl.ds(fld * 6 + row * 3 + face, SPAN, stride=16), :] = block
                for side, cols in enumerate(((0, 1), (63, 62))):
                    for depth, col in enumerate(cols):
                        place = row * 24 + fld * 12 + side * 6 + depth * 3 + face
                        ends[place : place + 1, :] = block[col : col + 1, :]
    tail = ends[...].astype(BF)
    for pos in range(SPAN):
        block = wide[pos * 16 : pos * 16 + 16, :].astype(BF)
        for d in range(BANDS):
            for j in range(POSITIONS):
                t = min(max(d - 2 + j if j < 5 else 56 - d + j, 0), SPAN - 1)
                if t == pos:
                    out_ref[d, j * 16 : j * 16 + 16, :] = block
    for d in range(BANDS):
        out_ref[d, ROWS_BLOCK:SLOT_ONE, :] = tail


def line_selector():
    select = np.zeros((2, 64, 80), np.float32)
    for parity in range(2):
        for fld in range(2):
            for depth in range(2):
                for face in range(3):
                    base = (fld * 2 + depth) * 16 + face
                    select[parity, base, fld * 6 + depth * 3 + face] = 1
                    select[parity, base + 3, 16 + fld * 6 + (1 - depth) * 3 + face] = 1
                    for side in range(2):
                        source = 32 + parity * 24 + fld * 12 + side * 6 + depth * 3 + face
                        select[parity, base + 6 + 3 * side, source] = 1
    return select


def gather_lines(sc_ref, sel_ref, in_ref, out_ref):
    band = sc_ref[0]
    for j in range(POSITIONS):
        t = band - 2 + j if j < 5 else 56 - band + j
        inside = jnp.logical_and(t >= 0, t < SPAN)
        t = jnp.clip(t, 0, SPAN - 1)
        ends = in_ref[t >> 1, ROWS_BLOCK:SLOT_ONE, :]
        rows = slice(j * 16, j * 16 + 16)
        pieces = jnp.concatenate([in_ref[0, rows, :], in_ref[BANDS - 1, rows, :], ends], axis=0)
        picked = mm(sel_ref[t & 1], pieces)
        out_ref[j] = jnp.where(inside, picked, 0.0).astype(BF)


def silu_parts(pre):
    logistic = 1.0 / (1.0 + jnp.exp(-pre))
    return pre * logistic, logistic * (1.0 + pre * (1.0 - logistic))


def side_frame(side, tap):
    dr, dc = tap[0] - 1, tap[1] - 1
    return ((dr, dc), (-dr, dc), (dc, dr), (-dc, dr))[side]


def main_kernel(
    sc_ref, idx_ref, a_ref, f_ref, fu_ref, fd_ref, g_ref, gu_ref, gd_ref, w1_ref, w2_ref,
    out_ref, gin_ref,
    f2, g2, w1t, w2t, xs, hal, lp, lg, lc, ob, ss, gp, gpu, acc,
):
    band = sc_ref[0]
    group = sc_ref[1]

    for k, (a, b) in enumerate(TAPS):
        w1t[k * CH : (k + 1) * CH, :] = w1_ref[a, b].T
        w2t[k * CH : (k + 1) * CH, :] = w2_ref[a, b].T

    for row in range(2):
        for face in range(3):
            for part, (fr, gr) in enumerate(((fu_ref, gu_ref), (f_ref, g_ref), (fd_ref, gd_ref))):
                start = (part * 2 + row) * 192 + face * 64
                f2[start : start + 64, :] = fr[face, row]
                g2[start : start + 64, :] = gr[face, row]

    def conv_weights(ref):
        return jnp.concatenate([ref[:, b].reshape(3 * CH, CH) for b in range(3)], axis=1)

    def back_weights(ref):
        columns = []
        for b in range(3):
            columns.append(jnp.concatenate([ref[(a * 3 + b) * CH : (a * 3 + b + 1) * CH, :] for a in (2, 1, 0)], axis=0))
        return jnp.concatenate(columns, axis=1)

    def up_one(value):
        return pltpu.roll(value, value.shape[0] - 1, 0)

    def down_one(value):
        return pltpu.roll(value, 1, 0)

    def three_rows(ref, first, count):
        return jnp.concatenate([ref[first + 192 * a : first + 192 * a + count, :] for a in range(3)], axis=1)

    y = mm(three_rows(f2, 0, 768), conv_weights(w1_ref))
    pre = down_one(y[:, :CH]) + y[:, CH : 2 * CH] + up_one(y[:, 2 * CH :])
    z = mm(three_rows(g2, 0, 768), back_weights(w2t))
    back = up_one(z[:, :CH]) + z[:, CH : 2 * CH] + down_one(z[:, 2 * CH :])
    hidden, slope = silu_parts(pre)
    index = lax.broadcasted_iota(I32, (768, CH), 0)
    step = (index >= 192).astype(I32) + (index >= 384).astype(I32) + (index >= 576).astype(I32)
    row = 2 * band - 1 + step
    col = index & 63
    inner = (row >= 1) & (row <= 62) & (col >= 1) & (col <= 62)
    gpre = jnp.where(inner, back * slope, 0.0).astype(BF)
    hid = jnp.where(inner, hidden, 0.0)[192:576].astype(BF)

    gown = gpre[192:576].astype(F32)
    gcat = jnp.concatenate([up_one(gown).astype(BF), gpre[192:576], down_one(gown).astype(BF)], axis=1)
    first = mm_t(three_rows(f2, 192, 384), gcat)
    hown = hid.astype(F32)
    hcat = jnp.concatenate([down_one(hown).astype(BF), hid, up_one(hown).astype(BF)], axis=1)
    gback = jnp.concatenate([g2[576:960, :], g2[384:768, :], g2[192:576, :]], axis=1)
    second = mm_t(hcat, gback)
    for k, (a, b) in enumerate(TAPS):
        acc[k * CH : (k + 1) * CH, :] = first[a * CH : (a + 1) * CH, b * CH : (b + 1) * CH]
        acc[1152 + k * CH : 1152 + (k + 1) * CH, :] = second[b * CH : (b + 1) * CH, a * CH : (a + 1) * CH]

    gthree = jnp.concatenate([gpre[0:384], gpre[192:576], gpre[384:768]], axis=1)
    z = mm(gthree, back_weights(w1t))
    gin_ref[...] = up_one(z[:, :CH]) + z[:, CH : 2 * CH] + down_one(z[:, 2 * CH :])

    line = lax.broadcasted_iota(I32, (64, 1), 0)
    place = line & 15
    side = (place >= 3).astype(I32) + (place >= 6).astype(I32) + (place >= 9).astype(I32)
    face = place - 3 * side
    home = line - place
    real = place < 12
    lane = lax.broadcasted_iota(I32, (64, 64), 1)

    def one_hot(target, keep):
        return (jnp.where(keep & real, target, -1) == lane).astype(F32).astype(BF)

    fn = idx_ref[:, 0:1]
    rot = idx_ref[:, 1:2]
    fn_group = (fn * 43) >> 7
    partner = fn_group * 16 + (rot & 3) * 3 + (fn - 3 * fn_group)
    straight = one_hot(partner, (rot >> 2) == 0)
    turned = one_hot(partner, (rot >> 2) == 1)
    fills = []
    for column in (2, 3):
        m = idx_ref[:, column : column + 1]
        mf = m >> 2
        mg = (mf * 43) >> 7
        target = mg * 16 + ((m >> 1) & 1) * 3 + (mf - 3 * mg)
        fills.append((one_hot(target, (m & 1) == 0), one_hot(target, (m & 1) == 1)))
    (lo_zero, lo_end), (hi_zero, hi_end) = fills
    even = (side & 1) == 0
    low_side = jnp.where(side < 2, 2, 0)
    high_side = jnp.where(side < 2, 3, 1)
    near = [one_hot(home + low_side * 3 + face, even), one_hot(home + low_side * 3 + face, ~even)]
    far = [one_hot(home + high_side * 3 + face, even), one_hot(home + high_side * 3 + face, ~even)]
    side_mask = [jnp.broadcast_to((side == s).astype(F32), (64, CH)).astype(BF) for s in range(4)]
    row_line = (side < 2).astype(F32)

    for j in range(POSITIONS):
        for block in range(4):
            xs[block, j] = jnp.concatenate([a_ref[g, j, block * 16 : block * 16 + 16, :] for g in range(4)], axis=0)
    for j in range(POSITIONS):
        hal[j] = (mm(straight, xs[0, j]) + mm(turned, xs[0, 9 - j])).astype(BF)

    start = 2 - band
    stop = 7 + band

    @pl.when(band < 2)
    def _():
        for depth in range(2):
            head = hal[start + depth]
            tail = hal[stop - depth]
            xs[depth, start - 1] = (mm(near[0], head) + mm(near[1], tail)).astype(BF)
            xs[depth, stop + 1] = (mm(far[0], head) + mm(far[1], tail)).astype(BF)
        head = xs[0, start]
        tail = xs[0, stop]
        hal[start - 1] = (mm(lo_zero, head) + mm(lo_end, tail)).astype(BF)
        hal[stop + 1] = (mm(hi_zero, head) + mm(hi_end, tail)).astype(BF)

    def choose(options):
        total = None
        for s, option in enumerate(options):
            if option is None:
                continue
            term = option * side_mask[s]
            total = term if total is None else total + term
        return jnp.zeros((64, CH), BF) if total is None else total

    def fill(target, block, source):
        for k, tap in enumerate(TAPS):
            target[block * 64 : block * 64 + 64, k * CH : (k + 1) * CH] = choose(
                [source(*side_frame(s, tap)) for s in range(4)]
            )

    def field_source(j):
        def source(delta, dt):
            return hal[j + dt] if delta == -1 else xs[delta, j + dt]
        return source

    def grad_source(e, j, depths):
        def source(delta, dt):
            depth, at = e - delta, j - dt
            if depth not in depths or not 0 <= at < POSITIONS:
                return None
            return depths[depth](at)
        return source

    order_pre = (2, 7, 1, 3, 6, 8)
    for block, j in enumerate(order_pre):
        fill(lp, block, field_source(j))
    order_back = [(0, 2), (0, 7), (-1, 2), (-1, 7), (-1, 1), (-1, 8), (0, 1), (0, 3), (0, 6), (0, 8), (-1, 0), (-1, 3), (-1, 6), (-1, 9)]
    given = {0: lambda at: xs[2, at], 1: lambda at: xs[3, at]}
    for block, (e, j) in enumerate(order_back):
        fill(lg, block, grad_source(e, j, given))

    pre = mm(lp[...], w1_ref[...].reshape(9 * CH, CH))
    back = mm(lg[...], w2t[...])

    def back_block(e, j):
        block = order_back.index((e, j))
        return back[block * 64 : block * 64 + 64]

    for j in (0, 1, 2, 3, 6, 7, 8, 9):
        ob[j] = back_block(-1, j).astype(BF)
    for j in (1, 2, 3, 6, 7, 8):
        ss[j] = mm(straight, ob[j]) + mm(turned, ob[9 - j])

    def corner_sums(low, high):
        low = (low.astype(F32) * row_line).astype(BF)
        high = (high.astype(F32) * row_line).astype(BF)
        return mm_t(lo_zero, low) + mm_t(hi_zero, high), mm_t(lo_end, low) + mm_t(hi_end, high)

    @pl.when(band < 2)
    def _():
        at_zero, at_end = corner_sums(ob[start - 1], ob[stop + 1])
        head = ss[start] + at_zero
        tail = ss[stop] + at_end
        head_b, tail_b = head.astype(BF), tail.astype(BF)
        ss[start] = head + mm(near[0], head_b) + mm(near[1], tail_b)
        ss[stop] = tail + mm(far[0], head_b) + mm(far[1], tail_b)

    def spot(j):
        return band - 2 + j if j < 5 else 56 - band + j

    unique = {}
    hid = {}
    for j in (0, 9):
        gp[j] = jnp.zeros((64, CH), BF)
        gpu[j] = jnp.zeros((64, CH), BF)
    for block, j in enumerate(order_pre):
        value = pre[block * 64 : block * 64 + 64]
        hidden, slope = silu_parts(value)
        t = spot(j)
        inside = jnp.logical_and(t >= 0, t < SPAN)
        corner = jnp.logical_or(t == 0, t == SPAN - 1)
        keep = jnp.where(corner, row_line, jnp.ones_like(row_line))
        unique[j] = keep
        grad = jnp.where(inside, (back_block(0, j) + ss[j]) * slope, 0.0).astype(BF)
        gp[j] = grad
        gpu[j] = (grad.astype(F32) * keep).astype(BF)
        if j in (2, 7):
            hid[j] = hidden.astype(BF)

    mine = (home == group * 16).astype(F32)
    edge = jnp.where(band == 0, 1.0, 0.0) * mine * row_line

    def scaled(value, factor):
        return (value.astype(F32) * factor).astype(BF)

    cells = jnp.concatenate([
        scaled(hid[2], mine * unique[2]),
        scaled(hid[7], mine * unique[7]),
        scaled(mm(straight, hid[2]) + mm(turned, hid[7]), mine),
        scaled(mm(straight, hid[7]) + mm(turned, hid[2]), mine),
        scaled(mm(lo_zero, hid[2]) + mm(lo_end, hid[7]), edge),
        scaled(mm(hi_zero, hid[2]) + mm(hi_end, hid[7]), edge),
    ], axis=0)
    second = mm_t(cells, lg[0:384, :])
    own = jnp.concatenate([scaled(gpu[2], mine), scaled(gpu[7], mine)], axis=0)
    first = mm_t(lp[0:128, :], own)
    acc[0:1152, :] += first
    for k in range(9):
        acc[1152 + k * CH : 1152 + (k + 1) * CH, :] += second[:, k * CH : (k + 1) * CH]

    order_in = [(0, 2), (0, 7), (1, 2), (1, 7), (-1, 1), (-1, 2), (-1, 7), (-1, 8)]
    for block, (e, j) in enumerate(order_in):
        depths = {0: (lambda at: gp[at]) if e == -1 else (lambda at: gpu[at])}
        fill(lc, block, grad_source(e, j, depths))
    back = mm(lc[...], w1t[...])
    part = [back[k * 64 : k * 64 + 64] for k in range(8)]
    o1, o2, o7, o8 = [p.astype(BF) for p in part[4:]]
    at_zero, at_end = corner_sums(o1, o8)
    at_edge = jnp.where(band == 0, 1.0, 0.0)
    owed = [
        part[0] + mm(straight, o2) + mm(turned, o7) + at_zero * at_edge,
        part[2],
        part[1] + mm(straight, o7) + mm(turned, o2) + at_end * at_edge,
        part[3],
    ]

    acc[2304:2312, :] = jnp.zeros((8, CH), F32)
    slot_row = lax.broadcasted_iota(I32, (SLOT_TWO, 64), 0)
    slot_lane = lax.broadcasted_iota(I32, (SLOT_TWO, 64), 1)
    head_row = lax.broadcasted_iota(I32, (SLOT_TWO, CH), 0) < CHUNK
    tails = {}
    for half in range(2):
        for g in range(4):
            tile = jnp.concatenate([o[g * 16 : g * 16 + 16] for o in owed], axis=0).astype(BF)
            row_target = group * 16 + half * 3 + (slot_row - 18)
            col_target = (half * 2 + (group & 1)) * 16 + 6 + 3 * (group >> 1) + (slot_row - 21)
            target = jnp.where(slot_row < 18, -1, jnp.where(slot_row < 21, row_target, col_target))
            tails[half, g] = mm((target == slot_lane).astype(F32).astype(BF), tile)
    for i in range(BANDS * GROUPS):
        piece = acc[CHUNK * i : CHUNK * i + SLOT_TWO, :]
        tail = tails[int(i // 4 >= 16), i % 4]
        out_ref[i] = jnp.where(head_row, piece, tail).astype(BF)


def reverse_selector():
    select = np.zeros((64, 64), np.float32)
    for b in range(32):
        select[b, b] = 1
        select[63 - b, 32 + b] = 1
    return select


def reduce_kernel(factor, sc_ref, in_ref, sum_ref):
    total = jnp.zeros((SLOT_TWO, CH), F32)
    for i in range(BANDS * GROUPS):
        total = total + in_ref[i].astype(F32)
    total = (total * factor).astype(BF)
    for i in range(BANDS * GROUPS):
        sum_ref[i] = total


def grad_kernel(sc_ref, rev_ref, in_ref, gin_ref, g_ref, out_ref, wide, total):
    band = sc_ref[0]
    for row in range(2):
        for face in range(3):
            start = row * 192 + face * 64
            total[row, face] = gin_ref[start : start + 64, :] + g_ref[face, row].astype(F32)
    low = band < 16
    for row in range(2):
        source = jnp.where(low, 2 * band + row, 63 - 2 * band - row)
        for sub in range(4):
            tile = in_ref[source * 4 + sub].astype(F32)
            depth, side = sub % 2, sub // 2
            column = depth if side == 0 else 63 - depth
            for face in range(3):
                total[row, face, column : column + 1, :] += tile[21 + face : 22 + face, :]

    @pl.when((band == 0) | (band == BANDS - 1))
    def _():
        for i in range(BANDS * GROUPS):
            wide[i * SLOT_TWO : (i + 1) * SLOT_TWO, :] = in_ref[i].astype(F32)
        for depth in range(2):
            for face in range(3):
                halves = [
                    wide[pl.ds((pos * 2 + depth) * SLOT_TWO + 18 + face, BANDS, stride=4 * SLOT_TWO), :]
                    for pos in range(2)
                ]
                extra = mm(rev_ref[...], jnp.concatenate(halves, axis=0).astype(BF))
                row = jnp.where(band == 0, depth, 1 - depth)
                total[row, face] += extra

    for row in range(2):
        for face in range(3):
            out_ref[face, row] = total[row, face].astype(BF)


def spread_kernel(in_ref, first_ref, second_ref):
    for i in range(BANDS * GROUPS):
        piece = in_ref[i].astype(F32)[0:CHUNK, :]
        ref = first_ref if i < 64 else second_ref
        start = CHUNK * (i % 64)
        ref[start : start + CHUNK, :] = piece


def by_line(table):
    return jnp.pad(table.reshape(4, 3, 4).transpose(0, 2, 1).reshape(4, 12), ((0, 0), (0, 4))).reshape(64)


def body(field_in, grad_out, first_weight, second_weight, face_neighbour, seam_rotation, corner_fill):
    band = lax.axis_index("tile")
    group = lax.axis_index("sub")
    scalars = jnp.stack([band, group]).astype(I32)
    factor = (1.0 * 12 * SPAN * SPAN) ** -0.5

    pair = jnp.stack([field_in, grad_out], axis=0)
    up = [(i, i + 1) for i in range(BANDS - 1)]
    down = [(j, i) for i, j in up]
    above = lax.ppermute(pair, "tile", up)
    below = lax.ppermute(pair, "tile", down)

    fill_low = jnp.stack([corner_fill[:, k] for k in (0, 2, 0, 1)], axis=1)
    fill_high = jnp.stack([corner_fill[:, k] for k in (1, 3, 2, 3)], axis=1)
    table = jnp.stack([by_line(t) for t in (face_neighbour, seam_rotation, fill_low, fill_high)], axis=1)

    slots = call(
        pack_lines,
        jax.ShapeDtypeStruct((BANDS, SLOT_ONE, CH), BF),
        [pltpu.VMEM((SPAN * 16, CH), F32), pltpu.VMEM((48, CH), F32)],
        (field_in, grad_out),
    )
    slots = lax.all_to_all(slots, "tile", 0, 0, tiled=True)
    lines = call(
        gather_lines,
        jax.ShapeDtypeStruct((POSITIONS, 64, CH), BF),
        [],
        (scalars, jnp.asarray(line_selector(), BF), slots),
        smem_first=True,
    )
    lines = lax.all_gather(lines, "sub", axis=0)

    slots, gin = call(
        main_kernel,
        [jax.ShapeDtypeStruct((BANDS * GROUPS, SLOT_TWO, CH), BF), jax.ShapeDtypeStruct((384, CH), F32)],
        [
            pltpu.VMEM((1152, CH), BF),
            pltpu.VMEM((1152, CH), BF),
            pltpu.VMEM((1152, CH), BF),
            pltpu.VMEM((1152, CH), BF),
            pltpu.VMEM((4, POSITIONS, 64, CH), BF),
            pltpu.VMEM((POSITIONS, 64, CH), BF),
            pltpu.VMEM((384, 1152), BF),
            pltpu.VMEM((896, 1152), BF),
            pltpu.VMEM((512, 1152), BF),
            pltpu.VMEM((POSITIONS, 64, CH), BF),
            pltpu.VMEM((POSITIONS, 64, CH), F32),
            pltpu.VMEM((POSITIONS, 64, CH), BF),
            pltpu.VMEM((POSITIONS, 64, CH), BF),
            pltpu.VMEM((2312, CH), F32),
        ],
        (
            scalars, table, lines, field_in, above[0], below[0], grad_out, above[1], below[1],
            first_weight, second_weight,
        ),
        smem_first=True,
    )
    slots = lax.all_to_all(slots, BOTH, 0, 0, tiled=True)
    reduced = call(
        lambda *refs: reduce_kernel(factor, *refs),
        jax.ShapeDtypeStruct((BANDS * GROUPS, SLOT_TWO, CH), BF),
        [],
        (scalars, slots),
        smem_first=True,
    )
    reduced = lax.all_to_all(reduced, BOTH, 0, 0, tiled=True)
    grad_in = call(
        grad_kernel,
        jax.ShapeDtypeStruct((3, 2, SPAN, CH), BF),
        [pltpu.VMEM((BANDS * GROUPS * SLOT_TWO, CH), F32), pltpu.VMEM((2, 3, SPAN, CH), F32)],
        (scalars, jnp.asarray(reverse_selector(), BF), slots, gin, grad_out),
        smem_first=True,
    )
    first, second = call(
        spread_kernel,
        [jax.ShapeDtypeStruct((1152, CH), F32), jax.ShapeDtypeStruct((1152, CH), F32)],
        [],
        (reduced,),
    )
    return grad_in, first.reshape(3, 3, CH, CH), second.reshape(3, 3, CH, CH)


def solution(mesh):
    return jax.shard_map(
        body,
        mesh=mesh,
        in_specs=(P("sub", "tile", None, None), P("sub", "tile", None, None), P(), P(), P(), P(), P()),
        out_specs=(P("sub", "tile", None, None), P(), P()),
        check_vma=False,
    )
```

time: 1070 us -> 104 us (0.10)
  waiting for transfers between devices: 708 us -> 32.3 us
  blocking collectives: 243 us -> 33.9 us
  local copies, waits for them, and re-layouts: 40 us -> 3.03 us
  other arithmetic: 21.3 us -> 0.13 us
  between operations: 16.1 us -> 0.83 us
  Pallas kernels: 0 us -> 12.6 us
  starting transfers between devices: 32.5 us -> 20.4 us
    psum x3 -> x0, waiting for transfers between devices: 708 us -> none  [the longest x1 331 us: scatter_back(): lax.psum(left_part.astype(jnp.bfloat16), 'tile').astype(jnp.float32)]
    all_gather x4 -> x1, blocking collectives: 199 us -> 9.07 us  [body(): lines = lax.all_gather(lines, 'sub', axis=0)]
    unnamed x2 -> x0, blocking collectives: 44.1 us -> none
    all_to_all x0 -> x1, blocking collectives: none -> 24.8 us  [body(): slots = lax.all_to_all(slots, BOTH, 0, 0, tiled=True)]
    ppermute x8 -> x2, waiting for transfers between devices: 0.02 us -> 17.2 us  [the longest x1 17.2 us: body(): below = lax.ppermute(pair, 'tile', down)]
    all_to_all x0 -> x2, waiting for transfers between devices: none -> 15.2 us  [the longest x1 15.2 us: body(): reduced = lax.all_to_all(reduced, BOTH, 0, 0, tiled=True)]
    all_to_all x0 -> x2, starting transfers between devices: none -> 15.1 us  [the longest x1 11.3 us: body(): slots = lax.all_to_all(slots, 'tile', 0, 0, tiled=True)]
    ppermute x8 -> x2, starting transfers between devices: 19.9 us -> 5.29 us  [the longest x1 4 us: body(): above = lax.ppermute(pair, 'tile', up)]
  transfers between devices with their start and end apart: 15 -> 4, of which waited for: 3 -> 2; matrix products, arithmetic and copies ran while one was open for 8% -> 1% of each run, Pallas kernels for 0% -> 1%
where the time goes in v1:
time: 104 us; the launch traced here: 103 us
  blocking collectives  33.9 us (33%)
  waiting for transfers between devices  32.3 us (31%)
  starting transfers between devices  20.4 us (20%)
  Pallas kernels  12.6 us (12%)
  local copies, waits for them, and re-layouts  3.03 us (3%)
    all_to_all x1, blocking collectives, body(): slots = lax.all_to_all(slots, BOTH, 0, 0, tiled=True)  24.8 us
    ppermute x1, waiting for transfers between devices, body(): below = lax.ppermute(pair, 'tile', down)  17.2 us
    all_to_all x1, waiting for transfers between devices, body(): reduced = lax.all_to_all(reduced, BOTH, 0, 0, tiled=True)  15.2 us
    pallas_call x6, Pallas kernels, call(): pl.pallas_call(kernel, out_shape=outs, in_specs=specs, out_specs=out_spec...  12.6 us
    all_to_all x1, starting transfers between devices, body(): slots = lax.all_to_all(slots, 'tile', 0, 0, tiled=True)  11.3 us
    all_gather x1, blocking collectives, body(): lines = lax.all_gather(lines, 'sub', axis=0)  9.07 us
    ppermute x1, starting transfers between devices, body(): above = lax.ppermute(pair, 'tile', up)  4 us
    all_to_all x1, starting transfers between devices, body(): reduced = lax.all_to_all(reduced, BOTH, 0, 0, tiled=True)  3.78 us
  transfers between devices with their start and end apart: 4, of which 2 were waited for; matrix products, arithmetic and copies ran while one was open for 1% of the time, Pallas kernels for 1%

profile of v1, /device:TPU:1, one launch (start us, length us, event | category | flops | bytes accessed | tf_op | source)
XLA Modules:
  0.0 103.2 jit_solution(3825734624690190494)
XLA Ops:
  0.6 0.0 copy-start
  0.6 0.9 copy-done
  1.5 0.0 copy-start.2
  1.5 0.9 copy-done.2
  2.4 1.6 %shard_map.112 = bf16[32,208,128]{2,1,0:T(8,128)(2,1)} custom-call(bf16[3,2,64,128]{3,2,1,0:T(8,128)(2,1)S(1)} %copy-done.2, bf16[3,2,64,128]{3,2,1,0:T(8,128)(2,1)S(1)} %copy-done), custom_call_target="tpu_custom_call" | custom-call | tf_op jit(solution)/shard_map/pallas_call | solution.py:40
  4.0 0.0 copy-start.1
  4.0 0.0 copy-start.3
  4.0 0.0 copy-start.8
  4.0 0.0 copy-start.9
  4.0 0.0 copy-start.10
  4.0 0.0 copy-start.6
  4.0 11.3 %all-to-all-start = ((bf16[32,208,128]{2,1,0:T(8,128)(2,1)}), bf16[32,208,128]{2,1,0:T(8,128)(2,1)S(1)}, u32[]{:S(2)}, u32[]{:S(2)}) async-start(bf16[32,208,128]{2,1,0:T(8,128)(2,1)} %shard_map.112), calls=%async_computation | async-start | bytes 3407872 | tf_op jit(solution)/shard_map/all_to_all | solution.py:455
  15.4 0.0 copy-done.1
  15.4 0.0 copy-done.3
  15.4 1.3 %collective-permute-start.1 = (bf16[2,3,2,64,128]{4,3,2,1,0:T(8,128)(2,1)S(1)}, bf16[2,3,2,64,128]{4,3,2,1,0:T(8,128)(2,1)S(1)}, u32[]{:S(2)}, u32[]{:S(2)}) collective-permute-start(bf16[2,3,2,64,128]{4,3,2,1,0:T(8,128)(2,1)S(1)} %pad_maximum_fusion), channel_id=1, source_target_pairs={{4,0},{8,4},{12,8},{16,12},{20,16},{24,20},{28,24},{32,28},{36,32}... | collective-permute-start | bytes 589832 | tf_op jit(solution)/shard_map/ppermute | solution.py:443
  16.7 4.0 %collective-permute-start = (bf16[2,3,2,64,128]{4,3,2,1,0:T(8,128)(2,1)S(1)}, bf16[2,3,2,64,128]{4,3,2,1,0:T(8,128)(2,1)S(1)}, u32[]{:S(2)}, u32[]{:S(2)}) collective-permute-start(bf16[2,3,2,64,128]{4,3,2,1,0:T(8,128)(2,1)S(1)} %pad_maximum_fusion), channel_id=1, source_target_pairs={{0,4},{4,8},{8,12},{12,16},{16,20},{20,24},{24,28},{28,32},{32,36}... | collective-permute-start | bytes 589832 | tf_op jit(solution)/shard_map/ppermute | solution.py:442
  20.7 0.0 copy-done.8
  20.8 0.1 reshape.40
  20.9 0.1 reshape.41
  21.0 0.1 stack_reshape.14
  21.0 0.1 reshape.42
  21.1 0.1 reshape.43
  21.2 0.1 stack_reshape.15
  21.3 0.0 copy-done.9
  21.3 0.1 reshape.36
  21.4 0.1 reshape.37
  21.5 0.1 stack_reshape.12
  21.6 0.0 copy-done.10
  21.6 0.1 reshape.38
  21.7 0.1 reshape.39
  21.8 0.1 stack_reshape.13
  21.9 0.1 copy.32.idx_ref
  22.0 0.1 pad_add_fusion.3.sc_ref.refs_0_
  22.1 0.0 copy-start.4
  22.1 0.0 copy-start.5
  22.1 17.2 %collective-permute-done.1 = bf16[2,3,2,64,128]{4,3,2,1,0:T(8,128)(2,1)S(1)} collective-permute-done((bf16[2,3,2,64,128]{4,3,2,1,0:T(8,128)(2,1)S(1)}, bf16[2,3,2,64,128]{4,3,2,1,0:T(8,128)(2,1)S(1)}, u32[]{:S(2)}, u32[]{:S(2)}) %collective-permute-start.1) | collective-permute-done | bytes 196640 | tf_op jit(solution)/shard_map/ppermute | solution.py:443
  39.2 0.0 collective-permute-done
  39.3 0.0 all-to-all-done.in_ref
  39.3 0.0 copy-done.6
  39.3 0.7 shard_map.113
  40.0 9.1 %all-gather = bf16[40,64,128]{2,1,0:T(8,128)(2,1)S(1)} all-gather(bf16[10,64,128]{2,1,0:T(8,128)(2,1)S(1)} %shard_map.113), channel_id=2, replica_groups=mesh['tile'=32,'sub'=4] {'sub'}, dimensions={0}, use_global_device_ids=true | all-gather | bytes 819200 | tf_op jit(solution)/shard_map/all_gather | solution.py:463
  49.1 0.0 copy-done.4
  49.1 0.0 copy-done.5
  49.1 6.1 %shard_map.114 = (bf16[128,24,128]{2,1,0:T(8,128)(2,1)S(1)}, f32[384,128]{1,0:T(8,128)S(1)}) custom-call(s32[2]{0:T(128)S(1)} %pad_add_fusion.3.sc_ref.refs_0_, s32[64,4]{1,0:T(8,128)S(1)} %copy.32.idx_ref, bf16[4,10,64,128]{3,2,1,0:T(8,128)(2,1)S(1)} %bitcast.27, bf16[3,2,64,128]{3,2,1,0:T(8,128)(2,1)S(1)} %copy-done.3, ...), custom_call_target="tpu_custom_call" | custom-call | tf_op jit(solution)/shard_map/pallas_call | solution.py:40
  55.2 24.8 %all_to_all.15.in_ref.refs_1_ = bf16[128,24,128]{2,1,0:T(8,128)(2,1)S(1)} all-to-all(bf16[128,24,128]{2,1,0:T(8,128)(2,1)S(1)} %get-tuple-element.7), channel_id=1, replica_groups=mesh['tile'=32,'sub'=4] {'tile','sub'}, dimensions={0} | all-to-all | bytes 1572864 | tf_op jit(solution)/shard_map/all_to_all | solution.py:490
  80.0 0.0 copy-start.7
  80.0 1.6 %shard_map.116 = bf16[128,24,128]{2,1,0:T(8,128)(2,1)} custom-call(s32[2]{0:T(128)S(1)} %pad_add_fusion.3.sc_ref.refs_0_, bf16[128,24,128]{2,1,0:T(8,128)(2,1)S(1)} %all_to_all.15.in_ref.refs_1_), custom_call_target="tpu_custom_call" | custom-call | tf_op jit(solution)/shard_map/pallas_call | solution.py:40
  81.6 3.8 %all-to-all-start.2 = ((bf16[128,24,128]{2,1,0:T(8,128)(2,1)}), bf16[128,24,128]{2,1,0:T(8,128)(2,1)S(1)}, u32[]{:S(2)}, u32[]{:S(2)}) async-start(bf16[128,24,128]{2,1,0:T(8,128)(2,1)} %shard_map.116), calls=%async_computation.2 | async-start | bytes 1572864 | tf_op jit(solution)/shard_map/all_to_all | solution.py:498
  85.4 0.0 copy-done.7
  85.4 1.5 %shard_map.115 = bf16[3,2,64,128]{3,2,1,0:T(8,128)(2,1)} custom-call(s32[2]{0:T(128)S(1)} %pad_add_fusion.3.sc_ref.refs_0_, bf16[64,64]{1,0:T(8,128)(2,1)S(1)} %copy-done.7, bf16[128,24,128]{2,1,0:T(8,128)(2,1)S(1)} %all_to_all.15.in_ref.refs_1_, f32[384,128]{1,0:T(8,128)S(1)} %get-tuple-element.8.gin_ref, bf16[3,2,64,128]{3,2,1,0:T(8,128)(2,1)S(1)} %copy-done.1), custom_call_target="tpu_custom_call" | custom-call | tf_op jit(solution)/shard_map/pallas_call | solution.py:40
  87.0 15.2 %all-to-all-done.2.in_ref = bf16[128,24,128]{2,1,0:T(8,128)(2,1)S(1)} async-done(((bf16[128,24,128]{2,1,0:T(8,128)(2,1)}), bf16[128,24,128]{2,1,0:T(8,128)(2,1)S(1)}, u32[]{:S(2)}, u32[]{:S(2)}) %all-to-all-start.2) | async-done | bytes 786464 | tf_op jit(solution)/shard_map/all_to_all | solution.py:498
  102.1 1.1 %shard_map.117 = (f32[1152,128]{1,0:T(8,128)}, f32[1152,128]{1,0:T(8,128)}) custom-call(bf16[128,24,128]{2,1,0:T(8,128)(2,1)S(1)} %all-to-all-done.2.in_ref), custom_call_target="tpu_custom_call" | custom-call | tf_op jit(solution)/shard_map/pallas_call | solution.py:40
  (15 shorter events, 0.2 us)
Async XLA Ops:
  0.6 0.9 copy-start
  1.5 0.9 copy-start.2
  4.0 11.4 %copy-start.1 = (bf16[3,2,64,128]{3,2,1,0:T(8,128)(2,1)S(1)}, bf16[3,2,64,128]{3,2,1,0:T(8,128)(2,1)}, u32[]{:S(2)}) copy-start(bf16[3,2,64,128]{3,2,1,0:T(8,128)(2,1)} %g_ref.5) | copy-start | bytes 294916
  4.0 11.4 %copy-start.3 = (bf16[3,2,64,128]{3,2,1,0:T(8,128)(2,1)S(1)}, bf16[3,2,64,128]{3,2,1,0:T(8,128)(2,1)}, u32[]{:S(2)}) copy-start(bf16[3,2,64,128]{3,2,1,0:T(8,128)(2,1)} %f_ref.3) | copy-start | bytes 294916
  4.0 16.7 %copy-start.8 = (s32[12,4]{0,1:T(4,128)S(1)}, s32[12,4]{0,1:T(4,128)}, u32[]{:S(2)}) copy-start(s32[12,4]{0,1:T(4,128)} %param.15) | copy-start | bytes 580
  4.0 17.3 %copy-start.9 = (s32[12,4]{0,1:T(4,128)S(1)}, s32[12,4]{0,1:T(4,128)}, u32[]{:S(2)}) copy-start(s32[12,4]{0,1:T(4,128)} %param.13) | copy-start | bytes 580
  4.0 17.6 %copy-start.10 = (s32[12,4]{0,1:T(4,128)S(1)}, s32[12,4]{0,1:T(4,128)}, u32[]{:S(2)}) copy-start(s32[12,4]{0,1:T(4,128)} %param.14) | copy-start | bytes 580
  4.0 35.3 %copy-start.6 = (bf16[2,64,80]{2,1,0:T(8,128)(2,1)S(1)}, bf16[2,64,80]{2,1,0:T(8,128)(2,1)}, u32[]{:S(2)}) copy-start(bf16[2,64,80]{2,1,0:T(8,128)(2,1)} %constant.15.clone.sel_ref) | copy-start | bytes 61444
  4.0 35.3 %all-to-all-start = ((bf16[32,208,128]{2,1,0:T(8,128)(2,1)}), bf16[32,208,128]{2,1,0:T(8,128)(2,1)S(1)}, u32[]{:S(2)}, u32[]{:S(2)}) async-start(bf16[32,208,128]{2,1,0:T(8,128)(2,1)} %shard_map.112), calls=%async_computation | async-start | bytes 3407872 | tf_op jit(solution)/shard_map/all_to_all | solution.py:455
  15.4 23.8 %collective-permute-start.1 = (bf16[2,3,2,64,128]{4,3,2,1,0:T(8,128)(2,1)S(1)}, bf16[2,3,2,64,128]{4,3,2,1,0:T(8,128)(2,1)S(1)}, u32[]{:S(2)}, u32[]{:S(2)}) collective-permute-start(bf16[2,3,2,64,128]{4,3,2,1,0:T(8,128)(2,1)S(1)} %pad_maximum_fusion), channel_id=1, source_target_pairs={{4,0},{8,4},{12,8},{16,12},{20,16},{24,20},{28,24},{32,28},{36,32}... | collective-permute-start | bytes 589832 | tf_op jit(solution)/shard_map/ppermute | solution.py:443
  16.7 22.5 %collective-permute-start = (bf16[2,3,2,64,128]{4,3,2,1,0:T(8,128)(2,1)S(1)}, bf16[2,3,2,64,128]{4,3,2,1,0:T(8,128)(2,1)S(1)}, u32[]{:S(2)}, u32[]{:S(2)}) collective-permute-start(bf16[2,3,2,64,128]{4,3,2,1,0:T(8,128)(2,1)S(1)} %pad_maximum_fusion), channel_id=1, source_target_pairs={{0,4},{4,8},{8,12},{12,16},{16,20},{20,24},{24,28},{28,32},{32,36}... | collective-permute-start | bytes 589832 | tf_op jit(solution)/shard_map/ppermute | solution.py:442
  22.1 27.1 %copy-start.4 = (bf16[3,3,128,128]{3,2,1,0:T(8,128)(2,1)S(1)}, bf16[3,3,128,128]{3,2,1,0:T(8,128)(2,1)}, u32[]{:S(2)}) copy-start(bf16[3,3,128,128]{3,2,1,0:T(8,128)(2,1)} %w1_ref.1) | copy-start | bytes 884740
  22.1 27.1 %copy-start.5 = (bf16[3,3,128,128]{3,2,1,0:T(8,128)(2,1)S(1)}, bf16[3,3,128,128]{3,2,1,0:T(8,128)(2,1)}, u32[]{:S(2)}) copy-start(bf16[3,3,128,128]{3,2,1,0:T(8,128)(2,1)} %w2_ref.1) | copy-start | bytes 884740
  80.0 5.4 %copy-start.7 = (bf16[64,64]{1,0:T(8,128)(2,1)S(1)}, bf16[64,64]{1,0:T(8,128)(2,1)}, u32[]{:S(2)}) copy-start(bf16[64,64]{1,0:T(8,128)(2,1)} %constant.16.clone.rev_ref) | copy-start | bytes 24580
  81.6 20.5 %all-to-all-start.2 = ((bf16[128,24,128]{2,1,0:T(8,128)(2,1)}), bf16[128,24,128]{2,1,0:T(8,128)(2,1)S(1)}, u32[]{:S(2)}, u32[]{:S(2)}) async-start(bf16[128,24,128]{2,1,0:T(8,128)(2,1)} %shard_map.116), calls=%async_computation.2 | async-start | bytes 1572864 | tf_op jit(solution)/shard_map/all_to_all | solution.py:498

commit v2 on v1

v2 whole, which is shorter than its diff:
```python
import jax
import jax.numpy as jnp
import numpy as np
from jax import lax
from jax.experimental import pallas as pl
from jax.experimental.pallas import tpu as pltpu
from jax.sharding import PartitionSpec as P

BF = jnp.bfloat16
F32 = jnp.float32
I32 = jnp.int32
BANDS = 32
SPAN = 64
CH = 128
TAPS = [(a, b) for a in range(3) for b in range(3)]
WINDOW = 6
ENDS = 48
STRIP = 12 * WINDOW
SLOT_ONE = 2 * STRIP
CHUNK = 72
TAIL = 48
SLOT_TWO = CHUNK + TAIL
VMEM_BYTES = 48 * 1024 * 1024


def mm(left, right):
    return jnp.dot(left, right, preferred_element_type=F32)


def mm_t(left, right):
    return lax.dot_general(left, right, (((0,), (0,)), ((), ())), preferred_element_type=F32)


def call(kernel, outs, scratch, operands, places=(), aliases=None):
    kinds = {"v": pltpu.VMEM, "s": pltpu.SMEM, "a": pl.ANY}
    places = dict(places)
    many = isinstance(outs, (list, tuple))
    out_specs = [pl.BlockSpec(memory_space=kinds[places.get(f"o{k}", "v")]) for k in range(len(outs) if many else 1)]
    return pl.pallas_call(
        kernel,
        out_shape=outs,
        in_specs=[pl.BlockSpec(memory_space=kinds[places.get(k, "v")]) for k in range(len(operands))],
        out_specs=out_specs if many else out_specs[0],
        scratch_shapes=scratch,
        input_output_aliases=aliases or {},
        compiler_params=pltpu.CompilerParams(vmem_limit_bytes=VMEM_BYTES),
    )(*operands)


def here():
    return lax.axis_index("tile"), lax.axis_index("sub")


def is_mirrored(fn_ref, rot_ref, face, side):
    rot = rot_ref[face, side]
    partner = 4 * fn_ref[face, side] + (rot & 3)
    return jnp.where(4 * face + side > partner, rot >> 2, 0)


def is_mirrored(fn_ref, rot_ref, face, side):
    rot = rot_ref[side, face]
    partner = 4 * fn_ref[side, face] + (rot & 3)
    return jnp.where(4 * face + side > partner, rot >> 2, 0)


def pack_lines(f_hbm, g_hbm, out_ref, buf, wide, ends, sems):
    copies = [pltpu.make_async_copy(src, buf.at[k], sems.at[k]) for k, src in enumerate((f_hbm, g_hbm))]
    for copy in copies:
        copy.start()
    band, _ = here()
    ends[ENDS:STRIP, :] = jnp.zeros((STRIP - ENDS, CH), F32)
    for fld in range(2):
        copies[fld].wait()
        for row in range(2):
            for face in range(3):
                block = buf[fld, face, row].astype(F32)
                wide[pl.ds(24 + fld * 6 + row * 3 + face, SPAN, stride=12), :] = block
                for edge, cols in enumerate(((0, 1), (63, 62))):
                    for depth, col in enumerate(cols):
                        place = row * 24 + fld * 12 + edge * 6 + depth * 3 + face
                        ends[place : place + 1, :] = block[col : col + 1, :]
    wide[0:24, :] = wide[SPAN * 12 : SPAN * 12 + 24, :]
    wide[SPAN * 12 + 24 : SPAN * 12 + 48, :] = wide[24:48, :]
    outer = (band == 0) | (band == BANDS - 1)
    strips = [wide[24 * d : 24 * d + STRIP, :] for d in range(BANDS)]
    for d in range(BANDS):
        rest = jnp.where(outer, strips[BANDS - 1 - d], ends[...])
        out_ref[d] = jnp.concatenate([strips[d], rest], axis=0).astype(BF)


def line_selector():
    select = np.zeros((2, WINDOW * 64, 4 * STRIP + 6 * ENDS), np.float32)
    for mirrored in range(2):
        for j in range(WINDOW):
            part, parity = j // 2, j % 2
            for fld in range(2):
                for depth in range(2):
                    for face in range(3):
                        base = j * 64 + (fld * 2 + depth) * 16 + face
                        column = STRIP * mirrored + (5 - j if mirrored else j) * 12 + fld * 6 + face
                        select[mirrored, base, column + depth * 3] = 1
                        select[mirrored, base + 3, 2 * STRIP + column + (1 - depth) * 3] = 1
                        for side in range(2):
                            source = 4 * STRIP + (3 * mirrored + part) * ENDS + (1 - parity if mirrored else parity) * 24
                            select[mirrored, base + 6 + 3 * side, source + fld * 12 + side * 6 + depth * 3 + face] = 1
    return select


def ends_selector():
    select = np.zeros((4, ENDS, SLOT_ONE), np.float32)
    for k, d in enumerate((0, 1, 30, 31)):
        for row in range(2):
            for fld in range(2):
                for side in range(2):
                    for depth in range(2):
                        col = 63 - depth if side else depth
                        at = (col - 2 * d + 2) % SPAN
                        other = (col - 60 + 2 * d) % SPAN
                        base = at * 12 if at < WINDOW else STRIP + other * 12
                        for face in range(3):
                            place = row * 24 + fld * 12 + side * 6 + depth * 3 + face
                            select[k, place, base + fld * 6 + row * 3 + face] = 1
    return select


def gather_lines(fn_ref, rot_ref, sel_ref, ends_ref, in_ref, out_ref):
    band, group = here()
    first, last = in_ref[0], in_ref[BANDS - 1]
    pick_ends = ends_ref[(band & 1) + 2 * (band >> 4)]
    first_ends, last_ends = mm(pick_ends, first), mm(pick_ends, last)
    ends = []
    for source in [band + 31 + part for part in range(3)] + [64 - band - part for part in range(3)]:
        source = source & 31
        block = in_ref[source].astype(F32)[STRIP : STRIP + ENDS]
        ends.append(jnp.where(source == 0, first_ends, jnp.where(source == BANDS - 1, last_ends, block)))
    pieces = jnp.concatenate([first.astype(F32), last.astype(F32)] + ends, axis=0).astype(BF)
    place = lax.broadcasted_iota(I32, (WINDOW * 64, CH), 0) & 15
    flip = jnp.zeros((WINDOW * 64, CH), I32)
    for side in range(4):
        for face in range(3):
            flip = jnp.where(place == side * 3 + face, is_mirrored(fn_ref, rot_ref, 3 * group + face, side), flip)
    picked = jnp.where(flip == 1, mm(sel_ref[1], pieces), mm(sel_ref[0], pieces)).astype(BF)
    for j in range(WINDOW):
        out_ref[j] = picked[j * 64 : j * 64 + 64]


def silu_parts(pre):
    logistic = 1.0 / (1.0 + jnp.exp(-pre))
    return pre * logistic, logistic * (1.0 + pre * (1.0 - logistic))


def side_frame(side, tap):
    dr, dc = tap[0] - 1, tap[1] - 1
    return ((dr, dc), (-dr, dc), (dc, dr), (-dc, dr))[side]


def transpose_weights(ref, out):
    for k, (a, b) in enumerate(TAPS):
        out[k * CH : (k + 1) * CH, :] = ref[a, b].T


def interior(band, in_ref, w1_ref, w1t, w2t, f2, g2, wide, acc, done):
    for s in range(BANDS):
        wide[s * STRIP : (s + 1) * STRIP, :] = in_ref[s].astype(F32)[0:STRIP]
    for q in range(WINDOW):
        for fld, target in enumerate((f2, g2)):
            for row in range(2):
                for face in range(3):
                    piece = wide[pl.ds(q * 12 + fld * 6 + row * 3 + face, BANDS, stride=STRIP), :]
                    target[pl.ds(q * 192 + face * 64 + row, BANDS, stride=2), :] = piece

    def conv_weights(ref):
        return jnp.concatenate([ref[a].reshape(3 * CH, CH) for a in range(3)], axis=1)

    def back_weights(ref):
        columns = []
        for a in range(3):
            columns.append(jnp.concatenate([ref[(a * 3 + b) * CH : (a * 3 + b + 1) * CH, :] for b in (2, 1, 0)], axis=0))
        return jnp.concatenate(columns, axis=1)

    def up_one(value):
        return pltpu.roll(value, value.shape[0] - 1, 0)

    def down_one(value):
        return pltpu.roll(value, 1, 0)

    def three_columns(ref, first, count):
        return jnp.concatenate([ref[first + 192 * b : first + 192 * b + count, :].astype(BF) for b in range(3)], axis=1)

    y = mm(three_columns(f2, 0, 768), conv_weights(w1_ref))
    pre = down_one(y[:, :CH]) + y[:, CH : 2 * CH] + up_one(y[:, 2 * CH :])
    z = mm(three_columns(g2, 0, 768), back_weights(w2t))
    back = up_one(z[:, :CH]) + z[:, CH : 2 * CH] + down_one(z[:, 2 * CH :])
    hidden, slope = silu_parts(pre)
    index = lax.broadcasted_iota(I32, (768, CH), 0)
    step = (index >= 192).astype(I32) + (index >= 384).astype(I32) + (index >= 576).astype(I32)
    col = 2 * band - 1 + step
    row = index & 63
    inner = (row >= 1) & (row <= 62) & (col >= 1) & (col <= 62)
    gpre = jnp.where(inner, back * slope, 0.0).astype(BF)
    hid = jnp.where(inner, hidden, 0.0)[192:576].astype(BF)

    gown = gpre[192:576].astype(F32)
    gcat = jnp.concatenate([up_one(gown).astype(BF), gpre[192:576], down_one(gown).astype(BF)], axis=1)
    first = mm_t(three_columns(f2, 192, 384), gcat)
    hown = hid.astype(F32)
    hcat = jnp.concatenate([down_one(hown).astype(BF), hid, up_one(hown).astype(BF)], axis=1)
    gback = jnp.concatenate([g2[start : start + 384, :].astype(BF) for start in (576, 384, 192)], axis=1)
    second = mm_t(hcat, gback)
    for k, (a, b) in enumerate(TAPS):
        top, low = k * CH, 1152 + k * CH
        acc[top : top + CH, :] = first[b * CH : (b + 1) * CH, a * CH : (a + 1) * CH]
        acc[low : low + CH, :] = second[a * CH : (a + 1) * CH, b * CH : (b + 1) * CH]

    gthree = jnp.concatenate([gpre[0:384], gpre[192:576], gpre[384:768]], axis=1)
    z = mm(gthree, back_weights(w1t))
    done[...] = up_one(z[:, :CH]) + z[:, CH : 2 * CH] + down_one(z[:, 2 * CH :]) + g2[384:768, :]


def main_kernel(
    fn_ref, rot_ref, fill_ref, sel_ref, a_ref, in_ref, w1_ref, w2_ref,
    out_ref,
    f2, g2, wide, total, done, sent, w1t, w2t, xs, hal, nb, cg, lp, lg, lc, ss, gp, gpu, owe,
):
    band, group = here()
    transpose_weights(w1_ref, w1t)
    transpose_weights(w2_ref, w2t)
    interior(band, in_ref, w1_ref, w1t, w2t, f2, g2, wide, total, done)

    line = lax.broadcasted_iota(I32, (64, 1), 0)
    place = line & 15
    side = (place >= 3).astype(I32) + (place >= 6).astype(I32) + (place >= 9).astype(I32)
    face = place - 3 * side
    home = line - place
    real = place < 12
    lane = lax.broadcasted_iota(I32, (64, 64), 1)

    def one_hot(target, keep):
        return (jnp.where(keep & real, target, -1) == lane).astype(F32).astype(BF)

    face_lane = lax.broadcasted_iota(I32, (64, 12), 1)
    faces = (jnp.where(real, 3 * (line >> 4) + face, -1) == face_lane).astype(F32).astype(BF)

    def by_line(ref, columns):
        table = ref[...].astype(F32).astype(BF)
        rows = lax.dot_general(faces, table, (((1,), (1,)), ((), ())), preferred_element_type=F32).astype(I32)
        value = rows[:, columns[0] : columns[0] + 1]
        for s in range(1, 4):
            value = jnp.where(side == s, rows[:, columns[s] : columns[s] + 1], value)
        return value

    fn = by_line(fn_ref, (0, 1, 2, 3))
    rot = by_line(rot_ref, (0, 1, 2, 3))
    fn_group = (fn * 43) >> 7
    partner = one_hot(fn_group * 16 + (rot & 3) * 3 + (fn - 3 * fn_group), real)
    number = 4 * (3 * (line >> 4) + face) + side
    flip = ((rot >> 2) == 1) & (number > 4 * fn + (rot & 3)) & real
    fills = []
    for columns in ((0, 2, 0, 1), (1, 3, 2, 3)):
        m = by_line(fill_ref, columns)
        mf = m >> 2
        mg = (mf * 43) >> 7
        target = mg * 16 + ((m >> 1) & 1) * 3 + (mf - 3 * mg)
        fills.append((one_hot(target, (m & 1) == 0), one_hot(target, (m & 1) == 1)))
    (lo_zero, lo_end), (hi_zero, hi_end) = fills
    even = (side & 1) == 0
    low_side = jnp.where(side < 2, 2, 0)
    high_side = jnp.where(side < 2, 3, 1)
    near = [one_hot(home + low_side * 3 + face, even), one_hot(home + low_side * 3 + face, ~even)]
    far = [one_hot(home + high_side * 3 + face, even), one_hot(home + high_side * 3 + face, ~even)]
    side_mask = [jnp.broadcast_to((side == s).astype(F32), (64, CH)).astype(BF) for s in range(4)]
    row_line = (side < 2).astype(F32)
    flip_f = jnp.broadcast_to(flip.astype(F32), (64, CH))
    flip_b, keep_b = flip_f.astype(BF), (1.0 - flip_f).astype(BF)

    def pick(plain, mirrored):
        return plain * keep_b + mirrored * flip_b

    def pick_f(plain, mirrored):
        return jnp.where(flip_f > 0.5, mirrored, plain)

    for j in range(WINDOW):
        for block in range(4):
            xs[block, j] = jnp.concatenate([a_ref[g, j, block * 16 : block * 16 + 16, :] for g in range(4)], axis=0)
    for j in range(WINDOW):
        hal[j] = mm(partner, xs[0, j]).astype(BF)

    def block_at(block, j):
        return hal[j] if block == 0 else xs[block - 1, j]

    for block in range(5):
        for j in range(1, 5):
            before, after = block_at(block, j - 1), block_at(block, j + 1)
            nb[0, block, j] = pick(before, after)
            nb[1, block, j] = pick(after, before)
    cg[...] = jnp.zeros_like(cg)

    def line_ends(zero, end, shift):
        lower, upper = zero + shift, end - shift
        return lambda value: (pick(value(lower), value(upper)), pick(value(upper), value(lower)))

    def fill_ends(zero, end):
        first = line_ends(zero, end, 0)
        second = line_ends(zero, end, 1)
        h_zero, h_end = first(lambda j: hal[j])
        h_one, h_last = second(lambda j: hal[j])
        f_zero, f_end = first(lambda j: xs[0, j])
        none = jnp.zeros((64, CH), BF)
        low = [
            (mm(lo_zero, f_zero) + mm(lo_end, f_end)).astype(BF),
            (mm(near[0], h_zero) + mm(near[1], h_end)).astype(BF),
            (mm(near[0], h_one) + mm(near[1], h_last)).astype(BF),
            none, none,
        ]
        high = [
            (mm(hi_zero, f_zero) + mm(hi_end, f_end)).astype(BF),
            (mm(far[0], h_zero) + mm(far[1], h_end)).astype(BF),
            (mm(far[0], h_one) + mm(far[1], h_last)).astype(BF),
            none, none,
        ]
        for block in range(5):
            nb[0, block, zero] = pick(low[block], nb[0, block, zero])
            nb[1, block, zero] = pick(nb[1, block, zero], high[block])
            nb[0, block, end] = pick(nb[0, block, end], low[block])
            nb[1, block, end] = pick(high[block], nb[1, block, end])
        cg[0], cg[1] = first(lambda j: xs[2, j])

    @pl.when(band == 0)
    def _():
        fill_ends(2, 1)

    @pl.when(band == BANDS - 1)
    def _():
        fill_ends(4, 3)

    def choose(options):
        result = None
        for s, option in enumerate(options):
            if option is None:
                continue
            term = option * side_mask[s]
            result = term if result is None else result + term
        return jnp.zeros((64, CH), BF) if result is None else result

    def fill(target, block, source):
        for k, tap in enumerate(TAPS):
            target[block * 64 : block * 64 + 64, k * CH : (k + 1) * CH] = choose(
                [source(*side_frame(s, tap)) for s in range(4)]
            )

    def field_source(j):
        def source(delta, dt):
            return block_at(delta + 1, j) if dt == 0 else nb[(dt + 1) // 2, delta + 1, j]
        return source

    def grad_source(e, j):
        def source(delta, dt):
            depth = e - delta
            if depth not in (0, 1):
                return None
            return xs[2 + depth, j] if dt == 0 else nb[(1 - dt) // 2, 3 + depth, j]
        return source

    def corner_source(which, value):
        def source(delta, dt):
            return value if (delta, dt) == (-1, 2 * which - 1) else None
        return source

    order_pre = (2, 3, 1, 4)
    for block, j in enumerate(order_pre):
        fill(lp, block, field_source(j))
    order_back = [(0, 2), (0, 3), (-1, 2), (-1, 3), None, None, (0, 1), (0, 4), (-1, 1), (-1, 4)]
    for block, at in enumerate(order_back):
        fill(lg, block, corner_source(block - 4, cg[block - 4]) if at is None else grad_source(*at))

    pre = mm(lp[...], w1_ref[...].reshape(9 * CH, CH))
    back = mm(lg[...], w2t[...])

    def back_block(e, j):
        block = order_back.index((e, j))
        return back[block * 64 : block * 64 + 64]

    for j in range(1, 5):
        ss[j] = mm(partner, back_block(-1, j).astype(BF))

    def corner_sums(low, high):
        low = (low * row_line).astype(BF)
        high = (high * row_line).astype(BF)
        return mm_t(lo_zero, low) + mm_t(hi_zero, high), mm_t(lo_end, low) + mm_t(hi_end, high)

    corner_low, corner_high = back[256:320], back[320:384]

    def close_ends(zero, end):
        at_zero, at_end = corner_sums(corner_low, corner_high)
        head = pick_f(ss[zero], ss[end]) + at_zero
        tail = pick_f(ss[end], ss[zero]) + at_end
        head_b, tail_b = head.astype(BF), tail.astype(BF)
        head += mm(near[0], head_b) + mm(near[1], tail_b)
        tail += mm(far[0], head_b) + mm(far[1], tail_b)
        ss[zero] = pick_f(head, tail)
        ss[end] = pick_f(tail, head)

    @pl.when(band == 0)
    def _():
        close_ends(2, 1)

    @pl.when(band == BANDS - 1)
    def _():
        close_ends(4, 3)

    unique = {}
    hid = {}
    for block, j in enumerate(order_pre):
        value = pre[block * 64 : block * 64 + 64]
        hidden, slope = silu_parts(value)
        t = (2 * band - 2 + j) & (SPAN - 1)
        corner = jnp.logical_or(t == 0, t == SPAN - 1)
        unique[j] = jnp.where(corner, row_line, jnp.ones_like(row_line))
        grad = ((back_block(0, j) + ss[j]) * slope).astype(BF)
        gp[j] = grad
        gpu[j] = (grad.astype(F32) * unique[j]).astype(BF)
        hid[j] = hidden.astype(BF)

    mine = (home == group * 16).astype(F32)
    edge = jnp.where(band == 0, 1.0, 0.0) * mine * row_line

    def scaled(value, factor):
        return (value.astype(F32) * factor).astype(BF)

    h_zero, h_end = pick(hid[2], hid[1]), pick(hid[1], hid[2])
    cells = jnp.concatenate([
        scaled(hid[2], mine * unique[2]),
        scaled(hid[3], mine * unique[3]),
        scaled(mm(partner, hid[2]), mine),
        scaled(mm(partner, hid[3]), mine),
        scaled(mm(lo_zero, h_zero) + mm(lo_end, h_end), edge),
        scaled(mm(hi_zero, h_zero) + mm(hi_end, h_end), edge),
    ], axis=0)
    second = mm_t(cells, lg[0:384, :])
    own = jnp.concatenate([scaled(gpu[2], mine), scaled(gpu[3], mine)], axis=0)
    first = mm_t(lp[0:128, :], own)

    at_first, at_last = band == 0, band == BANDS - 1
    inner_low = jnp.where(at_first, 0.0, 1.0)
    inner_high = jnp.where(at_last, 0.0, 1.0)

    def spread_source(e, j, ref):
        def source(delta, dt):
            if e - delta != 0:
                return None
            if dt == 0:
                return ref[j]
            before = scaled(ref[1], inner_low) if j == 2 else ref[2]
            after = ref[3] if j == 2 else scaled(ref[4], inner_high)
            return pick(before, after) if dt == 1 else pick(after, before)
        return source

    g_zero = jnp.where(at_first, gp[2], gp[4])
    g_end = jnp.where(at_first, gp[1], gp[3])
    g_zero, g_end = pick(g_zero, g_end), pick(g_end, g_zero)
    order_in = [(0, 2), (0, 3), (1, 2), (1, 3), (-1, 2), (-1, 3), None, None]
    for block, at in enumerate(order_in):
        if at is None:
            fill(lc, block, corner_source(block - 6, (g_zero, g_end)[block - 6]))
        else:
            fill(lc, block, spread_source(*at, gp if at[0] == -1 else gpu))
    back = mm(lc[...], w1t[...])
    part = [back[k * 64 : k * 64 + 64] for k in range(8)]
    at_zero, at_end = corner_sums(part[6], part[7])
    owe[0] = part[0] + mm(partner, part[4].astype(BF)) + pick_f(at_zero, at_end) * (1.0 - inner_low)
    owe[1] = part[2]
    owe[2] = part[1] + mm(partner, part[5].astype(BF)) + pick_f(at_end, at_zero) * (1.0 - inner_high)
    owe[3] = part[3]

    tile = jnp.concatenate([owe[k, pl.ds(pl.multiple_of(group * 16, 16), 16), :] for k in range(4)], axis=0)
    tails = mm(sel_ref[...], tile.astype(BF))
    total[0:1152, :] += first
    for k in range(9):
        total[1152 + k * CH : 1152 + (k + 1) * CH, :] += second[:, k * CH : (k + 1) * CH]
    sent[...] = jnp.zeros_like(sent)
    for q in range(2):
        for face in range(3):
            for row in range(2):
                piece = done[pl.ds(q * 192 + face * 64 + row, BANDS, stride=2), :]
                sent[pl.ds((q * 3 + face) * 2 + row, BANDS, stride=16), :] = piece
    for i in range(BANDS):
        half = i // 16
        tail = tails[half * 40 : half * 40 + 40]
        pixels = jnp.concatenate([sent[i * 16 : i * 16 + 16, :], jnp.zeros((32, CH), F32)], axis=0)
        shifted = jnp.concatenate([jnp.zeros((8, CH), F32), tail], axis=0)
        out_ref[i] = jnp.concatenate([total[CHUNK * i : CHUNK * i + CHUNK, :], pixels + shifted], axis=0).astype(BF)


def tail_selector():
    select = np.zeros((80, 64), np.float32)
    for half in range(2):
        for pos in range(2):
            for depth in range(2):
                for face in range(3):
                    lane = (pos * 2 + depth) * 16 + face
                    select[half * 40 + 4 + (pos * 2 + depth) * 3 + face, lane + half * 3] = 1
                    for side in range(2):
                        row = 16 + ((pos * 2 + side) * 2 + depth) * 3 + face
                        select[half * 40 + row, lane + 6 + 3 * side] = 1
    return select


def order_selector():
    select = np.zeros((2, 64, 64), np.float32)
    for pos in range(2):
        for b in range(BANDS):
            select[0, 2 * b + pos, pos * 32 + b] = 1
            select[1, 63 - 2 * b - pos, pos * 32 + b] = 1
    return select


def reduce_kernel(in_ref, sum_ref):
    total = in_ref[0].astype(F32)
    for i in range(1, BANDS):
        total = total + in_ref[i].astype(F32)
    sum_ref[...] = total[0:CHUNK]


def spread_kernel(factor, in_ref, out_ref):
    total = (in_ref[0] + in_ref[1]) + (in_ref[2] + in_ref[3])
    total = (total * factor).astype(BF)
    for i in range(BANDS):
        out_ref[i] = total


def final_kernel(fn_ref, rot_ref, sel_ref, in_ref, sum_ref, out_ref, first_ref, second_ref, wide, total):
    first_ref[...] = sum_ref[0:16].astype(F32).reshape(1152, CH)
    second_ref[...] = sum_ref[16:32].astype(F32).reshape(1152, CH)
    band, group = here()
    for i in range(BANDS):
        wide[i * TAIL : (i + 1) * TAIL, :] = in_ref[i].astype(F32)[CHUNK:SLOT_TWO]
    for q in range(2):
        for face in range(3):
            for row in range(2):
                piece = wide[pl.ds((q * 3 + face) * 2 + row, BANDS, stride=TAIL), :]
                total[row, face, pl.ds(q, BANDS, stride=2), :] = piece
    tiles = [wide[pl.ds(pl.multiple_of(src * TAIL, TAIL), TAIL), :] for src in (band, BANDS - 1 - band)]
    for side in range(2):
        for face in range(3):
            flip = is_mirrored(fn_ref, rot_ref, 3 * group + face, 2 + side) == 1
            for row in range(2):
                for depth in range(2):
                    column = depth if side == 0 else 63 - depth
                    k, m = [24 + ((pos * 2 + side) * 2 + depth) * 3 + face for pos in (row, 1 - row)]
                    extra = jnp.where(flip, tiles[1][m : m + 1, :], tiles[0][k : k + 1, :])
                    total[row, face, column : column + 1, :] += extra

    @pl.when((band == 0) | (band == BANDS - 1))
    def _():
        side = jnp.where(band == 0, 0, 1)
        for face in range(3):
            order = sel_ref[is_mirrored(fn_ref, rot_ref, 3 * group + face, side)]
            for depth in range(2):
                halves = [wide[pl.ds(12 + (pos * 2 + depth) * 3 + face, BANDS, stride=TAIL), :] for pos in range(2)]
                extra = mm(order, jnp.concatenate(halves, axis=0).astype(BF))
                row = jnp.where(band == 0, depth, 1 - depth)
                total[row, face] += extra

    for row in range(2):
        for face in range(3):
            out_ref[face, row] = total[row, face].astype(BF)


def body(field_in, grad_out, first_weight, second_weight, face_neighbour, seam_rotation, corner_fill):
    factor = (1.0 * 12 * SPAN * SPAN) ** -0.5
    seams = (face_neighbour.T, seam_rotation.T)
    in_smem = {0: "s", 1: "s"}

    slots = call(
        pack_lines,
        jax.ShapeDtypeStruct((BANDS, SLOT_ONE, CH), BF),
        [
            pltpu.VMEM((2, 3, 2, SPAN, CH), BF),
            pltpu.VMEM(((SPAN + 4) * 12, CH), F32),
            pltpu.VMEM((STRIP, CH), F32),
            pltpu.SemaphoreType.DMA((2,)),
        ],
        (field_in, grad_out),
        {0: "a", 1: "a"},
    )
    strips = lax.all_to_all(slots, "tile", 0, 0, tiled=True)
    lines = call(
        gather_lines,
        jax.ShapeDtypeStruct((WINDOW, 64, CH), BF),
        [],
        (*seams, jnp.asarray(line_selector(), BF), jnp.asarray(ends_selector(), BF), strips),
        in_smem,
    )
    lines = lax.all_gather(lines, "sub", axis=0)

    slots = call(
        main_kernel,
        jax.ShapeDtypeStruct((BANDS, SLOT_TWO, CH), BF),
        [
            pltpu.VMEM((1152, CH), F32),
            pltpu.VMEM((1152, CH), F32),
            pltpu.VMEM((BANDS * STRIP, CH), F32),
            pltpu.VMEM((2304, CH), F32),
            pltpu.VMEM((384, CH), F32),
            pltpu.VMEM((BANDS * 16, CH), F32),
            pltpu.VMEM((1152, CH), BF),
            pltpu.VMEM((1152, CH), BF),
            pltpu.VMEM((4, WINDOW, 64, CH), BF),
            pltpu.VMEM((WINDOW, 64, CH), BF),
            pltpu.VMEM((2, 5, 5, 64, CH), BF),
            pltpu.VMEM((2, 64, CH), BF),
            pltpu.VMEM((256, 1152), BF),
            pltpu.VMEM((640, 1152), BF),
            pltpu.VMEM((512, 1152), BF),
            pltpu.VMEM((5, 64, CH), F32),
            pltpu.VMEM((5, 64, CH), BF),
            pltpu.VMEM((5, 64, CH), BF),
            pltpu.VMEM((4, 64, CH), F32),
        ],
        (*seams, corner_fill.T, jnp.asarray(tail_selector(), BF), lines, strips, first_weight, second_weight),
    )
    slots = lax.all_to_all(slots, "tile", 0, 0, tiled=True)
    part = call(reduce_kernel, jax.ShapeDtypeStruct((CHUNK, CH), F32), [], (slots,))
    part = lax.all_gather(part, "sub", axis=0)
    reduced = call(
        lambda *refs: spread_kernel(factor, *refs),
        jax.ShapeDtypeStruct((BANDS, CHUNK, CH), BF),
        [],
        (part,),
    )
    reduced = lax.all_to_all(reduced, "tile", 0, 0, tiled=True)
    grad_in, first, second = call(
        final_kernel,
        [
            jax.ShapeDtypeStruct((3, 2, SPAN, CH), BF),
            jax.ShapeDtypeStruct((1152, CH), F32),
            jax.ShapeDtypeStruct((1152, CH), F32),
        ],
        [pltpu.VMEM((BANDS * TAIL, CH), F32), pltpu.VMEM((2, 3, SPAN, CH), F32)],
        (*seams, jnp.asarray(order_selector(), BF), slots, reduced),
        in_smem,
    )
    return grad_in, first.reshape(3, 3, CH, CH), second.reshape(3, 3, CH, CH)


def solution(mesh):
    return jax.shard_map(
        body,
        mesh=mesh,
        in_specs=(P("sub", "tile", None, None), P("sub", "tile", None, None), P(), P(), P(), P(), P()),
        out_specs=(P("sub", "tile", None, None), P(), P()),
        check_vma=False,
    )
```

time: 104 us -> 95.1 us (0.914)
  blocking collectives: 33.9 us -> 81.9 us
  waiting for transfers between devices: 32.3 us -> 0 us
  starting transfers between devices: 20.4 us -> 0 us
  Pallas kernels: 12.6 us -> 9.25 us
  local copies, waits for them, and re-layouts: 3.03 us -> 1.83 us
    all_to_all x1 -> x3, blocking collectives: 24.8 us -> 66.5 us  [the longest x1 30.5 us: body(): strips = lax.all_to_all(slots, 'tile', 0, 0, tiled=True)]
    ppermute x2 -> x0, waiting for transfers between devices: 17.2 us -> none  [the longest x1 17.2 us: body(): below = lax.ppermute(pair, 'tile', down)]
    all_to_all x2 -> x0, waiting for transfers between devices: 15.2 us -> none  [the longest x1 15.2 us: body(): reduced = lax.all_to_all(reduced, BOTH, 0, 0, tiled=True)]
    all_to_all x2 -> x0, starting transfers between devices: 15.1 us -> none  [the longest x1 11.3 us: body(): slots = lax.all_to_all(slots, 'tile', 0, 0, tiled=True)]
    all_gather x0 -> x1, blocking collectives: none -> 7.11 us  [body(): part = lax.all_gather(part, 'sub', axis=0)]
    ppermute x2 -> x0, starting transfers between devices: 5.29 us -> none  [the longest x1 4 us: body(): above = lax.ppermute(pair, 'tile', up)]
    pallas_call x6, Pallas kernels: 12.6 us -> 9.25 us  [call(): pl.pallas_call(kernel, out_shape=outs, in_specs=[pl.BlockSpec(memory_spac...]
  transfers between devices with their start and end apart: 4 -> 0, of which waited for: 2 -> 0; matrix products, arithmetic and copies ran while one was open for 1% -> 0% of each run, Pallas kernels for 1% -> 0%
where the time goes in v2:
time: 95.1 us; the launch traced here: 93.8 us
  blocking collectives  81.9 us (86%)
  Pallas kernels  9.25 us (10%)
  local copies, waits for them, and re-layouts  1.83 us (2%)
    all_to_all x1, blocking collectives, body(): strips = lax.all_to_all(slots, 'tile', 0, 0, tiled=True)  30.5 us
    all_to_all x1, blocking collectives, body(): slots = lax.all_to_all(slots, 'tile', 0, 0, tiled=True)  19.5 us
    all_to_all x1, blocking collectives, body(): reduced = lax.all_to_all(reduced, 'tile', 0, 0, tiled=True)  16.4 us
    pallas_call x6, Pallas kernels, call(): pl.pallas_call(kernel, out_shape=outs, in_specs=[pl.BlockSpec(memory_spac...  9.25 us
    all_gather x1, blocking collectives, body(): lines = lax.all_gather(lines, 'sub', axis=0)  8.34 us
    all_gather x1, blocking collectives, body(): part = lax.all_gather(part, 'sub', axis=0)  7.11 us

profile of v2, /device:TPU:1, one launch (start us, length us, event | category | flops | bytes accessed | tf_op | source)
XLA Modules:
  0.0 93.8 jit_solution(17893549906962441615)
XLA Ops:
  0.6 0.0 copy-start.4
  0.6 0.9 copy-done.4
  1.5 0.0 copy-start.5
  1.5 0.9 copy-done.5
  2.4 0.4 shard_map.130
  2.8 0.0 copy-start
  2.8 0.0 copy-start.3
  2.9 0.0 copy-start.8
  2.9 0.0 copy-start.9
  2.9 30.5 %all_to_all.15.in_ref = bf16[32,144,128]{2,1,0:T(8,128)(2,1)S(1)} all-to-all(bf16[32,144,128]{2,1,0:T(8,128)(2,1)S(1)} %shard_map.130), channel_id=1, replica_groups=mesh['tile'=32,'sub'=4] {'tile'}, dimensions={0} | all-to-all | bytes 2359296 | tf_op jit(solution)/shard_map/all_to_all | solution.py:586
  33.4 0.0 copy-done
  33.4 0.0 copy-done.3
  33.4 0.0 copy-done.8
  33.4 0.0 copy-done.9
  33.4 0.0 copy-start.1
  33.4 0.0 copy-start.2
  33.5 0.0 copy-start.7
  33.5 0.0 copy-start.10
  33.5 1.1 %shard_map.131 = bf16[6,64,128]{2,1,0:T(8,128)(2,1)S(1)} custom-call(s32[4,12]{1,0:T(4,128)S(1)} %bitcast.9, s32[4,12]{1,0:T(4,128)S(1)} %bitcast.12, bf16[2,384,576]{2,1,0:T(8,128)(2,1)S(1)} %copy-done, bf16[4,48,144]{2,1,0:T(8,128)(2,1)S(1)} %copy-done.3, bf16[32,144,128]{2,1,0:T(8,128)(2,1)S(1)} %all_to_all.15.in_ref), custom_call_target="tpu_custom_call" | custom-call | tf_op jit(solution)/shard_map/pallas_call | solution.py:39
  34.6 8.3 %all-gather = bf16[24,64,128]{2,1,0:T(8,128)(2,1)S(1)} all-gather(bf16[6,64,128]{2,1,0:T(8,128)(2,1)S(1)} %shard_map.131), channel_id=2, replica_groups=mesh['tile'=32,'sub'=4] {'sub'}, dimensions={0}, use_global_device_ids=true | all-gather | bytes 491520 | tf_op jit(solution)/shard_map/all_gather | solution.py:594
  43.0 0.0 copy-done.1
  43.0 0.0 copy-done.2
  43.0 0.0 copy-done.7
  43.0 0.0 copy-done.10
  43.0 5.6 %shard_map.132 = bf16[32,120,128]{2,1,0:T(8,128)(2,1)S(1)} custom-call(s32[4,12]{1,0:T(4,128)S(1)} %bitcast.10, s32[4,12]{1,0:T(4,128)S(1)} %bitcast.13, s32[4,12]{1,0:T(4,128)S(1)} %bitcast.15, bf16[80,64]{1,0:T(8,128)(2,1)S(1)} %copy-done.7, bf16[4,6,64,128]{3,2,1,0:T(8,128)(2,1)S(1)} %bitcast.7, bf16[32,144,128]{2,1,0:T(8,128)(2,1)S(1)} %all_to_all.15.in_ref, ...), custom_call_target="tpu_custom_call" | custom-call | tf_op jit(solution)/shard_map/pallas_call | solution.py:39
  48.5 19.5 %all_to_all.16.in_ref = bf16[32,120,128]{2,1,0:T(8,128)(2,1)S(1)} all-to-all(bf16[32,120,128]{2,1,0:T(8,128)(2,1)S(1)} %shard_map.132), channel_id=1, replica_groups=mesh['tile'=32,'sub'=4] {'tile'}, dimensions={0} | all-to-all | bytes 1966080 | tf_op jit(solution)/shard_map/all_to_all | solution.py:622
  68.1 0.1 shard_map.133
  68.2 0.0 copy-start.6
  68.2 7.1 %all-gather.1 = f32[288,128]{1,0:T(8,128)S(1)} all-gather(f32[72,128]{1,0:T(8,128)S(1)} %shard_map.133), channel_id=3, replica_groups=mesh['tile'=32,'sub'=4] {'sub'}, dimensions={0}, use_global_device_ids=true | all-gather | bytes 184320 | tf_op jit(solution)/shard_map/all_gather | solution.py:624
  75.3 16.4 %all_to_all.17.sum_ref = bf16[32,72,128]{2,1,0:T(8,128)(2,1)S(1)} all-to-all(bf16[32,72,128]{2,1,0:T(8,128)(2,1)S(1)} %shard_map.134), channel_id=1, replica_groups=mesh['tile'=32,'sub'=4] {'tile'}, dimensions={0} | all-to-all | bytes 1179648 | tf_op jit(solution)/shard_map/all_to_all | solution.py:631
  91.8 0.0 copy-done.6
  91.8 2.0 %shard_map.135 = (bf16[3,2,64,128]{3,2,1,0:T(8,128)(2,1)}, f32[1152,128]{1,0:T(8,128)}, f32[1152,128]{1,0:T(8,128)}) custom-call(s32[4,12]{1,0:T(4,128)S(1)} %bitcast.11, s32[4,12]{1,0:T(4,128)S(1)} %bitcast.14, bf16[2,64,64]{2,1,0:T(8,128)(2,1)S(1)} %copy-done.6, bf16[32,120,128]{2,1,0:T(8,128)(2,1)S(1)} %all_to_all.16.in_ref, ...), custom_call_target="tpu_custom_call" | custom-call | tf_op jit(solution)/shard_map/pallas_call | solution.py:39
  (1 shorter events, 0.0 us)
Async XLA Ops:
  0.6 0.9 copy-start.4
  1.5 0.9 copy-start.5
  2.8 30.6 %copy-start = (bf16[2,384,576]{2,1,0:T(8,128)(2,1)S(1)}, bf16[2,384,576]{2,1,0:T(8,128)(2,1)}, u32[]{:S(2)}) copy-start(bf16[2,384,576]{2,1,0:T(8,128)(2,1)} %constant.8.clone.sel_ref) | copy-start | bytes 2654212
  2.8 30.6 %copy-start.3 = (bf16[4,48,144]{2,1,0:T(8,128)(2,1)S(1)}, bf16[4,48,144]{2,1,0:T(8,128)(2,1)}, u32[]{:S(2)}) copy-start(bf16[4,48,144]{2,1,0:T(8,128)(2,1)} %constant.9.clone.ends_ref) | copy-start | bytes 165892
  2.9 30.6 %copy-start.8 = (s32[12,4]{0,1:T(4,128)S(1)}, s32[12,4]{0,1:T(4,128)}, u32[]{:S(2)}) copy-start(s32[12,4]{0,1:T(4,128)} %param.15) | copy-start | bytes 580
  2.9 30.6 %copy-start.9 = (s32[12,4]{0,1:T(4,128)S(1)}, s32[12,4]{0,1:T(4,128)}, u32[]{:S(2)}) copy-start(s32[12,4]{0,1:T(4,128)} %param.16) | copy-start | bytes 580
  33.4 9.5 %copy-start.1 = (bf16[3,3,128,128]{3,2,1,0:T(8,128)(2,1)S(1)}, bf16[3,3,128,128]{3,2,1,0:T(8,128)(2,1)}, u32[]{:S(2)}) copy-start(bf16[3,3,128,128]{3,2,1,0:T(8,128)(2,1)} %w1_ref.1) | copy-start | bytes 884740
  33.4 9.5 %copy-start.2 = (bf16[3,3,128,128]{3,2,1,0:T(8,128)(2,1)S(1)}, bf16[3,3,128,128]{3,2,1,0:T(8,128)(2,1)}, u32[]{:S(2)}) copy-start(bf16[3,3,128,128]{3,2,1,0:T(8,128)(2,1)} %w2_ref.1) | copy-start | bytes 884740
  33.5 9.5 %copy-start.7 = (bf16[80,64]{1,0:T(8,128)(2,1)S(1)}, bf16[80,64]{1,0:T(8,128)(2,1)}, u32[]{:S(2)}) copy-start(bf16[80,64]{1,0:T(8,128)(2,1)} %constant.10.clone.sel_ref) | copy-start | bytes 30724
  33.5 9.5 %copy-start.10 = (s32[12,4]{0,1:T(4,128)S(1)}, s32[12,4]{0,1:T(4,128)}, u32[]{:S(2)}) copy-start(s32[12,4]{0,1:T(4,128)} %param.17) | copy-start | bytes 580
  68.2 23.6 %copy-start.6 = (bf16[2,64,64]{2,1,0:T(8,128)(2,1)S(1)}, bf16[2,64,64]{2,1,0:T(8,128)(2,1)}, u32[]{:S(2)}) copy-start(bf16[2,64,64]{2,1,0:T(8,128)(2,1)} %constant.11.clone.sel_ref) | copy-start | bytes 49156

commit v3 on v2

--- a/solution.py
+++ b/solution.py
@@ -32,7 +32,7 @@
 
 
 def call(kernel, outs, scratch, operands, places=(), aliases=None):
-    kinds = {"v": pltpu.VMEM, "s": pltpu.SMEM, "a": pl.ANY}
+    kinds = {"v": pltpu.VMEM, "s": pltpu.SMEM, "h": pltpu.HBM}
     places = dict(places)
     many = isinstance(outs, (list, tuple))
     out_specs = [pl.BlockSpec(memory_space=kinds[places.get(f"o{k}", "v")]) for k in range(len(outs) if many else 1)]
@@ -134,12 +134,13 @@
         block = in_ref[source].astype(F32)[STRIP : STRIP + ENDS]
         ends.append(jnp.where(source == 0, first_ends, jnp.where(source == BANDS - 1, last_ends, block)))
     pieces = jnp.concatenate([first.astype(F32), last.astype(F32)] + ends, axis=0).astype(BF)
-    place = lax.broadcasted_iota(I32, (WINDOW * 64, CH), 0) & 15
-    flip = jnp.zeros((WINDOW * 64, CH), I32)
+    place = lax.broadcasted_iota(I32, (WINDOW * 64, 1), 0) & 15
+    flip = jnp.zeros((WINDOW * 64, 1), I32)
     for side in range(4):
         for face in range(3):
             flip = jnp.where(place == side * 3 + face, is_mirrored(fn_ref, rot_ref, 3 * group + face, side), flip)
-    picked = jnp.where(flip == 1, mm(sel_ref[1], pieces), mm(sel_ref[0], pieces)).astype(BF)
+    flip = jnp.broadcast_to(flip.astype(F32), sel_ref.shape[1:]).astype(BF)
+    picked = mm(sel_ref[0] * (1 - flip) + sel_ref[1] * flip, pieces).astype(BF)
     for j in range(WINDOW):
         out_ref[j] = picked[j * 64 : j * 64 + 64]
 
@@ -159,7 +160,10 @@
         out[k * CH : (k + 1) * CH, :] = ref[a, b].T
 
 
-def interior(band, in_ref, w1_ref, w1t, w2t, f2, g2, wide, acc, done):
+def interior_kernel(in_ref, w1_ref, w2_ref, acc, done, w1t, w2t, f2, g2, wide):
+    band, _ = here()
+    transpose_weights(w1_ref, w1t)
+    transpose_weights(w2_ref, w2t)
     for s in range(BANDS):
         wide[s * STRIP : (s + 1) * STRIP, :] = in_ref[s].astype(F32)[0:STRIP]
     for q in range(WINDOW):
@@ -218,14 +222,13 @@
 
 
 def main_kernel(
-    fn_ref, rot_ref, fill_ref, sel_ref, a_ref, in_ref, w1_ref, w2_ref,
+    fn_ref, rot_ref, fill_ref, sel_ref, own_ref, one_ref, two_ref, three_ref, acc, done, w1_ref, w2_ref,
     out_ref,
-    f2, g2, wide, total, done, sent, w1t, w2t, xs, hal, nb, cg, lp, lg, lc, ss, gp, gpu, owe,
+    total, sent, w1t, w2t, xs, hal, nb, cg, lp, lg, lc, ss, gp, gpu, owe,
 ):
     band, group = here()
     transpose_weights(w1_ref, w1t)
     transpose_weights(w2_ref, w2t)
-    interior(band, in_ref, w1_ref, w1t, w2t, f2, g2, wide, total, done)
 
     line = lax.broadcasted_iota(I32, (64, 1), 0)
     place = line & 15
@@ -279,9 +282,11 @@
     def pick_f(plain, mirrored):
         return jnp.where(flip_f > 0.5, mirrored, plain)
 
-    for j in range(WINDOW):
-        for block in range(4):
-            xs[block, j] = jnp.concatenate([a_ref[g, j, block * 16 : block * 16 + 16, :] for g in range(4)], axis=0)
+    for step, ref in enumerate((own_ref, one_ref, two_ref, three_ref)):
+        start = pl.multiple_of(((group - step) & 3) * 16, 16)
+        for j in range(WINDOW):
+            for block in range(4):
+                xs[block, j, pl.ds(start, 16), :] = ref[j, block * 16 : block * 16 + 16, :]
     for j in range(WINDOW):
         hal[j] = mm(partner, xs[0, j]).astype(BF)
 
@@ -474,9 +479,10 @@
 
     tile = jnp.concatenate([owe[k, pl.ds(pl.multiple_of(group * 16, 16), 16), :] for k in range(4)], axis=0)
     tails = mm(sel_ref[...], tile.astype(BF))
-    total[0:1152, :] += first
+    total[0:1152, :] = acc[0:1152, :] + first
     for k in range(9):
-        total[1152 + k * CH : 1152 + (k + 1) * CH, :] += second[:, k * CH : (k + 1) * CH]
+        low = 1152 + k * CH
+        total[low : low + CH, :] = acc[low : low + CH, :] + second[:, k * CH : (k + 1) * CH]
     sent[...] = jnp.zeros_like(sent)
     for q in range(2):
         for face in range(3):
@@ -521,8 +527,11 @@
     sum_ref[...] = total[0:CHUNK]
 
 
-def spread_kernel(factor, in_ref, out_ref):
-    total = (in_ref[0] + in_ref[1]) + (in_ref[2] + in_ref[3])
+def spread_kernel(factor, own_ref, one_ref, two_ref, three_ref, out_ref, parts):
+    _, group = here()
+    for step, ref in enumerate((own_ref, one_ref, two_ref, three_ref)):
+        parts[(group - step) & 3] = ref[...]
+    total = (parts[0] + parts[1]) + (parts[2] + parts[3])
     total = (total * factor).astype(BF)
     for i in range(BANDS):
         out_ref[i] = total
@@ -566,6 +575,11 @@
             out_ref[face, row] = total[row, face].astype(BF)
 
 
+def around(value):
+    moved = [lax.ppermute(value, "sub", [(i, (i + step) % 4) for i in range(4)]) for step in (1, 2, 3)]
+    return (value, *moved)
+
+
 def body(field_in, grad_out, first_weight, second_weight, face_neighbour, seam_rotation, corner_fill):
     factor = (1.0 * 12 * SPAN * SPAN) ** -0.5
     seams = (face_neighbour.T, seam_rotation.T)
@@ -580,8 +594,8 @@
             pltpu.VMEM((STRIP, CH), F32),
             pltpu.SemaphoreType.DMA((2,)),
         ],
-        (field_in, grad_out),
-        {0: "a", 1: "a"},
+        tuple(pltpu.with_memory_space_constraint(value, pltpu.HBM) for value in (field_in, grad_out)),
+        {0: "h", 1: "h"},
     )
     strips = lax.all_to_all(slots, "tile", 0, 0, tiled=True)
     lines = call(
@@ -591,17 +605,25 @@
         (*seams, jnp.asarray(line_selector(), BF), jnp.asarray(ends_selector(), BF), strips),
         in_smem,
     )
-    lines = lax.all_gather(lines, "sub", axis=0)
+    lines = around(lines)
+    acc, done = call(
+        interior_kernel,
+        [jax.ShapeDtypeStruct((2304, CH), F32), jax.ShapeDtypeStruct((384, CH), F32)],
+        [
+            pltpu.VMEM((1152, CH), BF),
+            pltpu.VMEM((1152, CH), BF),
+            pltpu.VMEM((1152, CH), F32),
+            pltpu.VMEM((1152, CH), F32),
+            pltpu.VMEM((BANDS * STRIP, CH), F32),
+        ],
+        (strips, first_weight, second_weight),
+    )
 
     slots = call(
         main_kernel,
         jax.ShapeDtypeStruct((BANDS, SLOT_TWO, CH), BF),
         [
-            pltpu.VMEM((1152, CH), F32),
-            pltpu.VMEM((1152, CH), F32),
-            pltpu.VMEM((BANDS * STRIP, CH), F32),
             pltpu.VMEM((2304, CH), F32),
-            pltpu.VMEM((384, CH), F32),
             pltpu.VMEM((BANDS * 16, CH), F32),
             pltpu.VMEM((1152, CH), BF),
             pltpu.VMEM((1152, CH), BF),
@@ -617,16 +639,16 @@
             pltpu.VMEM((5, 64, CH), BF),
             pltpu.VMEM((4, 64, CH), F32),
         ],
-        (*seams, corner_fill.T, jnp.asarray(tail_selector(), BF), lines, strips, first_weight, second_weight),
+        (*seams, corner_fill.T, jnp.asarray(tail_selector(), BF), *lines, acc, done, first_weight, second_weight),
     )
     slots = lax.all_to_all(slots, "tile", 0, 0, tiled=True)
     part = call(reduce_kernel, jax.ShapeDtypeStruct((CHUNK, CH), F32), [], (slots,))
-    part = lax.all_gather(part, "sub", axis=0)
+    part = around(part)
     reduced = call(
         lambda *refs: spread_kernel(factor, *refs),
         jax.ShapeDtypeStruct((BANDS, CHUNK, CH), BF),
-        [],
-        (part,),
+        [pltpu.VMEM((4, CHUNK, CH), F32)],
+        part,
     )
     reduced = lax.all_to_all(reduced, "tile", 0, 0, tiled=True)
     grad_in, first, second = call(
@@ -636,7 +658,10 @@
             jax.ShapeDtypeStruct((1152, CH), F32),
             jax.ShapeDtypeStruct((1152, CH), F32),
         ],
-        [pltpu.VMEM((BANDS * TAIL, CH), F32), pltpu.VMEM((2, 3, SPAN, CH), F32)],
+        [
+            pltpu.VMEM((BANDS * TAIL, CH), F32),
+            pltpu.VMEM((2, 3, SPAN, CH), F32),
+        ],
         (*seams, jnp.asarray(order_selector(), BF), slots, reduced),
         in_smem,
     )

time: 95.1 us -> 89.4 us (0.940)
  the two profiles are of different devices: /device:TPU:1 before, /device:TPU:0 now
where the time goes in v3:
time: 89.4 us; the launch traced here: 89.2 us
  blocking collectives  68.7 us (77%)
  Pallas kernels  10.1 us (11%)
  waiting for transfers between devices  7.34 us (8%)
  starting transfers between devices  2.16 us (2%)
    all_to_all x1, blocking collectives, body(): strips = lax.all_to_all(slots, 'tile', 0, 0, tiled=True)  31.5 us
    all_to_all x1, blocking collectives, body(): slots = lax.all_to_all(slots, 'tile', 0, 0, tiled=True)  19.9 us
    all_to_all x1, blocking collectives, body(): reduced = lax.all_to_all(reduced, 'tile', 0, 0, tiled=True)  17.3 us
    pallas_call x7, Pallas kernels, call(): pl.pallas_call(kernel, out_shape=outs, in_specs=[pl.BlockSpec(memory_spac...  10.1 us
    ppermute x6, waiting for transfers between devices, around(): lax.ppermute(value, 'sub', [(i, (i + step) % 4) for i in range(4)])  7.34 us
    ppermute x6, starting transfers between devices, around(): lax.ppermute(value, 'sub', [(i, (i + step) % 4) for i in range(4)])  2.16 us
  transfers between devices with their start and end apart: 6, of which 4 were waited for; matrix products, arithmetic and copies ran while one was open for 0% of the time, Pallas kernels for 2%

profile of v3, /device:TPU:0, one launch (start us, length us, event | category | flops | bytes accessed | tf_op | source)
XLA Modules:
  0.0 89.2 jit_solution(4417622807432288949)
XLA Ops:
  0.6 1.1 %shard_map.130 = bf16[32,144,128]{2,1,0:T(8,128)(2,1)S(1)} custom-call(bf16[3,2,64,128]{3,2,1,0:T(8,128)(2,1)} %f_hbm.1, bf16[3,2,64,128]{3,2,1,0:T(8,128)(2,1)} %g_hbm.1), custom_call_target="tpu_custom_call" | custom-call | tf_op jit(solution)/shard_map/pallas_call | solution.py:39
  1.7 0.0 copy-start.2
  1.7 0.0 copy-start.3
  1.8 0.0 copy-start.6
  1.8 0.0 copy-start.7
  1.8 31.5 %all_to_all.15.in_ref = bf16[32,144,128]{2,1,0:T(8,128)(2,1)S(1)} all-to-all(bf16[32,144,128]{2,1,0:T(8,128)(2,1)S(1)} %shard_map.130), channel_id=1, replica_groups=mesh['tile'=32,'sub'=4] {'tile'}, dimensions={0} | all-to-all | bytes 2359296 | tf_op jit(solution)/shard_map/all_to_all | solution.py:600
  33.2 0.0 copy-done.2
  33.2 0.0 copy-done.3
  33.2 0.0 copy-done.6
  33.3 0.0 copy-done.7
  33.3 0.0 copy-start
  33.3 0.0 copy-start.1
  33.3 1.0 %shard_map.131.own_ref = bf16[6,64,128]{2,1,0:T(8,128)(2,1)S(1)} custom-call(s32[4,12]{1,0:T(4,128)S(1)} %bitcast.5, s32[4,12]{1,0:T(4,128)S(1)} %bitcast.8, bf16[2,384,576]{2,1,0:T(8,128)(2,1)S(1)} %copy-done.2, bf16[4,48,144]{2,1,0:T(8,128)(2,1)S(1)} %copy-done.3, bf16[32,144,128]{2,1,0:T(8,128)(2,1)S(1)} %all_to_all.15.in_ref), custom_call_target="tpu_custom_call" | custom-call | tf_op jit(solution)/shard_map/pallas_call | solution.py:39
  34.3 0.0 copy-start.5
  34.3 0.0 copy-start.8
  34.4 0.1 collective-permute-start.2
  34.4 1.1 %collective-permute-start.1 = (bf16[6,64,128]{2,1,0:T(8,128)(2,1)S(1)}, bf16[6,64,128]{2,1,0:T(8,128)(2,1)S(1)}, u32[]{:S(2)}, u32[]{:S(2)}) collective-permute-start(bf16[6,64,128]{2,1,0:T(8,128)(2,1)S(1)} %shard_map.131.own_ref), channel_id=1, source_target_pairs={{0,2},{1,3},{2,0},{3,1},{4,6},{5,7},{6,4},{7,5},{8,10},{9,11},{10,... | collective-permute-start | bytes 294920 | tf_op jit(solution)/shard_map/ppermute | solution.py:579
  35.5 0.2 collective-permute-start
  35.7 0.0 copy-done
  35.7 0.0 copy-done.1
  35.7 1.8 %shard_map.132 = (f32[2304,128]{1,0:T(8,128)S(1)}, f32[384,128]{1,0:T(8,128)S(1)}) custom-call(bf16[32,144,128]{2,1,0:T(8,128)(2,1)S(1)} %all_to_all.15.in_ref, bf16[3,3,128,128]{3,2,1,0:T(8,128)(2,1)S(1)} %copy-done, bf16[3,3,128,128]{3,2,1,0:T(8,128)(2,1)S(1)} %copy-done.1), custom_call_target="tpu_custom_call" | custom-call | tf_op jit(solution)/shard_map/pallas_call | solution.py:39
  37.5 0.0 collective-permute-done.2.three_ref
  37.5 3.2 %collective-permute-done.1.two_ref = bf16[6,64,128]{2,1,0:T(8,128)(2,1)S(1)} collective-permute-done((bf16[6,64,128]{2,1,0:T(8,128)(2,1)S(1)}, bf16[6,64,128]{2,1,0:T(8,128)(2,1)S(1)}, u32[]{:S(2)}, u32[]{:S(2)}) %collective-permute-start.1) | collective-permute-done | bytes 98336 | tf_op jit(solution)/shard_map/ppermute | solution.py:579
  40.7 0.5 collective-permute-done.one_ref
  41.2 0.0 copy-done.5
  41.2 0.0 copy-done.8
  41.2 4.0 %shard_map.133 = bf16[32,120,128]{2,1,0:T(8,128)(2,1)S(1)} custom-call(s32[4,12]{1,0:T(4,128)S(1)} %bitcast.6, s32[4,12]{1,0:T(4,128)S(1)} %bitcast.9, s32[4,12]{1,0:T(4,128)S(1)} %bitcast.11, bf16[80,64]{1,0:T(8,128)(2,1)S(1)} %copy-done.5, bf16[6,64,128]{2,1,0:T(8,128)(2,1)S(1)} %shard_map.131.own_ref, ...), custom_call_target="tpu_custom_call" | custom-call | tf_op jit(solution)/shard_map/pallas_call | solution.py:39
  45.2 19.9 %all_to_all.16.in_ref = bf16[32,120,128]{2,1,0:T(8,128)(2,1)S(1)} all-to-all(bf16[32,120,128]{2,1,0:T(8,128)(2,1)S(1)} %shard_map.133), channel_id=1, replica_groups=mesh['tile'=32,'sub'=4] {'tile'}, dimensions={0} | all-to-all | bytes 1966080 | tf_op jit(solution)/shard_map/all_to_all | solution.py:644
  65.2 0.1 shard_map.134.refs_0_
  65.2 0.0 copy-start.4
  65.3 0.1 collective-permute-start.5
  65.3 0.6 collective-permute-start.4
  65.9 0.2 collective-permute-start.3
  66.1 1.0 %collective-permute-done.5.refs_3_ = f32[72,128]{1,0:T(8,128)S(1)} collective-permute-done((f32[72,128]{1,0:T(8,128)S(1)}, f32[72,128]{1,0:T(8,128)S(1)}, u32[]{:S(2)}, u32[]{:S(2)}) %collective-permute-start.5) | collective-permute-done | bytes 36896 | tf_op jit(solution)/shard_map/ppermute | solution.py:579
  67.1 2.6 %collective-permute-done.4.refs_2_ = f32[72,128]{1,0:T(8,128)S(1)} collective-permute-done((f32[72,128]{1,0:T(8,128)S(1)}, f32[72,128]{1,0:T(8,128)S(1)}, u32[]{:S(2)}, u32[]{:S(2)}) %collective-permute-start.4) | collective-permute-done | bytes 36896 | tf_op jit(solution)/shard_map/ppermute | solution.py:579
  69.7 0.0 collective-permute-done.3.refs_1_
  69.7 0.1 shard_map.135
  69.8 17.3 %all_to_all.17.sum_ref = bf16[32,72,128]{2,1,0:T(8,128)(2,1)S(1)} all-to-all(bf16[32,72,128]{2,1,0:T(8,128)(2,1)S(1)} %shard_map.135), channel_id=1, replica_groups=mesh['tile'=32,'sub'=4] {'tile'}, dimensions={0} | all-to-all | bytes 1179648 | tf_op jit(solution)/shard_map/all_to_all | solution.py:653
  87.1 0.0 copy-done.4
  87.1 2.0 %shard_map.136 = (bf16[3,2,64,128]{3,2,1,0:T(8,128)(2,1)}, f32[1152,128]{1,0:T(8,128)}, f32[1152,128]{1,0:T(8,128)}) custom-call(s32[4,12]{1,0:T(4,128)S(1)} %bitcast.7, s32[4,12]{1,0:T(4,128)S(1)} %bitcast.10, bf16[2,64,64]{2,1,0:T(8,128)(2,1)S(1)} %copy-done.4, bf16[32,120,128]{2,1,0:T(8,128)(2,1)S(1)} %all_to_all.16.in_ref, ...), custom_call_target="tpu_custom_call" | custom-call | tf_op jit(solution)/shard_map/pallas_call | solution.py:39
Async XLA Ops:
  1.7 31.5 %copy-start.2 = (bf16[2,384,576]{2,1,0:T(8,128)(2,1)S(1)}, bf16[2,384,576]{2,1,0:T(8,128)(2,1)}, u32[]{:S(2)}) copy-start(bf16[2,384,576]{2,1,0:T(8,128)(2,1)} %constant.8.clone.sel_ref) | copy-start | bytes 2654212
  1.7 31.5 %copy-start.3 = (bf16[4,48,144]{2,1,0:T(8,128)(2,1)S(1)}, bf16[4,48,144]{2,1,0:T(8,128)(2,1)}, u32[]{:S(2)}) copy-start(bf16[4,48,144]{2,1,0:T(8,128)(2,1)} %constant.9.clone.ends_ref) | copy-start | bytes 165892
  1.8 31.5 %copy-start.6 = (s32[12,4]{0,1:T(4,128)S(1)}, s32[12,4]{0,1:T(4,128)}, u32[]{:S(2)}) copy-start(s32[12,4]{0,1:T(4,128)} %param.15) | copy-start | bytes 580
  1.8 31.5 %copy-start.7 = (s32[12,4]{0,1:T(4,128)S(1)}, s32[12,4]{0,1:T(4,128)}, u32[]{:S(2)}) copy-start(s32[12,4]{0,1:T(4,128)} %param.16) | copy-start | bytes 580
  33.3 2.4 %copy-start = (bf16[3,3,128,128]{3,2,1,0:T(8,128)(2,1)S(1)}, bf16[3,3,128,128]{3,2,1,0:T(8,128)(2,1)}, u32[]{:S(2)}) copy-start(bf16[3,3,128,128]{3,2,1,0:T(8,128)(2,1)} %w1_ref.3) | copy-start | bytes 884740
  33.3 2.4 %copy-start.1 = (bf16[3,3,128,128]{3,2,1,0:T(8,128)(2,1)S(1)}, bf16[3,3,128,128]{3,2,1,0:T(8,128)(2,1)}, u32[]{:S(2)}) copy-start(bf16[3,3,128,128]{3,2,1,0:T(8,128)(2,1)} %w2_ref.3) | copy-start | bytes 884740
  34.3 6.9 %copy-start.5 = (bf16[80,64]{1,0:T(8,128)(2,1)S(1)}, bf16[80,64]{1,0:T(8,128)(2,1)}, u32[]{:S(2)}) copy-start(bf16[80,64]{1,0:T(8,128)(2,1)} %constant.10.clone.sel_ref) | copy-start | bytes 30724
  34.3 6.9 %copy-start.8 = (s32[12,4]{0,1:T(4,128)S(1)}, s32[12,4]{0,1:T(4,128)}, u32[]{:S(2)}) copy-start(s32[12,4]{0,1:T(4,128)} %param.17) | copy-start | bytes 580
  34.4 3.1 %collective-permute-start.2 = (bf16[6,64,128]{2,1,0:T(8,128)(2,1)S(1)}, bf16[6,64,128]{2,1,0:T(8,128)(2,1)S(1)}, u32[]{:S(2)}, u32[]{:S(2)}) collective-permute-start(bf16[6,64,128]{2,1,0:T(8,128)(2,1)S(1)} %shard_map.131.own_ref), channel_id=1, source_target_pairs={{0,3},{1,0},{2,1},{3,2},{4,7},{5,4},{6,5},{7,6},{8,11},{9,8},{10,9... | collective-permute-start | bytes 294920 | tf_op jit(solution)/shard_map/ppermute | solution.py:579
  34.4 6.3 %collective-permute-start.1 = (bf16[6,64,128]{2,1,0:T(8,128)(2,1)S(1)}, bf16[6,64,128]{2,1,0:T(8,128)(2,1)S(1)}, u32[]{:S(2)}, u32[]{:S(2)}) collective-permute-start(bf16[6,64,128]{2,1,0:T(8,128)(2,1)S(1)} %shard_map.131.own_ref), channel_id=1, source_target_pairs={{0,2},{1,3},{2,0},{3,1},{4,6},{5,7},{6,4},{7,5},{8,10},{9,11},{10,... | collective-permute-start | bytes 294920 | tf_op jit(solution)/shard_map/ppermute | solution.py:579
  35.5 5.7 %collective-permute-start = (bf16[6,64,128]{2,1,0:T(8,128)(2,1)S(1)}, bf16[6,64,128]{2,1,0:T(8,128)(2,1)S(1)}, u32[]{:S(2)}, u32[]{:S(2)}) collective-permute-start(bf16[6,64,128]{2,1,0:T(8,128)(2,1)S(1)} %shard_map.131.own_ref), channel_id=1, source_target_pairs={{0,1},{1,2},{2,3},{3,0},{4,5},{5,6},{6,7},{7,4},{8,9},{9,10},{10,1... | collective-permute-start | bytes 294920 | tf_op jit(solution)/shard_map/ppermute | solution.py:579
  65.2 21.9 %copy-start.4 = (bf16[2,64,64]{2,1,0:T(8,128)(2,1)S(1)}, bf16[2,64,64]{2,1,0:T(8,128)(2,1)}, u32[]{:S(2)}) copy-start(bf16[2,64,64]{2,1,0:T(8,128)(2,1)} %constant.11.clone.sel_ref) | copy-start | bytes 49156
  65.3 1.9 %collective-permute-start.5 = (f32[72,128]{1,0:T(8,128)S(1)}, f32[72,128]{1,0:T(8,128)S(1)}, u32[]{:S(2)}, u32[]{:S(2)}) collective-permute-start(f32[72,128]{1,0:T(8,128)S(1)} %shard_map.134.refs_0_), channel_id=1, source_target_pairs={{0,3},{1,0},{2,1},{3,2},{4,7},{5,4},{6,5},{7,6},{8,11},{9,8},{10,9... | collective-permute-start | bytes 110600 | tf_op jit(solution)/shard_map/ppermute | solution.py:579
  65.3 4.4 %collective-permute-start.4 = (f32[72,128]{1,0:T(8,128)S(1)}, f32[72,128]{1,0:T(8,128)S(1)}, u32[]{:S(2)}, u32[]{:S(2)}) collective-permute-start(f32[72,128]{1,0:T(8,128)S(1)} %shard_map.134.refs_0_), channel_id=1, source_target_pairs={{0,2},{1,3},{2,0},{3,1},{4,6},{5,7},{6,4},{7,5},{8,10},{9,11},{10,... | collective-permute-start | bytes 110600 | tf_op jit(solution)/shard_map/ppermute | solution.py:579
  65.9 3.8 %collective-permute-start.3 = (f32[72,128]{1,0:T(8,128)S(1)}, f32[72,128]{1,0:T(8,128)S(1)}, u32[]{:S(2)}, u32[]{:S(2)}) collective-permute-start(f32[72,128]{1,0:T(8,128)S(1)} %shard_map.134.refs_0_), channel_id=1, source_target_pairs={{0,1},{1,2},{2,3},{3,0},{4,5},{5,6},{6,7},{7,4},{8,9},{9,10},{10,1... | collective-permute-start | bytes 110600 | tf_op jit(solution)/shard_map/ppermute | solution.py:579

commit v4 on v3

--- a/solution.py
+++ b/solution.py
@@ -17,7 +17,8 @@
 ENDS = 48
 STRIP = 12 * WINDOW
 SLOT_ONE = 2 * STRIP
-CHUNK = 72
+HALF = 9 * CH
+CHUNK = 40
 TAIL = 48
 SLOT_TWO = CHUNK + TAIL
 VMEM_BYTES = 48 * 1024 * 1024
@@ -32,7 +33,7 @@
 
 
 def call(kernel, outs, scratch, operands, places=(), aliases=None):
-    kinds = {"v": pltpu.VMEM, "s": pltpu.SMEM, "h": pltpu.HBM}
+    kinds = {"v": pltpu.VMEM, "s": pltpu.SMEM, "h": pltpu.HBM, "a": pl.ANY}
     places = dict(places)
     many = isinstance(outs, (list, tuple))
     out_specs = [pl.BlockSpec(memory_space=kinds[places.get(f"o{k}", "v")]) for k in range(len(outs) if many else 1)]
@@ -160,8 +161,10 @@
         out[k * CH : (k + 1) * CH, :] = ref[a, b].T
 
 
-def interior_kernel(in_ref, w1_ref, w2_ref, acc, done, w1t, w2t, f2, g2, wide):
-    band, _ = here()
+def interior_kernel(
+    in_ref, w1_ref, w2_ref, own_ref, away_ref, sent, acc, done, w1t, w2t, f2, g2, wide
+):
+    band, group = here()
     transpose_weights(w1_ref, w1t)
     transpose_weights(w2_ref, w2t)
     for s in range(BANDS):
@@ -215,16 +218,25 @@
         top, low = k * CH, 1152 + k * CH
         acc[top : top + CH, :] = first[b * CH : (b + 1) * CH, a * CH : (a + 1) * CH]
         acc[low : low + CH, :] = second[a * CH : (a + 1) * CH, b * CH : (b + 1) * CH]
+    core = group & 1
+    own_ref[...] = acc[pl.ds(pl.multiple_of(core * HALF, CH), HALF), :]
+    away_ref[...] = acc[pl.ds(pl.multiple_of((1 - core) * HALF, CH), HALF), :].astype(BF)
 
     gthree = jnp.concatenate([gpre[0:384], gpre[192:576], gpre[384:768]], axis=1)
     z = mm(gthree, back_weights(w1t))
     done[...] = up_one(z[:, :CH]) + z[:, CH : 2 * CH] + down_one(z[:, 2 * CH :]) + g2[384:768, :]
+    sent[...] = jnp.zeros_like(sent)
+    for q in range(2):
+        for face in range(3):
+            for row in range(2):
+                piece = done[pl.ds(q * 192 + face * 64 + row, BANDS, stride=2), :]
+                sent[pl.ds((q * 3 + face) * 2 + row, BANDS, stride=16), :] = piece
 
 
 def main_kernel(
-    fn_ref, rot_ref, fill_ref, sel_ref, own_ref, one_ref, two_ref, three_ref, acc, done, w1_ref, w2_ref,
-    out_ref,
-    total, sent, w1t, w2t, xs, hal, nb, cg, lp, lg, lc, ss, gp, gpu, owe,
+    fn_ref, rot_ref, fill_ref, sel_ref, own_ref, one_ref, two_ref, three_ref, w1_ref, w2_ref,
+    share_ref, tail_ref,
+    w1t, w2t, xs, hal, nb, cg, lp, lg, lc, ss, gp, gpu, owe,
 ):
     band, group = here()
     transpose_weights(w1_ref, w1t)
@@ -265,12 +277,15 @@
         mg = (mf * 43) >> 7
         target = mg * 16 + ((m >> 1) & 1) * 3 + (mf - 3 * mg)
         fills.append((one_hot(target, (m & 1) == 0), one_hot(target, (m & 1) == 1)))
-    (lo_zero, lo_end), (hi_zero, hi_end) = fills
+    corner_cells = jnp.concatenate([jnp.concatenate(pair, axis=1) for pair in fills], axis=0)
+    corner_back = corner_cells.astype(F32).T.astype(BF)
     even = (side & 1) == 0
     low_side = jnp.where(side < 2, 2, 0)
     high_side = jnp.where(side < 2, 3, 1)
-    near = [one_hot(home + low_side * 3 + face, even), one_hot(home + low_side * 3 + face, ~even)]
-    far = [one_hot(home + high_side * 3 + face, even), one_hot(home + high_side * 3 + face, ~even)]
+    beside = jnp.concatenate([
+        jnp.concatenate([one_hot(home + other * 3 + face, even), one_hot(home + other * 3 + face, ~even)], axis=1)
+        for other in (low_side, high_side)
+    ], axis=0)
     side_mask = [jnp.broadcast_to((side == s).astype(F32), (64, CH)).astype(BF) for s in range(4)]
     row_line = (side < 2).astype(F32)
     flip_f = jnp.broadcast_to(flip.astype(F32), (64, CH))
@@ -283,12 +298,13 @@
         return jnp.where(flip_f > 0.5, mirrored, plain)
 
     for step, ref in enumerate((own_ref, one_ref, two_ref, three_ref)):
-        start = pl.multiple_of(((group - step) & 3) * 16, 16)
+        start = pl.multiple_of((group ^ step) * 16, 16)
         for j in range(WINDOW):
             for block in range(4):
                 xs[block, j, pl.ds(start, 16), :] = ref[j, block * 16 : block * 16 + 16, :]
+    halos = mm(partner, jnp.concatenate([xs[0, j] for j in range(WINDOW)], axis=1)).astype(BF)
     for j in range(WINDOW):
-        hal[j] = mm(partner, xs[0, j]).astype(BF)
+        hal[j] = halos[:, j * CH : (j + 1) * CH]
 
     def block_at(block, j):
         return hal[j] if block == 0 else xs[block - 1, j]
@@ -311,18 +327,13 @@
         h_one, h_last = second(lambda j: hal[j])
         f_zero, f_end = first(lambda j: xs[0, j])
         none = jnp.zeros((64, CH), BF)
-        low = [
-            (mm(lo_zero, f_zero) + mm(lo_end, f_end)).astype(BF),
-            (mm(near[0], h_zero) + mm(near[1], h_end)).astype(BF),
-            (mm(near[0], h_one) + mm(near[1], h_last)).astype(BF),
-            none, none,
-        ]
-        high = [
-            (mm(hi_zero, f_zero) + mm(hi_end, f_end)).astype(BF),
-            (mm(far[0], h_zero) + mm(far[1], h_end)).astype(BF),
-            (mm(far[0], h_one) + mm(far[1], h_last)).astype(BF),
-            none, none,
-        ]
+        cells = mm(corner_cells, jnp.concatenate([f_zero, f_end], axis=0)).astype(BF)
+        sides = jnp.concatenate([
+            jnp.concatenate([h_zero, h_one], axis=1), jnp.concatenate([h_end, h_last], axis=1)
+        ], axis=0)
+        sides = mm(beside, sides).astype(BF)
+        low = [cells[:64], sides[:64, :CH], sides[:64, CH:], none, none]
+        high = [cells[64:], sides[64:, :CH], sides[64:, CH:], none, none]
         for block in range(5):
             nb[0, block, zero] = pick(low[block], nb[0, block, zero])
             nb[1, block, zero] = pick(nb[1, block, zero], high[block])
@@ -385,23 +396,24 @@
         block = order_back.index((e, j))
         return back[block * 64 : block * 64 + 64]
 
+    seams = jnp.concatenate([back_block(-1, j).astype(BF) for j in range(1, 5)], axis=1)
+    seams = mm(partner, seams)
     for j in range(1, 5):
-        ss[j] = mm(partner, back_block(-1, j).astype(BF))
-
-    def corner_sums(low, high):
-        low = (low * row_line).astype(BF)
-        high = (high * row_line).astype(BF)
-        return mm_t(lo_zero, low) + mm_t(hi_zero, high), mm_t(lo_end, low) + mm_t(hi_end, high)
-
-    corner_low, corner_high = back[256:320], back[320:384]
+        ss[j] = seams[:, (j - 1) * CH : j * CH]
+    both_rows = jnp.concatenate([row_line, row_line], axis=0)
+
+    def corner_sums(both):
+        sums = mm(corner_back, (both * both_rows).astype(BF))
+        return sums[:64], sums[64:]
+
 
     def close_ends(zero, end):
-        at_zero, at_end = corner_sums(corner_low, corner_high)
+        at_zero, at_end = corner_sums(back[256:384])
         head = pick_f(ss[zero], ss[end]) + at_zero
         tail = pick_f(ss[end], ss[zero]) + at_end
-        head_b, tail_b = head.astype(BF), tail.astype(BF)
-        head += mm(near[0], head_b) + mm(near[1], tail_b)
-        tail += mm(far[0], head_b) + mm(far[1], tail_b)
+        sides = mm(beside, jnp.concatenate([head, tail], axis=0).astype(BF))
+        head += sides[:64]
+        tail += sides[64:]
         ss[zero] = pick_f(head, tail)
         ss[end] = pick_f(tail, head)
 
@@ -426,24 +438,33 @@
         gpu[j] = (grad.astype(F32) * unique[j]).astype(BF)
         hid[j] = hidden.astype(BF)
 
-    mine = (home == group * 16).astype(F32)
+    mine = ((line >> 5) == (group >> 1)).astype(F32)
     edge = jnp.where(band == 0, 1.0, 0.0) * mine * row_line
 
     def scaled(value, factor):
         return (value.astype(F32) * factor).astype(BF)
 
     h_zero, h_end = pick(hid[2], hid[1]), pick(hid[1], hid[2])
+    halos = mm(partner, jnp.concatenate([hid[2], hid[3]], axis=1))
+    ends = mm(corner_cells, jnp.concatenate([h_zero, h_end], axis=0))
     cells = jnp.concatenate([
         scaled(hid[2], mine * unique[2]),
         scaled(hid[3], mine * unique[3]),
-        scaled(mm(partner, hid[2]), mine),
-        scaled(mm(partner, hid[3]), mine),
-        scaled(mm(lo_zero, h_zero) + mm(lo_end, h_end), edge),
-        scaled(mm(hi_zero, h_zero) + mm(hi_end, h_end), edge),
+        scaled(halos[:, :CH], mine),
+        scaled(halos[:, CH:], mine),
+        scaled(ends[:64], edge),
+        scaled(ends[64:], edge),
     ], axis=0)
-    second = mm_t(cells, lg[0:384, :])
-    own = jnp.concatenate([scaled(gpu[2], mine), scaled(gpu[3], mine)], axis=0)
-    first = mm_t(lp[0:128, :], own)
+    @pl.when((group & 1) == 0)
+    def _():
+        own = jnp.concatenate([scaled(gpu[2], mine), scaled(gpu[3], mine)], axis=0)
+        share_ref[...] = mm_t(lp[0:128, :], own)
+
+    @pl.when((group & 1) == 1)
+    def _():
+        second = mm_t(cells, lg[0:384, :])
+        for k in range(9):
+            share_ref[k * CH : (k + 1) * CH, :] = second[:, k * CH : (k + 1) * CH]
 
     at_first, at_last = band == 0, band == BANDS - 1
     inner_low = jnp.where(at_first, 0.0, 1.0)
@@ -471,27 +492,27 @@
             fill(lc, block, spread_source(*at, gp if at[0] == -1 else gpu))
     back = mm(lc[...], w1t[...])
     part = [back[k * 64 : k * 64 + 64] for k in range(8)]
-    at_zero, at_end = corner_sums(part[6], part[7])
-    owe[0] = part[0] + mm(partner, part[4].astype(BF)) + pick_f(at_zero, at_end) * (1.0 - inner_low)
+    at_zero, at_end = corner_sums(back[384:512])
+    seams = mm(partner, jnp.concatenate([part[4], part[5]], axis=1).astype(BF))
+    owe[0] = part[0] + seams[:, :CH] + pick_f(at_zero, at_end) * (1.0 - inner_low)
     owe[1] = part[2]
-    owe[2] = part[1] + mm(partner, part[5].astype(BF)) + pick_f(at_end, at_zero) * (1.0 - inner_high)
+    owe[2] = part[1] + seams[:, CH:] + pick_f(at_end, at_zero) * (1.0 - inner_high)
     owe[3] = part[3]
 
     tile = jnp.concatenate([owe[k, pl.ds(pl.multiple_of(group * 16, 16), 16), :] for k in range(4)], axis=0)
-    tails = mm(sel_ref[...], tile.astype(BF))
-    total[0:1152, :] = acc[0:1152, :] + first
-    for k in range(9):
-        low = 1152 + k * CH
-        total[low : low + CH, :] = acc[low : low + CH, :] + second[:, k * CH : (k + 1) * CH]
-    sent[...] = jnp.zeros_like(sent)
-    for q in range(2):
-        for face in range(3):
-            for row in range(2):
-                piece = done[pl.ds(q * 192 + face * 64 + row, BANDS, stride=2), :]
-                sent[pl.ds((q * 3 + face) * 2 + row, BANDS, stride=16), :] = piece
+    tail_ref[...] = mm(sel_ref[...], tile.astype(BF))
+
+
+def after_kernel(*refs):
+    pass
+
+
+def share_kernel(own_ref, other_ref, line_ref, tail_ref, sent, out_ref, total):
+    total[0:HALF, :] = own_ref[...] + other_ref[...].astype(F32) + line_ref[...]
+    total[HALF : BANDS * CHUNK, :] = jnp.zeros((BANDS * CHUNK - HALF, CH), F32)
     for i in range(BANDS):
         half = i // 16
-        tail = tails[half * 40 : half * 40 + 40]
+        tail = tail_ref[half * 40 : half * 40 + 40, :]
         pixels = jnp.concatenate([sent[i * 16 : i * 16 + 16, :], jnp.zeros((32, CH), F32)], axis=0)
         shifted = jnp.concatenate([jnp.zeros((8, CH), F32), tail], axis=0)
         out_ref[i] = jnp.concatenate([total[CHUNK * i : CHUNK * i + CHUNK, :], pixels + shifted], axis=0).astype(BF)
@@ -520,26 +541,30 @@
     return select
 
 
-def reduce_kernel(in_ref, sum_ref):
-    total = in_ref[0].astype(F32)
+def reduce_kernel(in_ref, out_ref):
+    total = in_ref[0, 0:48, :].astype(F32)
     for i in range(1, BANDS):
-        total = total + in_ref[i].astype(F32)
-    sum_ref[...] = total[0:CHUNK]
-
-
-def spread_kernel(factor, own_ref, one_ref, two_ref, three_ref, out_ref, parts):
-    _, group = here()
-    for step, ref in enumerate((own_ref, one_ref, two_ref, three_ref)):
-        parts[(group - step) & 3] = ref[...]
-    total = (parts[0] + parts[1]) + (parts[2] + parts[3])
-    total = (total * factor).astype(BF)
+        total = total + in_ref[i, 0:48, :].astype(F32)
+    out_ref[...] = total[0:CHUNK]
+
+
+def spread_kernel(factor, own_ref, other_ref, out_ref):
+    total = ((own_ref[...] + other_ref[...]) * factor).astype(BF)
     for i in range(BANDS):
         out_ref[i] = total
 
 
-def final_kernel(fn_ref, rot_ref, sel_ref, in_ref, sum_ref, out_ref, first_ref, second_ref, wide, total):
-    first_ref[...] = sum_ref[0:16].astype(F32).reshape(1152, CH)
-    second_ref[...] = sum_ref[16:32].astype(F32).reshape(1152, CH)
+def unpack_kernel(own_ref, other_ref, first_ref, second_ref):
+    _, group = here()
+    core = group & 1
+    for i in range(29):
+        own, other = own_ref[i].astype(F32), other_ref[i].astype(F32)
+        rows = min(CHUNK, HALF - CHUNK * i)
+        first_ref[CHUNK * i : CHUNK * i + rows, :] = jnp.where(core == 0, own, other)[0:rows]
+        second_ref[CHUNK * i : CHUNK * i + rows, :] = jnp.where(core == 0, other, own)[0:rows]
+
+
+def grad_kernel(fn_ref, rot_ref, sel_ref, in_ref, out_ref, wide, total):
     band, group = here()
     for i in range(BANDS):
         wide[i * TAIL : (i + 1) * TAIL, :] = in_ref[i].astype(F32)[CHUNK:SLOT_TWO]
@@ -575,9 +600,8 @@
             out_ref[face, row] = total[row, face].astype(BF)
 
 
-def around(value):
-    moved = [lax.ppermute(value, "sub", [(i, (i + step) % 4) for i in range(4)]) for step in (1, 2, 3)]
-    return (value, *moved)
+def swapped(value, step):
+    return lax.ppermute(value, "sub", [(i, i ^ step) for i in range(4)])
 
 
 def body(field_in, grad_out, first_weight, second_weight, face_neighbour, seam_rotation, corner_fill):
@@ -605,11 +629,14 @@
         (*seams, jnp.asarray(line_selector(), BF), jnp.asarray(ends_selector(), BF), strips),
         in_smem,
     )
-    lines = around(lines)
-    acc, done = call(
+    lines = (lines, *[swapped(lines, step) for step in (1, 2, 3)])
+    share = jax.ShapeDtypeStruct((HALF, CH), F32)
+    own, away, sent = call(
         interior_kernel,
-        [jax.ShapeDtypeStruct((2304, CH), F32), jax.ShapeDtypeStruct((384, CH), F32)],
+        [share, jax.ShapeDtypeStruct((HALF, CH), BF), jax.ShapeDtypeStruct((BANDS * 16, CH), F32)],
         [
+            pltpu.VMEM((2304, CH), F32),
+            pltpu.VMEM((384, CH), F32),
             pltpu.VMEM((1152, CH), BF),
             pltpu.VMEM((1152, CH), BF),
             pltpu.VMEM((1152, CH), F32),
@@ -618,13 +645,13 @@
         ],
         (strips, first_weight, second_weight),
     )
-
-    slots = call(
+    away = call(after_kernel, jax.ShapeDtypeStruct((HALF, CH), BF), [], (away, *lines[1:]), dict.fromkeys((0, 1, 2, 3, "o0"), "a"), {0: 0})
+    other = swapped(away, 1)
+
+    line, tails = call(
         main_kernel,
-        jax.ShapeDtypeStruct((BANDS, SLOT_TWO, CH), BF),
+        [share, jax.ShapeDtypeStruct((80, CH), F32)],
         [
-            pltpu.VMEM((2304, CH), F32),
-            pltpu.VMEM((BANDS * 16, CH), F32),
             pltpu.VMEM((1152, CH), BF),
             pltpu.VMEM((1152, CH), BF),
             pltpu.VMEM((4, WINDOW, 64, CH), BF),
@@ -639,31 +666,36 @@
             pltpu.VMEM((5, 64, CH), BF),
             pltpu.VMEM((4, 64, CH), F32),
         ],
-        (*seams, corner_fill.T, jnp.asarray(tail_selector(), BF), *lines, acc, done, first_weight, second_weight),
+        (*seams, corner_fill.T, jnp.asarray(tail_selector(), BF), *lines, first_weight, second_weight),
+    )
+    slots = call(
+        share_kernel,
+        jax.ShapeDtypeStruct((BANDS, SLOT_TWO, CH), BF),
+        [pltpu.VMEM((BANDS * CHUNK, CH), F32)],
+        (own, other, line, tails, sent),
     )
     slots = lax.all_to_all(slots, "tile", 0, 0, tiled=True)
     part = call(reduce_kernel, jax.ShapeDtypeStruct((CHUNK, CH), F32), [], (slots,))
-    part = around(part)
     reduced = call(
         lambda *refs: spread_kernel(factor, *refs),
         jax.ShapeDtypeStruct((BANDS, CHUNK, CH), BF),
-        [pltpu.VMEM((4, CHUNK, CH), F32)],
-        part,
+        [],
+        (part, swapped(part, 2)),
     )
     reduced = lax.all_to_all(reduced, "tile", 0, 0, tiled=True)
-    grad_in, first, second = call(
-        final_kernel,
-        [
-            jax.ShapeDtypeStruct((3, 2, SPAN, CH), BF),
-            jax.ShapeDtypeStruct((1152, CH), F32),
-            jax.ShapeDtypeStruct((1152, CH), F32),
-        ],
-        [
-            pltpu.VMEM((BANDS * TAIL, CH), F32),
-            pltpu.VMEM((2, 3, SPAN, CH), F32),
-        ],
-        (*seams, jnp.asarray(order_selector(), BF), slots, reduced),
+    swap = swapped(reduced, 1)
+    grad_in = call(
+        grad_kernel,
+        jax.ShapeDtypeStruct((3, 2, SPAN, CH), BF),
+        [pltpu.VMEM((BANDS * TAIL, CH), F32), pltpu.VMEM((2, 3, SPAN, CH), F32)],
+        (*seams, jnp.asarray(order_selector(), BF), slots),
         in_smem,
+    )
+    first, second = call(
+        unpack_kernel,
+        [jax.ShapeDtypeStruct((1152, CH), F32), jax.ShapeDtypeStruct((1152, CH), F32)],
+        [],
+        (reduced, swap),
     )
     return grad_in, first.reshape(3, 3, CH, CH), second.reshape(3, 3, CH, CH)
 

time: 89.4 us -> 87.9 us (0.983)
  the two profiles are of different devices: /device:TPU:0 before, /device:TPU:1 now
where the time goes in v4:
time: 87.9 us; the launch traced here: 87.7 us
  blocking collectives  62.9 us (72%)
  Pallas kernels  11 us (13%)
  starting transfers between devices  7.78 us (9%)
  waiting for transfers between devices  5.14 us (6%)
    all_to_all x1, blocking collectives, body(): strips = lax.all_to_all(slots, 'tile', 0, 0, tiled=True)  30.5 us
    all_to_all x1, blocking collectives, body(): slots = lax.all_to_all(slots, 'tile', 0, 0, tiled=True)  17.5 us
    all_to_all x1, blocking collectives, body(): reduced = lax.all_to_all(reduced, 'tile', 0, 0, tiled=True)  14.8 us
    pallas_call x10, Pallas kernels, call(): pl.pallas_call(kernel, out_shape=outs, in_specs=[pl.BlockSpec(memory_spac...  11 us
    ppermute x6, starting transfers between devices, swapped(): return lax.ppermute(value, 'sub', [(i, i ^ step) for i in range(4)])  7.78 us
    ppermute x6, waiting for transfers between devices, swapped(): return lax.ppermute(value, 'sub', [(i, i ^ step) for i in range(4)])  5.14 us
  transfers between devices with their start and end apart: 6, of which 3 were waited for; matrix products, arithmetic and copies ran while one was open for 0% of the time, Pallas kernels for 9%

profile of v4, /device:TPU:1, one launch (start us, length us, event | category | flops | bytes accessed | tf_op | source)
XLA Modules:
  0.0 87.7 jit_solution(17240429746433086492)
XLA Ops:
  0.6 1.1 %shard_map.130 = bf16[32,144,128]{2,1,0:T(8,128)(2,1)S(1)} custom-call(bf16[3,2,64,128]{3,2,1,0:T(8,128)(2,1)} %f_hbm.1, bf16[3,2,64,128]{3,2,1,0:T(8,128)(2,1)} %g_hbm.1), custom_call_target="tpu_custom_call" | custom-call | tf_op jit(solution)/shard_map/pallas_call | solution.py:40
  1.7 0.0 copy-start.2
  1.7 0.0 copy-start.3
  1.8 0.0 copy-start.6
  1.8 0.0 copy-start.7
  1.8 30.5 %all_to_all.15.in_ref = bf16[32,144,128]{2,1,0:T(8,128)(2,1)S(1)} all-to-all(bf16[32,144,128]{2,1,0:T(8,128)(2,1)S(1)} %shard_map.130), channel_id=1, replica_groups=mesh['tile'=32,'sub'=4] {'tile'}, dimensions={0} | all-to-all | bytes 2359296 | tf_op jit(solution)/shard_map/all_to_all | solution.py:624
  32.3 0.0 copy-done.2
  32.3 0.0 copy-done.3
  32.3 0.0 copy-done.6
  32.3 0.0 copy-done.7
  32.3 0.0 copy-start
  32.3 0.0 copy-start.1
  32.4 1.0 %shard_map.132.own_ref = bf16[6,64,128]{2,1,0:T(8,128)(2,1)S(1)} custom-call(s32[4,12]{1,0:T(4,128)S(1)} %bitcast.5, s32[4,12]{1,0:T(4,128)S(1)} %bitcast.8, bf16[2,384,576]{2,1,0:T(8,128)(2,1)S(1)} %copy-done.2, bf16[4,48,144]{2,1,0:T(8,128)(2,1)S(1)} %copy-done.3, bf16[32,144,128]{2,1,0:T(8,128)(2,1)S(1)} %all_to_all.15.in_ref), custom_call_target="tpu_custom_call" | custom-call | tf_op jit(solution)/shard_map/pallas_call | solution.py:40
  33.4 0.0 copy-start.5
  33.4 0.0 copy-start.8
  33.4 3.1 %collective-permute-start.2 = (bf16[6,64,128]{2,1,0:T(8,128)(2,1)S(1)}, bf16[6,64,128]{2,1,0:T(8,128)(2,1)S(1)}, u32[]{:S(2)}, u32[]{:S(2)}) collective-permute-start(bf16[6,64,128]{2,1,0:T(8,128)(2,1)S(1)} %shard_map.132.own_ref), channel_id=1, source_target_pairs={{0,3},{1,2},{2,1},{3,0},{4,7},{5,6},{6,5},{7,4},{8,11},{9,10},{10,... | collective-permute-start | bytes 294920 | tf_op jit(solution)/shard_map/ppermute | solution.py:604
  36.5 0.7 collective-permute-start.1
  37.2 0.0 collective-permute-start
  37.2 0.0 copy-done
  37.2 0.0 copy-done.1
  37.2 2.0 %shard_map.131 = (f32[1152,128]{1,0:T(8,128)S(1)}, bf16[1152,128]{1,0:T(8,128)(2,1)S(1)}, f32[512,128]{1,0:T(8,128)S(1)}) custom-call(bf16[32,144,128]{2,1,0:T(8,128)(2,1)S(1)} %all_to_all.15.in_ref, bf16[3,3,128,128]{3,2,1,0:T(8,128)(2,1)S(1)} %copy-done, bf16[3,3,128,128]{3,2,1,0:T(8,128)(2,1)S(1)} %copy-done.1), custom_call_target="tpu_custom_call" | custom-call | tf_op jit(solution)/shard_map/pallas_call | solution.py:40
  39.3 0.5 collective-permute-done.2.refs_3_.three_ref
  39.8 2.2 %collective-permute-done.1.refs_2_.two_ref = bf16[6,64,128]{2,1,0:T(8,128)(2,1)S(1)} collective-permute-done((bf16[6,64,128]{2,1,0:T(8,128)(2,1)S(1)}, bf16[6,64,128]{2,1,0:T(8,128)(2,1)S(1)}, u32[]{:S(2)}, u32[]{:S(2)}) %collective-permute-start.1) | collective-permute-done | bytes 98336 | tf_op jit(solution)/shard_map/ppermute | solution.py:604
  41.9 0.0 collective-permute-done.refs_1_.one_ref
  42.0 0.3 collective-permute-start.3
  42.3 0.0 copy-done.5
  42.3 0.0 copy-done.8
  42.3 4.0 %shard_map.134 = (f32[1152,128]{1,0:T(8,128)S(1)}, f32[80,128]{1,0:T(8,128)S(1)}) custom-call(s32[4,12]{1,0:T(4,128)S(1)} %bitcast.6, s32[4,12]{1,0:T(4,128)S(1)} %bitcast.9, s32[4,12]{1,0:T(4,128)S(1)} %bitcast.11, bf16[80,64]{1,0:T(8,128)(2,1)S(1)} %copy-done.5, bf16[6,64,128]{2,1,0:T(8,128)(2,1)S(1)} %shard_map.132.own_ref, ...), custom_call_target="tpu_custom_call" | custom-call | tf_op jit(solution)/shard_map/pallas_call | solution.py:40
  46.3 0.0 collective-permute-done.3.other_ref
  46.3 0.1 shard_map.135
  46.4 17.5 %all_to_all.16.in_ref = bf16[32,88,128]{2,1,0:T(8,128)(2,1)S(1)} all-to-all(bf16[32,88,128]{2,1,0:T(8,128)(2,1)S(1)} %shard_map.135), channel_id=1, replica_groups=mesh['tile'=32,'sub'=4] {'tile'}, dimensions={0} | all-to-all | bytes 1441792 | tf_op jit(solution)/shard_map/all_to_all | solution.py:677
  64.0 0.0 copy-start.4
  64.0 0.1 shard_map.137.refs_0_
  64.0 0.3 collective-permute-start.4
  64.3 2.5 %collective-permute-done.4.refs_1_ = f32[40,128]{1,0:T(8,128)S(1)} collective-permute-done((f32[40,128]{1,0:T(8,128)S(1)}, f32[40,128]{1,0:T(8,128)S(1)}, u32[]{:S(2)}, u32[]{:S(2)}) %collective-permute-start.4) | collective-permute-done | bytes 20512 | tf_op jit(solution)/shard_map/ppermute | solution.py:604
  66.8 14.8 %all_to_all.17.own_ref = bf16[32,40,128]{2,1,0:T(8,128)(2,1)S(1)} all-to-all(bf16[32,40,128]{2,1,0:T(8,128)(2,1)S(1)} %shard_map.138), channel_id=1, replica_groups=mesh['tile'=32,'sub'=4] {'tile'}, dimensions={0} | all-to-all | bytes 655360 | tf_op jit(solution)/shard_map/all_to_all | solution.py:685
  81.6 3.4 %collective-permute-start.5 = (bf16[32,40,128]{2,1,0:T(8,128)(2,1)S(1)}, bf16[32,40,128]{2,1,0:T(8,128)(2,1)S(1)}, u32[]{:S(2)}, u32[]{:S(2)}) collective-permute-start(bf16[32,40,128]{2,1,0:T(8,128)(2,1)S(1)} %all_to_all.17.own_ref), channel_id=1, source_target_pairs={{0,1},{1,0},{2,3},{3,2},{4,5},{5,4},{6,7},{7,6},{8,9},{9,8},{10,11... | collective-permute-start | bytes 983048 | tf_op jit(solution)/shard_map/ppermute | solution.py:604
  85.0 0.0 copy-done.4
  85.0 1.6 %shard_map.136 = bf16[3,2,64,128]{3,2,1,0:T(8,128)(2,1)} custom-call(s32[4,12]{1,0:T(4,128)S(1)} %bitcast.7, s32[4,12]{1,0:T(4,128)S(1)} %bitcast.10, bf16[2,64,64]{2,1,0:T(8,128)(2,1)S(1)} %copy-done.4, bf16[32,88,128]{2,1,0:T(8,128)(2,1)S(1)} %all_to_all.16.in_ref), custom_call_target="tpu_custom_call" | custom-call | tf_op jit(solution)/shard_map/pallas_call | solution.py:40
  86.6 0.0 collective-permute-done.5.other_ref
  86.6 1.1 %shard_map.139 = (f32[1152,128]{1,0:T(8,128)}, f32[1152,128]{1,0:T(8,128)}) custom-call(bf16[32,40,128]{2,1,0:T(8,128)(2,1)S(1)} %all_to_all.17.own_ref, bf16[32,40,128]{2,1,0:T(8,128)(2,1)S(1)} %collective-permute-done.5.other_ref), custom_call_target="tpu_custom_call" | custom-call | tf_op jit(solution)/shard_map/pallas_call | solution.py:40
  (2 shorter events, 0.0 us)
Async XLA Ops:
  1.7 30.6 %copy-start.2 = (bf16[2,384,576]{2,1,0:T(8,128)(2,1)S(1)}, bf16[2,384,576]{2,1,0:T(8,128)(2,1)}, u32[]{:S(2)}) copy-start(bf16[2,384,576]{2,1,0:T(8,128)(2,1)} %constant.8.clone.sel_ref) | copy-start | bytes 2654212
  1.7 30.6 %copy-start.3 = (bf16[4,48,144]{2,1,0:T(8,128)(2,1)S(1)}, bf16[4,48,144]{2,1,0:T(8,128)(2,1)}, u32[]{:S(2)}) copy-start(bf16[4,48,144]{2,1,0:T(8,128)(2,1)} %constant.9.clone.ends_ref) | copy-start | bytes 165892
  1.8 30.6 %copy-start.6 = (s32[12,4]{0,1:T(4,128)S(1)}, s32[12,4]{0,1:T(4,128)}, u32[]{:S(2)}) copy-start(s32[12,4]{0,1:T(4,128)} %param.15) | copy-start | bytes 580
  1.8 30.6 %copy-start.7 = (s32[12,4]{0,1:T(4,128)S(1)}, s32[12,4]{0,1:T(4,128)}, u32[]{:S(2)}) copy-start(s32[12,4]{0,1:T(4,128)} %param.16) | copy-start | bytes 580
  32.3 4.9 %copy-start = (bf16[3,3,128,128]{3,2,1,0:T(8,128)(2,1)S(1)}, bf16[3,3,128,128]{3,2,1,0:T(8,128)(2,1)}, u32[]{:S(2)}) copy-start(bf16[3,3,128,128]{3,2,1,0:T(8,128)(2,1)} %w1_ref.3) | copy-start | bytes 884740
  32.3 4.9 %copy-start.1 = (bf16[3,3,128,128]{3,2,1,0:T(8,128)(2,1)S(1)}, bf16[3,3,128,128]{3,2,1,0:T(8,128)(2,1)}, u32[]{:S(2)}) copy-start(bf16[3,3,128,128]{3,2,1,0:T(8,128)(2,1)} %w2_ref.3) | copy-start | bytes 884740
  33.4 8.9 %copy-start.5 = (bf16[80,64]{1,0:T(8,128)(2,1)S(1)}, bf16[80,64]{1,0:T(8,128)(2,1)}, u32[]{:S(2)}) copy-start(bf16[80,64]{1,0:T(8,128)(2,1)} %constant.10.clone.sel_ref) | copy-start | bytes 30724
  33.4 8.9 %copy-start.8 = (s32[12,4]{0,1:T(4,128)S(1)}, s32[12,4]{0,1:T(4,128)}, u32[]{:S(2)}) copy-start(s32[12,4]{0,1:T(4,128)} %param.17) | copy-start | bytes 580
  33.4 6.4 %collective-permute-start.2 = (bf16[6,64,128]{2,1,0:T(8,128)(2,1)S(1)}, bf16[6,64,128]{2,1,0:T(8,128)(2,1)S(1)}, u32[]{:S(2)}, u32[]{:S(2)}) collective-permute-start(bf16[6,64,128]{2,1,0:T(8,128)(2,1)S(1)} %shard_map.132.own_ref), channel_id=1, source_target_pairs={{0,3},{1,2},{2,1},{3,0},{4,7},{5,6},{6,5},{7,4},{8,11},{9,10},{10,... | collective-permute-start | bytes 294920 | tf_op jit(solution)/shard_map/ppermute | solution.py:604
  36.5 5.5 %collective-permute-start.1 = (bf16[6,64,128]{2,1,0:T(8,128)(2,1)S(1)}, bf16[6,64,128]{2,1,0:T(8,128)(2,1)S(1)}, u32[]{:S(2)}, u32[]{:S(2)}) collective-permute-start(bf16[6,64,128]{2,1,0:T(8,128)(2,1)S(1)} %shard_map.132.own_ref), channel_id=1, source_target_pairs={{0,2},{1,3},{2,0},{3,1},{4,6},{5,7},{6,4},{7,5},{8,10},{9,11},{10,... | collective-permute-start | bytes 294920 | tf_op jit(solution)/shard_map/ppermute | solution.py:604
  37.2 4.7 %collective-permute-start = (bf16[6,64,128]{2,1,0:T(8,128)(2,1)S(1)}, bf16[6,64,128]{2,1,0:T(8,128)(2,1)S(1)}, u32[]{:S(2)}, u32[]{:S(2)}) collective-permute-start(bf16[6,64,128]{2,1,0:T(8,128)(2,1)S(1)} %shard_map.132.own_ref), channel_id=1, source_target_pairs={{0,1},{1,0},{2,3},{3,2},{4,5},{5,4},{6,7},{7,6},{8,9},{9,8},{10,11... | collective-permute-start | bytes 294920 | tf_op jit(solution)/shard_map/ppermute | solution.py:604
  42.0 4.3 %collective-permute-start.3 = (bf16[1152,128]{1,0:T(8,128)(2,1)S(1)}, bf16[1152,128]{1,0:T(8,128)(2,1)S(1)}, u32[]{:S(2)}, u32[]{:S(2)}) collective-permute-start(bf16[1152,128]{1,0:T(8,128)(2,1)S(1)} %shard_map.133), channel_id=1, source_target_pairs={{0,1},{1,0},{2,3},{3,2},{4,5},{5,4},{6,7},{7,6},{8,9},{9,8},{10,11... | collective-permute-start | bytes 884744 | tf_op jit(solution)/shard_map/ppermute | solution.py:604
  64.0 21.0 %copy-start.4 = (bf16[2,64,64]{2,1,0:T(8,128)(2,1)S(1)}, bf16[2,64,64]{2,1,0:T(8,128)(2,1)}, u32[]{:S(2)}) copy-start(bf16[2,64,64]{2,1,0:T(8,128)(2,1)} %constant.11.clone.sel_ref) | copy-start | bytes 49156
  64.0 2.7 %collective-permute-start.4 = (f32[40,128]{1,0:T(8,128)S(1)}, f32[40,128]{1,0:T(8,128)S(1)}, u32[]{:S(2)}, u32[]{:S(2)}) collective-permute-start(f32[40,128]{1,0:T(8,128)S(1)} %shard_map.137.refs_0_), channel_id=1, source_target_pairs={{0,2},{1,3},{2,0},{3,1},{4,6},{5,7},{6,4},{7,5},{8,10},{9,11},{10,... | collective-permute-start | bytes 61448 | tf_op jit(solution)/shard_map/ppermute | solution.py:604
  81.6 5.0 %collective-permute-start.5 = (bf16[32,40,128]{2,1,0:T(8,128)(2,1)S(1)}, bf16[32,40,128]{2,1,0:T(8,128)(2,1)S(1)}, u32[]{:S(2)}, u32[]{:S(2)}) collective-permute-start(bf16[32,40,128]{2,1,0:T(8,128)(2,1)S(1)} %all_to_all.17.own_ref), channel_id=1, source_target_pairs={{0,1},{1,0},{2,3},{3,2},{4,5},{5,4},{6,7},{7,6},{8,9},{9,8},{10,11... | collective-permute-start | bytes 983048 | tf_op jit(solution)/shard_map/ppermute | solution.py:604

commit v5 on v4

--- a/solution.py
+++ b/solution.py
@@ -18,9 +18,10 @@
 STRIP = 12 * WINDOW
 SLOT_ONE = 2 * STRIP
 HALF = 9 * CH
-CHUNK = 40
-TAIL = 48
+CHUNK = 36
+TAIL = 36
 SLOT_TWO = CHUNK + TAIL
+SLOT_THREE = 40
 VMEM_BYTES = 48 * 1024 * 1024
 
 
@@ -61,6 +62,13 @@
 def is_mirrored(fn_ref, rot_ref, face, side):
     rot = rot_ref[side, face]
     partner = 4 * fn_ref[side, face] + (rot & 3)
+    return jnp.where(4 * face + side > partner, rot >> 2, 0)
+
+
+def mirrored_in(fn_ref, rot_ref, face, side):
+    lane = lax.broadcasted_iota(I32, (1, 12), 1) == face
+    rot = jnp.sum(jnp.where(lane, rot_ref[side : side + 1, :], 0))
+    partner = 4 * jnp.sum(jnp.where(lane, fn_ref[side : side + 1, :], 0)) + (rot & 3)
     return jnp.where(4 * face + side > partner, rot >> 2, 0)
 
 
@@ -234,7 +242,7 @@
 
 
 def main_kernel(
-    fn_ref, rot_ref, fill_ref, sel_ref, own_ref, one_ref, two_ref, three_ref, w1_ref, w2_ref,
+    fn_ref, rot_ref, fill_ref, plan_ref, sel_ref, own_ref, one_ref, two_ref, three_ref, w1_ref, w2_ref,
     share_ref, tail_ref,
     w1t, w2t, xs, hal, nb, cg, lp, lg, lc, ss, gp, gpu, owe,
 ):
@@ -286,13 +294,13 @@
         jnp.concatenate([one_hot(home + other * 3 + face, even), one_hot(home + other * 3 + face, ~even)], axis=1)
         for other in (low_side, high_side)
     ], axis=0)
-    side_mask = [jnp.broadcast_to((side == s).astype(F32), (64, CH)).astype(BF) for s in range(4)]
+    side_mask = [jnp.broadcast_to((side == s).astype(F32), (64, CH)).astype(BF) > 0.5 for s in range(4)]
     row_line = (side < 2).astype(F32)
     flip_f = jnp.broadcast_to(flip.astype(F32), (64, CH))
-    flip_b, keep_b = flip_f.astype(BF), (1.0 - flip_f).astype(BF)
+    flip_b = flip_f.astype(BF) > 0.5
 
     def pick(plain, mirrored):
-        return plain * keep_b + mirrored * flip_b
+        return jnp.where(flip_b, mirrored, plain)
 
     def pick_f(plain, mirrored):
         return jnp.where(flip_f > 0.5, mirrored, plain)
@@ -350,13 +358,12 @@
         fill_ends(4, 3)
 
     def choose(options):
-        result = None
+        whole = all(option is not None for option in options)
+        result = options[0] if whole else jnp.zeros((64, CH), BF)
         for s, option in enumerate(options):
-            if option is None:
-                continue
-            term = option * side_mask[s]
-            result = term if result is None else result + term
-        return jnp.zeros((64, CH), BF) if result is None else result
+            if option is not None and not (whole and s == 0):
+                result = jnp.where(side_mask[s], option, result)
+        return result
 
     def fill(target, block, source):
         for k, tap in enumerate(TAPS):
@@ -500,7 +507,45 @@
     owe[3] = part[3]
 
     tile = jnp.concatenate([owe[k, pl.ds(pl.multiple_of(group * 16, 16), 16), :] for k in range(4)], axis=0)
-    tail_ref[...] = mm(sel_ref[...], tile.astype(BF))
+    plan = [plan_ref[:, k : k + 1] for k in range(8)]
+    flips = [jnp.zeros((48, 1), I32) for _ in range(2)]
+    for which in range(4):
+        for face_index in range(3):
+            value = mirrored_in(fn_ref, rot_ref, 3 * group + face_index, which)
+            for k in range(2):
+                flips[k] = jnp.where(plan[6 + k] == which * 3 + face_index, value, flips[k])
+    last = jnp.where(at_last, 1, 0)
+    outer = jnp.logical_or(at_first, at_last)
+    row_lane = jnp.where(flips[0] ^ last == plan[4], jnp.where(at_last, plan[1], plan[0]), -1)
+    col_lane = jnp.where(flips[1] ^ last == plan[5], jnp.where(at_last, plan[3], plan[2]), -1)
+    lanes = lax.broadcasted_iota(I32, (48, 64), 1)
+    patch = (row_lane == lanes).astype(F32) + (col_lane == lanes).astype(F32)
+    select = jnp.concatenate([jnp.where(outer, patch, sel_ref[0:48, :]), sel_ref[48:72, :]], axis=0)
+    tail_ref[...] = mm(select.astype(BF), tile.astype(BF))
+
+
+def tail_plan():
+    select = np.zeros((72, 64), np.float32)
+    plan = np.zeros((48, 8), np.int32)
+    for pos in range(2):
+        for depth in range(2):
+            for face in range(3):
+                lane = (pos * 2 + depth) * 16 + face
+                for half in range(2):
+                    select[half * 24 + (pos * 2 + depth) * 3 + face, lane + half * 3] = 1
+                for side in range(2):
+                    select[48 + ((pos * 2 + side) * 2 + depth) * 3 + face, lane + 6 + 3 * side] = 1
+    for half in range(2):
+        for side in range(2):
+            for face in range(3):
+                for row in range(2):
+                    for col in range(2):
+                        place = half * 24 + ((side * 3 + face) * 2 + row) * 2 + col
+                        for last in range(2):
+                            plan[place, last] = ((col ^ last) * 2 + row) * 16 + half * 3 + face
+                            plan[place, 2 + last] = ((row ^ last) * 2 + col) * 16 + (2 + side) * 3 + face
+                        plan[place, 4:] = side, half, half * 3 + face, (2 + side) * 3 + face
+    return select, plan
 
 
 def after_kernel(*refs):
@@ -508,28 +553,11 @@
 
 
 def share_kernel(own_ref, other_ref, line_ref, tail_ref, sent, out_ref, total):
-    total[0:HALF, :] = own_ref[...] + other_ref[...].astype(F32) + line_ref[...]
-    total[HALF : BANDS * CHUNK, :] = jnp.zeros((BANDS * CHUNK - HALF, CH), F32)
+    total[...] = own_ref[...] + other_ref[...].astype(F32) + line_ref[...]
     for i in range(BANDS):
-        half = i // 16
-        tail = tail_ref[half * 40 : half * 40 + 40, :]
-        pixels = jnp.concatenate([sent[i * 16 : i * 16 + 16, :], jnp.zeros((32, CH), F32)], axis=0)
-        shifted = jnp.concatenate([jnp.zeros((8, CH), F32), tail], axis=0)
-        out_ref[i] = jnp.concatenate([total[CHUNK * i : CHUNK * i + CHUNK, :], pixels + shifted], axis=0).astype(BF)
-
-
-def tail_selector():
-    select = np.zeros((80, 64), np.float32)
-    for half in range(2):
-        for pos in range(2):
-            for depth in range(2):
-                for face in range(3):
-                    lane = (pos * 2 + depth) * 16 + face
-                    select[half * 40 + 4 + (pos * 2 + depth) * 3 + face, lane + half * 3] = 1
-                    for side in range(2):
-                        row = 16 + ((pos * 2 + side) * 2 + depth) * 3 + face
-                        select[half * 40 + row, lane + 6 + 3 * side] = 1
-    return select
+        start = 0 if i == 0 else 24 if i == BANDS - 1 else 48
+        parts = [total[CHUNK * i : CHUNK * i + CHUNK, :], sent[i * 16 : i * 16 + 12, :], tail_ref[start : start + 24, :]]
+        out_ref[i] = jnp.concatenate(parts, axis=0).astype(BF)
 
 
 def order_selector():
@@ -545,7 +573,7 @@
     total = in_ref[0, 0:48, :].astype(F32)
     for i in range(1, BANDS):
         total = total + in_ref[i, 0:48, :].astype(F32)
-    out_ref[...] = total[0:CHUNK]
+    out_ref[...] = total[0:SLOT_THREE]
 
 
 def spread_kernel(factor, own_ref, other_ref, out_ref):
@@ -557,43 +585,54 @@
 def unpack_kernel(own_ref, other_ref, first_ref, second_ref):
     _, group = here()
     core = group & 1
-    for i in range(29):
+    for i in range(BANDS):
         own, other = own_ref[i].astype(F32), other_ref[i].astype(F32)
-        rows = min(CHUNK, HALF - CHUNK * i)
-        first_ref[CHUNK * i : CHUNK * i + rows, :] = jnp.where(core == 0, own, other)[0:rows]
-        second_ref[CHUNK * i : CHUNK * i + rows, :] = jnp.where(core == 0, other, own)[0:rows]
+        rows = slice(CHUNK * i, CHUNK * i + CHUNK)
+        first_ref[rows, :] = jnp.where(core == 0, own, other)[0:CHUNK]
+        second_ref[rows, :] = jnp.where(core == 0, other, own)[0:CHUNK]
 
 
 def grad_kernel(fn_ref, rot_ref, sel_ref, in_ref, out_ref, wide, total):
     band, group = here()
     for i in range(BANDS):
-        wide[i * TAIL : (i + 1) * TAIL, :] = in_ref[i].astype(F32)[CHUNK:SLOT_TWO]
+        wide[i * 40 : i * 40 + 40, :] = in_ref[i].astype(F32)[32:SLOT_TWO]
     for q in range(2):
         for face in range(3):
             for row in range(2):
-                piece = wide[pl.ds((q * 3 + face) * 2 + row, BANDS, stride=TAIL), :]
+                piece = wide[pl.ds(4 + (q * 3 + face) * 2 + row, BANDS, stride=40), :]
                 total[row, face, pl.ds(q, BANDS, stride=2), :] = piece
-    tiles = [wide[pl.ds(pl.multiple_of(src * TAIL, TAIL), TAIL), :] for src in (band, BANDS - 1 - band)]
-    for side in range(2):
+    tiles = [wide[pl.ds(pl.multiple_of(src * 40, 8), 40), :] for src in (band, BANDS - 1 - band)]
+    outer = (band == 0) | (band == BANDS - 1)
+
+    @pl.when(~outer)
+    def _():
+        for side in range(2):
+            for face in range(3):
+                flip = is_mirrored(fn_ref, rot_ref, 3 * group + face, 2 + side) == 1
+                for row in range(2):
+                    for depth in range(2):
+                        column = depth if side == 0 else 63 - depth
+                        k, m = [16 + ((pos * 2 + side) * 2 + depth) * 3 + face for pos in (row, 1 - row)]
+                        extra = jnp.where(flip, tiles[1][m : m + 1, :], tiles[0][k : k + 1, :])
+                        total[row, face, column : column + 1, :] += extra
+
+    @pl.when(outer)
+    def _():
+        half = jnp.where(band == 0, 0, 1)
+        patches = tiles[0] + tiles[1]
+        place = lax.broadcasted_iota(I32, (SPAN, CH), 0)
+        inner = (place >= 2) & (place < SPAN - 2)
         for face in range(3):
-            flip = is_mirrored(fn_ref, rot_ref, 3 * group + face, 2 + side) == 1
-            for row in range(2):
-                for depth in range(2):
-                    column = depth if side == 0 else 63 - depth
-                    k, m = [24 + ((pos * 2 + side) * 2 + depth) * 3 + face for pos in (row, 1 - row)]
-                    extra = jnp.where(flip, tiles[1][m : m + 1, :], tiles[0][k : k + 1, :])
-                    total[row, face, column : column + 1, :] += extra
-
-    @pl.when((band == 0) | (band == BANDS - 1))
-    def _():
-        side = jnp.where(band == 0, 0, 1)
-        for face in range(3):
-            order = sel_ref[is_mirrored(fn_ref, rot_ref, 3 * group + face, side)]
+            order = sel_ref[is_mirrored(fn_ref, rot_ref, 3 * group + face, half)]
             for depth in range(2):
-                halves = [wide[pl.ds(12 + (pos * 2 + depth) * 3 + face, BANDS, stride=TAIL), :] for pos in range(2)]
+                halves = [wide[pl.ds(16 + (pos * 2 + depth) * 3 + face, BANDS, stride=40), :] for pos in range(2)]
                 extra = mm(order, jnp.concatenate(halves, axis=0).astype(BF))
-                row = jnp.where(band == 0, depth, 1 - depth)
-                total[row, face] += extra
+                total[depth ^ half, face] += jnp.where(inner, extra, 0.0)
+                for side in range(2):
+                    for col in range(2):
+                        k = 16 + ((side * 3 + face) * 2 + depth) * 2 + col
+                        column = 63 - col if side else col
+                        total[depth ^ half, face, column : column + 1, :] += patches[k : k + 1, :]
 
     for row in range(2):
         for face in range(3):
@@ -608,6 +647,7 @@
     factor = (1.0 * 12 * SPAN * SPAN) ** -0.5
     seams = (face_neighbour.T, seam_rotation.T)
     in_smem = {0: "s", 1: "s"}
+    select, plan = tail_plan()
 
     slots = call(
         pack_lines,
@@ -650,7 +690,7 @@
 
     line, tails = call(
         main_kernel,
-        [share, jax.ShapeDtypeStruct((80, CH), F32)],
+        [share, jax.ShapeDtypeStruct((72, CH), F32)],
         [
             pltpu.VMEM((1152, CH), BF),
             pltpu.VMEM((1152, CH), BF),
@@ -666,19 +706,19 @@
             pltpu.VMEM((5, 64, CH), BF),
             pltpu.VMEM((4, 64, CH), F32),
         ],
-        (*seams, corner_fill.T, jnp.asarray(tail_selector(), BF), *lines, first_weight, second_weight),
+        (*seams, corner_fill.T, jnp.asarray(plan), jnp.asarray(select, F32), *lines, first_weight, second_weight),
     )
     slots = call(
         share_kernel,
         jax.ShapeDtypeStruct((BANDS, SLOT_TWO, CH), BF),
-        [pltpu.VMEM((BANDS * CHUNK, CH), F32)],
+        [pltpu.VMEM((HALF, CH), F32)],
         (own, other, line, tails, sent),
     )
     slots = lax.all_to_all(slots, "tile", 0, 0, tiled=True)
-    part = call(reduce_kernel, jax.ShapeDtypeStruct((CHUNK, CH), F32), [], (slots,))
+    part = call(reduce_kernel, jax.ShapeDtypeStruct((SLOT_THREE, CH), F32), [], (slots,))
     reduced = call(
         lambda *refs: spread_kernel(factor, *refs),
-        jax.ShapeDtypeStruct((BANDS, CHUNK, CH), BF),
+        jax.ShapeDtypeStruct((BANDS, SLOT_THREE, CH), BF),
         [],
         (part, swapped(part, 2)),
     )
@@ -687,7 +727,7 @@
     grad_in = call(
         grad_kernel,
         jax.ShapeDtypeStruct((3, 2, SPAN, CH), BF),
-        [pltpu.VMEM((BANDS * TAIL, CH), F32), pltpu.VMEM((2, 3, SPAN, CH), F32)],
+        [pltpu.VMEM((BANDS * 40, CH), F32), pltpu.VMEM((2, 3, SPAN, CH), F32)],
         (*seams, jnp.asarray(order_selector(), BF), slots),
         in_smem,
     )

time: 87.9 us -> 86.4 us (0.983)
  blocking collectives: 62.9 us -> 61.6 us
    all_to_all x1, blocking collectives: 17.5 us -> 16.2 us  [body(): slots = lax.all_to_all(slots, 'tile', 0, 0, tiled=True)]
  transfers between devices with their start and end apart: 6 -> 6, of which waited for: 3 -> 3; matrix products, arithmetic and copies ran while one was open for 0% -> 0% of each run, Pallas kernels for 9% -> 8%
where the time goes in v5:
time: 86.4 us; the launch traced here: 86.1 us
  blocking collectives  61.6 us (71%)
  Pallas kernels  10.7 us (12%)
  starting transfers between devices  7.97 us (9%)
  waiting for transfers between devices  5.02 us (6%)
    all_to_all x1, blocking collectives, body(): strips = lax.all_to_all(slots, 'tile', 0, 0, tiled=True)  30.5 us
    all_to_all x1, blocking collectives, body(): slots = lax.all_to_all(slots, 'tile', 0, 0, tiled=True)  16.2 us
    all_to_all x1, blocking collectives, body(): reduced = lax.all_to_all(reduced, 'tile', 0, 0, tiled=True)  14.8 us
    pallas_call x10, Pallas kernels, call(): pl.pallas_call(kernel, out_shape=outs, in_specs=[pl.BlockSpec(memory_spac...  10.7 us
    ppermute x6, starting transfers between devices, swapped(): return lax.ppermute(value, 'sub', [(i, i ^ step) for i in range(4)])  7.97 us
    ppermute x6, waiting for transfers between devices, swapped(): return lax.ppermute(value, 'sub', [(i, i ^ step) for i in range(4)])  5.02 us
  transfers between devices with their start and end apart: 6, of which 3 were waited for; matrix products, arithmetic and copies ran while one was open for 0% of the time, Pallas kernels for 8%

profile of v5, /device:TPU:1, one launch (start us, length us, event | category | flops | bytes accessed | tf_op | source)
XLA Modules:
  0.0 86.1 jit_solution(17533344184497645855)
XLA Ops:
  0.6 1.1 %shard_map.139 = bf16[32,144,128]{2,1,0:T(8,128)(2,1)S(1)} custom-call(bf16[3,2,64,128]{3,2,1,0:T(8,128)(2,1)} %f_hbm.1, bf16[3,2,64,128]{3,2,1,0:T(8,128)(2,1)} %g_hbm.1), custom_call_target="tpu_custom_call" | custom-call | tf_op jit(solution)/shard_map/pallas_call | solution.py:41
  1.7 0.0 copy-start.2
  1.7 0.0 copy-start.3
  1.8 0.0 copy-start.7
  1.8 0.0 copy-start.8
  1.8 30.5 %all_to_all.15.in_ref = bf16[32,144,128]{2,1,0:T(8,128)(2,1)S(1)} all-to-all(bf16[32,144,128]{2,1,0:T(8,128)(2,1)S(1)} %shard_map.139), channel_id=1, replica_groups=mesh['tile'=32,'sub'=4] {'tile'}, dimensions={0} | all-to-all | bytes 2359296 | tf_op jit(solution)/shard_map/all_to_all | solution.py:664
  32.3 0.0 copy-done.2
  32.3 0.0 copy-done.3
  32.3 0.0 copy-done.7
  32.3 0.0 copy-done.8
  32.3 0.0 copy-start
  32.3 0.0 copy-start.1
  32.4 1.0 %shard_map.141.own_ref = bf16[6,64,128]{2,1,0:T(8,128)(2,1)S(1)} custom-call(s32[4,12]{1,0:T(4,128)S(1)} %bitcast.5, s32[4,12]{1,0:T(4,128)S(1)} %bitcast.8, bf16[2,384,576]{2,1,0:T(8,128)(2,1)S(1)} %copy-done.2, bf16[4,48,144]{2,1,0:T(8,128)(2,1)S(1)} %copy-done.3, bf16[32,144,128]{2,1,0:T(8,128)(2,1)S(1)} %all_to_all.15.in_ref), custom_call_target="tpu_custom_call" | custom-call | tf_op jit(solution)/shard_map/pallas_call | solution.py:41
  33.4 0.0 copy-start.4
  33.4 0.0 copy-start.6
  33.4 0.0 copy-start.9
  33.4 3.1 %collective-permute-start.2 = (bf16[6,64,128]{2,1,0:T(8,128)(2,1)S(1)}, bf16[6,64,128]{2,1,0:T(8,128)(2,1)S(1)}, u32[]{:S(2)}, u32[]{:S(2)}) collective-permute-start(bf16[6,64,128]{2,1,0:T(8,128)(2,1)S(1)} %shard_map.141.own_ref), channel_id=1, source_target_pairs={{0,3},{1,2},{2,1},{3,0},{4,7},{5,6},{6,5},{7,4},{8,11},{9,10},{10,... | collective-permute-start | bytes 294920 | tf_op jit(solution)/shard_map/ppermute | solution.py:643
  36.5 0.7 collective-permute-start.1
  37.2 0.0 collective-permute-start
  37.2 0.0 copy-done
  37.2 0.0 copy-done.1
  37.2 2.0 %shard_map.140 = (f32[1152,128]{1,0:T(8,128)S(1)}, bf16[1152,128]{1,0:T(8,128)(2,1)S(1)}, f32[512,128]{1,0:T(8,128)S(1)}) custom-call(bf16[32,144,128]{2,1,0:T(8,128)(2,1)S(1)} %all_to_all.15.in_ref, bf16[3,3,128,128]{3,2,1,0:T(8,128)(2,1)S(1)} %copy-done, bf16[3,3,128,128]{3,2,1,0:T(8,128)(2,1)S(1)} %copy-done.1), custom_call_target="tpu_custom_call" | custom-call | tf_op jit(solution)/shard_map/pallas_call | solution.py:41
  39.3 0.5 collective-permute-done.2.refs_3_.three_ref
  39.8 2.2 %collective-permute-done.1.refs_2_.two_ref = bf16[6,64,128]{2,1,0:T(8,128)(2,1)S(1)} collective-permute-done((bf16[6,64,128]{2,1,0:T(8,128)(2,1)S(1)}, bf16[6,64,128]{2,1,0:T(8,128)(2,1)S(1)}, u32[]{:S(2)}, u32[]{:S(2)}) %collective-permute-start.1) | collective-permute-done | bytes 98336 | tf_op jit(solution)/shard_map/ppermute | solution.py:643
  42.0 0.0 collective-permute-done.refs_1_.one_ref
  42.0 0.3 collective-permute-start.3
  42.3 0.0 copy-done.4
  42.3 0.0 copy-done.6
  42.3 0.0 copy-done.9
  42.3 3.7 %shard_map.143 = (f32[1152,128]{1,0:T(8,128)S(1)}, f32[72,128]{1,0:T(8,128)S(1)}) custom-call(s32[4,12]{1,0:T(4,128)S(1)} %bitcast.6, s32[4,12]{1,0:T(4,128)S(1)} %bitcast.9, s32[4,12]{1,0:T(4,128)S(1)} %bitcast.11, s32[48,8]{1,0:T(8,128)S(1)} %copy-done.6, f32[72,64]{1,0:T(8,128)S(1)} %copy-done.4, bf16[6,64,128]{2,1,0:T(8,128)(2,1)S(1)} %shard_map.141.own_ref, ...), custom_call_target="tpu_custom_call" | custom-call | tf_op jit(solution)/shard_map/pallas_call | solution.py:41
  46.0 0.0 collective-permute-done.3.other_ref
  46.0 0.2 shard_map.144
  46.2 0.0 copy-start.5
  46.2 16.2 %all_to_all.16.in_ref = bf16[32,72,128]{2,1,0:T(8,128)(2,1)S(1)} all-to-all(bf16[32,72,128]{2,1,0:T(8,128)(2,1)S(1)} %shard_map.144), channel_id=1, replica_groups=mesh['tile'=32,'sub'=4] {'tile'}, dimensions={0} | all-to-all | bytes 1179648 | tf_op jit(solution)/shard_map/all_to_all | solution.py:717
  62.4 0.1 shard_map.146.refs_0_
  62.5 0.4 collective-permute-start.4
  62.8 2.3 %collective-permute-done.4.refs_1_ = f32[40,128]{1,0:T(8,128)S(1)} collective-permute-done((f32[40,128]{1,0:T(8,128)S(1)}, f32[40,128]{1,0:T(8,128)S(1)}, u32[]{:S(2)}, u32[]{:S(2)}) %collective-permute-start.4) | collective-permute-done | bytes 20512 | tf_op jit(solution)/shard_map/ppermute | solution.py:643
  65.2 14.8 %all_to_all.17.own_ref = bf16[32,40,128]{2,1,0:T(8,128)(2,1)S(1)} all-to-all(bf16[32,40,128]{2,1,0:T(8,128)(2,1)S(1)} %shard_map.147), channel_id=1, replica_groups=mesh['tile'=32,'sub'=4] {'tile'}, dimensions={0} | all-to-all | bytes 655360 | tf_op jit(solution)/shard_map/all_to_all | solution.py:725
  80.0 3.5 %collective-permute-start.5 = (bf16[32,40,128]{2,1,0:T(8,128)(2,1)S(1)}, bf16[32,40,128]{2,1,0:T(8,128)(2,1)S(1)}, u32[]{:S(2)}, u32[]{:S(2)}) collective-permute-start(bf16[32,40,128]{2,1,0:T(8,128)(2,1)S(1)} %all_to_all.17.own_ref), channel_id=1, source_target_pairs={{0,1},{1,0},{2,3},{3,2},{4,5},{5,4},{6,7},{7,6},{8,9},{9,8},{10,11... | collective-permute-start | bytes 983048 | tf_op jit(solution)/shard_map/ppermute | solution.py:643
  83.5 0.0 copy-done.5
  83.5 1.5 %shard_map.145 = bf16[3,2,64,128]{3,2,1,0:T(8,128)(2,1)} custom-call(s32[4,12]{1,0:T(4,128)S(1)} %bitcast.7, s32[4,12]{1,0:T(4,128)S(1)} %bitcast.10, bf16[2,64,64]{2,1,0:T(8,128)(2,1)S(1)} %copy-done.5, bf16[32,72,128]{2,1,0:T(8,128)(2,1)S(1)} %all_to_all.16.in_ref), custom_call_target="tpu_custom_call" | custom-call | tf_op jit(solution)/shard_map/pallas_call | solution.py:41
  85.0 0.0 collective-permute-done.5.other_ref
  85.0 1.1 %shard_map.148 = (f32[1152,128]{1,0:T(8,128)}, f32[1152,128]{1,0:T(8,128)}) custom-call(bf16[32,40,128]{2,1,0:T(8,128)(2,1)S(1)} %all_to_all.17.own_ref, bf16[32,40,128]{2,1,0:T(8,128)(2,1)S(1)} %collective-permute-done.5.other_ref), custom_call_target="tpu_custom_call" | custom-call | tf_op jit(solution)/shard_map/pallas_call | solution.py:41
  (2 shorter events, 0.0 us)
Async XLA Ops:
  1.7 30.6 %copy-start.2 = (bf16[2,384,576]{2,1,0:T(8,128)(2,1)S(1)}, bf16[2,384,576]{2,1,0:T(8,128)(2,1)}, u32[]{:S(2)}) copy-start(bf16[2,384,576]{2,1,0:T(8,128)(2,1)} %constant.10.clone.sel_ref) | copy-start | bytes 2654212
  1.7 30.6 %copy-start.3 = (bf16[4,48,144]{2,1,0:T(8,128)(2,1)S(1)}, bf16[4,48,144]{2,1,0:T(8,128)(2,1)}, u32[]{:S(2)}) copy-start(bf16[4,48,144]{2,1,0:T(8,128)(2,1)} %constant.11.clone.ends_ref) | copy-start | bytes 165892
  1.8 30.6 %copy-start.7 = (s32[12,4]{0,1:T(4,128)S(1)}, s32[12,4]{0,1:T(4,128)}, u32[]{:S(2)}) copy-start(s32[12,4]{0,1:T(4,128)} %param.16) | copy-start | bytes 580
  1.8 30.6 %copy-start.8 = (s32[12,4]{0,1:T(4,128)S(1)}, s32[12,4]{0,1:T(4,128)}, u32[]{:S(2)}) copy-start(s32[12,4]{0,1:T(4,128)} %param.17) | copy-start | bytes 580
  32.3 4.9 %copy-start = (bf16[3,3,128,128]{3,2,1,0:T(8,128)(2,1)S(1)}, bf16[3,3,128,128]{3,2,1,0:T(8,128)(2,1)}, u32[]{:S(2)}) copy-start(bf16[3,3,128,128]{3,2,1,0:T(8,128)(2,1)} %w1_ref.3) | copy-start | bytes 884740
  32.3 4.9 %copy-start.1 = (bf16[3,3,128,128]{3,2,1,0:T(8,128)(2,1)S(1)}, bf16[3,3,128,128]{3,2,1,0:T(8,128)(2,1)}, u32[]{:S(2)}) copy-start(bf16[3,3,128,128]{3,2,1,0:T(8,128)(2,1)} %w2_ref.3) | copy-start | bytes 884740
  33.4 8.9 %copy-start.4 = (f32[72,64]{1,0:T(8,128)S(1)}, f32[72,64]{1,0:T(8,128)}, u32[]{:S(2)}) copy-start(f32[72,64]{1,0:T(8,128)} %constant.13.clone.sel_ref) | copy-start | bytes 55300
  33.4 8.9 %copy-start.6 = (s32[48,8]{1,0:T(8,128)S(1)}, s32[48,8]{1,0:T(8,128)}, u32[]{:S(2)}) copy-start(s32[48,8]{1,0:T(8,128)} %constant.12.clone.plan_ref) | copy-start | bytes 4612
  33.4 8.9 %copy-start.9 = (s32[12,4]{0,1:T(4,128)S(1)}, s32[12,4]{0,1:T(4,128)}, u32[]{:S(2)}) copy-start(s32[12,4]{0,1:T(4,128)} %param.18) | copy-start | bytes 580
  33.4 6.4 %collective-permute-start.2 = (bf16[6,64,128]{2,1,0:T(8,128)(2,1)S(1)}, bf16[6,64,128]{2,1,0:T(8,128)(2,1)S(1)}, u32[]{:S(2)}, u32[]{:S(2)}) collective-permute-start(bf16[6,64,128]{2,1,0:T(8,128)(2,1)S(1)} %shard_map.141.own_ref), channel_id=1, source_target_pairs={{0,3},{1,2},{2,1},{3,0},{4,7},{5,6},{6,5},{7,4},{8,11},{9,10},{10,... | collective-permute-start | bytes 294920 | tf_op jit(solution)/shard_map/ppermute | solution.py:643
  36.5 5.5 %collective-permute-start.1 = (bf16[6,64,128]{2,1,0:T(8,128)(2,1)S(1)}, bf16[6,64,128]{2,1,0:T(8,128)(2,1)S(1)}, u32[]{:S(2)}, u32[]{:S(2)}) collective-permute-start(bf16[6,64,128]{2,1,0:T(8,128)(2,1)S(1)} %shard_map.141.own_ref), channel_id=1, source_target_pairs={{0,2},{1,3},{2,0},{3,1},{4,6},{5,7},{6,4},{7,5},{8,10},{9,11},{10,... | collective-permute-start | bytes 294920 | tf_op jit(solution)/shard_map/ppermute | solution.py:643
  37.2 4.7 %collective-permute-start = (bf16[6,64,128]{2,1,0:T(8,128)(2,1)S(1)}, bf16[6,64,128]{2,1,0:T(8,128)(2,1)S(1)}, u32[]{:S(2)}, u32[]{:S(2)}) collective-permute-start(bf16[6,64,128]{2,1,0:T(8,128)(2,1)S(1)} %shard_map.141.own_ref), channel_id=1, source_target_pairs={{0,1},{1,0},{2,3},{3,2},{4,5},{5,4},{6,7},{7,6},{8,9},{9,8},{10,11... | collective-permute-start | bytes 294920 | tf_op jit(solution)/shard_map/ppermute | solution.py:643
  42.0 4.0 %collective-permute-start.3 = (bf16[1152,128]{1,0:T(8,128)(2,1)S(1)}, bf16[1152,128]{1,0:T(8,128)(2,1)S(1)}, u32[]{:S(2)}, u32[]{:S(2)}) collective-permute-start(bf16[1152,128]{1,0:T(8,128)(2,1)S(1)} %shard_map.142), channel_id=1, source_target_pairs={{0,1},{1,0},{2,3},{3,2},{4,5},{5,4},{6,7},{7,6},{8,9},{9,8},{10,11... | collective-permute-start | bytes 884744 | tf_op jit(solution)/shard_map/ppermute | solution.py:643
  46.2 37.3 %copy-start.5 = (bf16[2,64,64]{2,1,0:T(8,128)(2,1)S(1)}, bf16[2,64,64]{2,1,0:T(8,128)(2,1)}, u32[]{:S(2)}) copy-start(bf16[2,64,64]{2,1,0:T(8,128)(2,1)} %constant.14.clone.sel_ref) | copy-start | bytes 49156
  62.5 2.7 %collective-permute-start.4 = (f32[40,128]{1,0:T(8,128)S(1)}, f32[40,128]{1,0:T(8,128)S(1)}, u32[]{:S(2)}, u32[]{:S(2)}) collective-permute-start(f32[40,128]{1,0:T(8,128)S(1)} %shard_map.146.refs_0_), channel_id=1, source_target_pairs={{0,2},{1,3},{2,0},{3,1},{4,6},{5,7},{6,4},{7,5},{8,10},{9,11},{10,... | collective-permute-start | bytes 61448 | tf_op jit(solution)/shard_map/ppermute | solution.py:643
  80.0 5.0 %collective-permute-start.5 = (bf16[32,40,128]{2,1,0:T(8,128)(2,1)S(1)}, bf16[32,40,128]{2,1,0:T(8,128)(2,1)S(1)}, u32[]{:S(2)}, u32[]{:S(2)}) collective-permute-start(bf16[32,40,128]{2,1,0:T(8,128)(2,1)S(1)} %all_to_all.17.own_ref), channel_id=1, source_target_pairs={{0,1},{1,0},{2,3},{3,2},{4,5},{5,4},{6,7},{7,6},{8,9},{9,8},{10,11... | collective-permute-start | bytes 983048 | tf_op jit(solution)/shard_map/ppermute | solution.py:643

commit v6 on v5

--- a/solution.py
+++ b/solution.py
@@ -98,14 +98,14 @@
 
 
 def line_selector():
-    select = np.zeros((2, WINDOW * 64, 4 * STRIP + 6 * ENDS), np.float32)
+    select = np.zeros((2, WINDOW * ENDS, 4 * STRIP + 6 * ENDS), np.float32)
     for mirrored in range(2):
         for j in range(WINDOW):
             part, parity = j // 2, j % 2
             for fld in range(2):
                 for depth in range(2):
                     for face in range(3):
-                        base = j * 64 + (fld * 2 + depth) * 16 + face
+                        base = j * ENDS + (fld * 2 + depth) * 12 + face
                         column = STRIP * mirrored + (5 - j if mirrored else j) * 12 + fld * 6 + face
                         select[mirrored, base, column + depth * 3] = 1
                         select[mirrored, base + 3, 2 * STRIP + column + (1 - depth) * 3] = 1
@@ -143,15 +143,16 @@
         block = in_ref[source].astype(F32)[STRIP : STRIP + ENDS]
         ends.append(jnp.where(source == 0, first_ends, jnp.where(source == BANDS - 1, last_ends, block)))
     pieces = jnp.concatenate([first.astype(F32), last.astype(F32)] + ends, axis=0).astype(BF)
-    place = lax.broadcasted_iota(I32, (WINDOW * 64, 1), 0) & 15
-    flip = jnp.zeros((WINDOW * 64, 1), I32)
+    place = lax.broadcasted_iota(I32, (WINDOW * ENDS, 1), 0)
+    place = place - 12 * ((place * 171) >> 11)
+    flip = jnp.zeros((WINDOW * ENDS, 1), I32)
     for side in range(4):
         for face in range(3):
             flip = jnp.where(place == side * 3 + face, is_mirrored(fn_ref, rot_ref, 3 * group + face, side), flip)
     flip = jnp.broadcast_to(flip.astype(F32), sel_ref.shape[1:]).astype(BF)
     picked = mm(sel_ref[0] * (1 - flip) + sel_ref[1] * flip, pieces).astype(BF)
     for j in range(WINDOW):
-        out_ref[j] = picked[j * 64 : j * 64 + 64]
+        out_ref[j] = picked[j * ENDS : (j + 1) * ENDS]
 
 
 def silu_parts(pre):
@@ -244,7 +245,7 @@
 def main_kernel(
     fn_ref, rot_ref, fill_ref, plan_ref, sel_ref, own_ref, one_ref, two_ref, three_ref, w1_ref, w2_ref,
     share_ref, tail_ref,
-    w1t, w2t, xs, hal, nb, cg, lp, lg, lc, ss, gp, gpu, owe,
+    w1t, w2t, xs, hal, nb, lp, lg, lc, ss, gp, gpu, owe,
 ):
     band, group = here()
     transpose_weights(w1_ref, w1t)
@@ -305,11 +306,16 @@
     def pick_f(plain, mirrored):
         return jnp.where(flip_f > 0.5, mirrored, plain)
 
-    for step, ref in enumerate((own_ref, one_ref, two_ref, three_ref)):
-        start = pl.multiple_of((group ^ step) * 16, 16)
-        for j in range(WINDOW):
-            for block in range(4):
-                xs[block, j, pl.ds(start, 16), :] = ref[j, block * 16 : block * 16 + 16, :]
+    arrived = (own_ref, one_ref, two_ref, three_ref)
+    arrived = [jnp.concatenate([ref[j] for ref in arrived], axis=0) for j in range(WINDOW)]
+    row = lax.broadcasted_iota(I32, (256, 1), 0)
+    source = (((row >> 4) & 3) ^ group) * ENDS + (row >> 6) * 12 + (row & 15)
+    source = jnp.where((row & 15) < 12, source, -1)
+    expand = (source == lax.broadcasted_iota(I32, (256, 4 * ENDS), 1)).astype(F32).astype(BF)
+    arrived = mm(expand, jnp.concatenate(arrived, axis=1)).astype(BF)
+    for j in range(WINDOW):
+        for block in range(4):
+            xs[block, j] = arrived[block * 64 : block * 64 + 64, j * CH : (j + 1) * CH]
     halos = mm(partner, jnp.concatenate([xs[0, j] for j in range(WINDOW)], axis=1)).astype(BF)
     for j in range(WINDOW):
         hal[j] = halos[:, j * CH : (j + 1) * CH]
@@ -322,40 +328,31 @@
             before, after = block_at(block, j - 1), block_at(block, j + 1)
             nb[0, block, j] = pick(before, after)
             nb[1, block, j] = pick(after, before)
-    cg[...] = jnp.zeros_like(cg)
-
-    def line_ends(zero, end, shift):
-        lower, upper = zero + shift, end - shift
-        return lambda value: (pick(value(lower), value(upper)), pick(value(upper), value(lower)))
-
-    def fill_ends(zero, end):
-        first = line_ends(zero, end, 0)
-        second = line_ends(zero, end, 1)
-        h_zero, h_end = first(lambda j: hal[j])
-        h_one, h_last = second(lambda j: hal[j])
-        f_zero, f_end = first(lambda j: xs[0, j])
-        none = jnp.zeros((64, CH), BF)
-        cells = mm(corner_cells, jnp.concatenate([f_zero, f_end], axis=0)).astype(BF)
-        sides = jnp.concatenate([
-            jnp.concatenate([h_zero, h_one], axis=1), jnp.concatenate([h_end, h_last], axis=1)
-        ], axis=0)
-        sides = mm(beside, sides).astype(BF)
-        low = [cells[:64], sides[:64, :CH], sides[:64, CH:], none, none]
-        high = [cells[64:], sides[64:, :CH], sides[64:, CH:], none, none]
-        for block in range(5):
-            nb[0, block, zero] = pick(low[block], nb[0, block, zero])
-            nb[1, block, zero] = pick(nb[1, block, zero], high[block])
-            nb[0, block, end] = pick(nb[0, block, end], low[block])
-            nb[1, block, end] = pick(high[block], nb[1, block, end])
-        cg[0], cg[1] = first(lambda j: xs[2, j])
-
-    @pl.when(band == 0)
-    def _():
-        fill_ends(2, 1)
-
-    @pl.when(band == BANDS - 1)
-    def _():
-        fill_ends(4, 3)
+    at_first, at_last = band == 0, band == BANDS - 1
+
+    def line_ends(value, lower, upper, choice):
+        zero = jnp.where(at_last, value(lower + 2), value(lower))
+        end = jnp.where(at_last, value(upper + 2), value(upper))
+        return choice(zero, end), choice(end, zero)
+
+    h_zero, h_end = line_ends(lambda j: hal[j], 2, 1, pick)
+    h_one, h_last = line_ends(lambda j: hal[j], 3, 0, pick)
+    f_zero, f_end = line_ends(lambda j: xs[0, j], 2, 1, pick)
+    none = jnp.zeros((64, CH), BF)
+    cells = mm(corner_cells, jnp.concatenate([f_zero, f_end], axis=0)).astype(BF)
+    sides = jnp.concatenate([jnp.concatenate([h_zero, h_one], axis=1), jnp.concatenate([h_end, h_last], axis=1)], axis=0)
+    sides = mm(beside, sides).astype(BF)
+    low = [cells[:64], sides[:64, :CH], sides[:64, CH:], none, none]
+    high = [cells[64:], sides[64:, :CH], sides[64:, CH:], none, none]
+    for block in range(5):
+        for slot, here_now in ((2, at_first), (4, at_last)):
+            before, after = nb[0, block, slot], nb[1, block, slot]
+            nb[0, block, slot] = jnp.where(here_now, pick(low[block], before), before)
+            nb[1, block, slot] = jnp.where(here_now, pick(after, high[block]), after)
+            before, after = nb[0, block, slot - 1], nb[1, block, slot - 1]
+            nb[0, block, slot - 1] = jnp.where(here_now, pick(before, low[block]), before)
+            nb[1, block, slot - 1] = jnp.where(here_now, pick(high[block], after), after)
+    corner_grad = line_ends(lambda j: xs[2, j], 2, 1, pick)
 
     def choose(options):
         whole = all(option is not None for option in options)
@@ -394,7 +391,7 @@
         fill(lp, block, field_source(j))
     order_back = [(0, 2), (0, 3), (-1, 2), (-1, 3), None, None, (0, 1), (0, 4), (-1, 1), (-1, 4)]
     for block, at in enumerate(order_back):
-        fill(lg, block, corner_source(block - 4, cg[block - 4]) if at is None else grad_source(*at))
+        fill(lg, block, corner_source(block - 4, corner_grad[block - 4]) if at is None else grad_source(*at))
 
     pre = mm(lp[...], w1_ref[...].reshape(9 * CH, CH))
     back = mm(lg[...], w2t[...])
@@ -414,23 +411,14 @@
         return sums[:64], sums[64:]
 
 
-    def close_ends(zero, end):
-        at_zero, at_end = corner_sums(back[256:384])
-        head = pick_f(ss[zero], ss[end]) + at_zero
-        tail = pick_f(ss[end], ss[zero]) + at_end
-        sides = mm(beside, jnp.concatenate([head, tail], axis=0).astype(BF))
-        head += sides[:64]
-        tail += sides[64:]
-        ss[zero] = pick_f(head, tail)
-        ss[end] = pick_f(tail, head)
-
-    @pl.when(band == 0)
-    def _():
-        close_ends(2, 1)
-
-    @pl.when(band == BANDS - 1)
-    def _():
-        close_ends(4, 3)
+    at_zero, at_end = corner_sums(back[256:384])
+    head, tail = line_ends(lambda j: ss[j], 2, 1, pick_f)
+    head, tail = head + at_zero, tail + at_end
+    sides = mm(beside, jnp.concatenate([head, tail], axis=0).astype(BF))
+    head, tail = head + sides[:64], tail + sides[64:]
+    for slot, here_now in ((2, at_first), (4, at_last)):
+        ss[slot] = jnp.where(here_now, pick_f(head, tail), ss[slot])
+        ss[slot - 1] = jnp.where(here_now, pick_f(tail, head), ss[slot - 1])
 
     unique = {}
     hid = {}
@@ -473,7 +461,6 @@
         for k in range(9):
             share_ref[k * CH : (k + 1) * CH, :] = second[:, k * CH : (k + 1) * CH]
 
-    at_first, at_last = band == 0, band == BANDS - 1
     inner_low = jnp.where(at_first, 0.0, 1.0)
     inner_high = jnp.where(at_last, 0.0, 1.0)
 
@@ -664,7 +651,7 @@
     strips = lax.all_to_all(slots, "tile", 0, 0, tiled=True)
     lines = call(
         gather_lines,
-        jax.ShapeDtypeStruct((WINDOW, 64, CH), BF),
+        jax.ShapeDtypeStruct((WINDOW, ENDS, CH), BF),
         [],
         (*seams, jnp.asarray(line_selector(), BF), jnp.asarray(ends_selector(), BF), strips),
         in_smem,
@@ -697,7 +684,6 @@
             pltpu.VMEM((4, WINDOW, 64, CH), BF),
             pltpu.VMEM((WINDOW, 64, CH), BF),
             pltpu.VMEM((2, 5, 5, 64, CH), BF),
-            pltpu.VMEM((2, 64, CH), BF),
             pltpu.VMEM((256, 1152), BF),
             pltpu.VMEM((640, 1152), BF),
             pltpu.VMEM((512, 1152), BF),

time: 86.4 us -> 85.1 us (0.985)
  transfers between devices with their start and end apart: 6 -> 6, of which waited for: 3 -> 2; matrix products, arithmetic and copies ran while one was open for 0% -> 0% of each run, Pallas kernels for 8% -> 8%
where the time goes in v6:
time: 85.1 us; the launch traced here: 84.8 us
  blocking collectives  61.6 us (72%)
  Pallas kernels  10.4 us (12%)
  starting transfers between devices  7.68 us (9%)
  waiting for transfers between devices  4.25 us (5%)
    all_to_all x1, blocking collectives, body(): strips = lax.all_to_all(slots, 'tile', 0, 0, tiled=True)  30.5 us
    all_to_all x1, blocking collectives, body(): slots = lax.all_to_all(slots, 'tile', 0, 0, tiled=True)  16.3 us
    all_to_all x1, blocking collectives, body(): reduced = lax.all_to_all(reduced, 'tile', 0, 0, tiled=True)  14.8 us
    pallas_call x10, Pallas kernels, call(): pl.pallas_call(kernel, out_shape=outs, in_specs=[pl.BlockSpec(memory_spac...  10.4 us
    ppermute x6, starting transfers between devices, swapped(): return lax.ppermute(value, 'sub', [(i, i ^ step) for i in range(4)])  7.68 us
    ppermute x6, waiting for transfers between devices, swapped(): return lax.ppermute(value, 'sub', [(i, i ^ step) for i in range(4)])  4.25 us
  transfers between devices with their start and end apart: 6, of which 2 were waited for; matrix products, arithmetic and copies ran while one was open for 0% of the time, Pallas kernels for 8%

profile of v6, /device:TPU:1, one launch (start us, length us, event | category | flops | bytes accessed | tf_op | source)
XLA Modules:
  0.0 84.8 jit_solution(3732322217399231971)
XLA Ops:
  0.6 1.1 %shard_map.139 = bf16[32,144,128]{2,1,0:T(8,128)(2,1)S(1)} custom-call(bf16[3,2,64,128]{3,2,1,0:T(8,128)(2,1)} %f_hbm.1, bf16[3,2,64,128]{3,2,1,0:T(8,128)(2,1)} %g_hbm.1), custom_call_target="tpu_custom_call" | custom-call | tf_op jit(solution)/shard_map/pallas_call | solution.py:41
  1.7 0.0 copy-start.2
  1.7 0.0 copy-start.3
  1.8 0.0 copy-start.7
  1.8 0.0 copy-start.8
  1.8 30.5 %all_to_all.15.in_ref = bf16[32,144,128]{2,1,0:T(8,128)(2,1)S(1)} all-to-all(bf16[32,144,128]{2,1,0:T(8,128)(2,1)S(1)} %shard_map.139), channel_id=1, replica_groups=mesh['tile'=32,'sub'=4] {'tile'}, dimensions={0} | all-to-all | bytes 2359296 | tf_op jit(solution)/shard_map/all_to_all | solution.py:651
  32.3 0.0 copy-start
  32.3 0.0 copy-start.1
  32.3 0.0 copy-done.2
  32.3 0.0 copy-done.3
  32.3 0.0 copy-done.7
  32.3 0.0 copy-done.8
  32.3 1.0 %shard_map.141.own_ref = bf16[6,48,128]{2,1,0:T(8,128)(2,1)S(1)} custom-call(s32[4,12]{1,0:T(4,128)S(1)} %bitcast.5, s32[4,12]{1,0:T(4,128)S(1)} %bitcast.8, bf16[2,288,576]{2,1,0:T(8,128)(2,1)S(1)} %copy-done.2, bf16[4,48,144]{2,1,0:T(8,128)(2,1)S(1)} %copy-done.3, bf16[32,144,128]{2,1,0:T(8,128)(2,1)S(1)} %all_to_all.15.in_ref), custom_call_target="tpu_custom_call" | custom-call | tf_op jit(solution)/shard_map/pallas_call | solution.py:41
  33.4 0.0 copy-start.4
  33.4 0.0 copy-start.6
  33.4 0.0 copy-start.9
  33.4 3.1 %collective-permute-start.2 = (bf16[6,48,128]{2,1,0:T(8,128)(2,1)S(1)}, bf16[6,48,128]{2,1,0:T(8,128)(2,1)S(1)}, u32[]{:S(2)}, u32[]{:S(2)}) collective-permute-start(bf16[6,48,128]{2,1,0:T(8,128)(2,1)S(1)} %shard_map.141.own_ref), channel_id=1, source_target_pairs={{0,3},{1,2},{2,1},{3,0},{4,7},{5,6},{6,5},{7,4},{8,11},{9,10},{10,... | collective-permute-start | bytes 221192 | tf_op jit(solution)/shard_map/ppermute | solution.py:630
  36.5 0.7 collective-permute-start.1
  37.2 0.0 collective-permute-start
  37.2 0.0 copy-done
  37.2 0.0 copy-done.1
  37.2 2.0 %shard_map.140 = (f32[1152,128]{1,0:T(8,128)S(1)}, bf16[1152,128]{1,0:T(8,128)(2,1)S(1)}, f32[512,128]{1,0:T(8,128)S(1)}) custom-call(bf16[32,144,128]{2,1,0:T(8,128)(2,1)S(1)} %all_to_all.15.in_ref, bf16[3,3,128,128]{3,2,1,0:T(8,128)(2,1)S(1)} %copy-done, bf16[3,3,128,128]{3,2,1,0:T(8,128)(2,1)S(1)} %copy-done.1), custom_call_target="tpu_custom_call" | custom-call | tf_op jit(solution)/shard_map/pallas_call | solution.py:41
  39.3 0.0 collective-permute-done.2.refs_3_.three_ref
  39.3 1.6 %collective-permute-done.1.refs_2_.two_ref = bf16[6,48,128]{2,1,0:T(8,128)(2,1)S(1)} collective-permute-done((bf16[6,48,128]{2,1,0:T(8,128)(2,1)S(1)}, bf16[6,48,128]{2,1,0:T(8,128)(2,1)S(1)}, u32[]{:S(2)}, u32[]{:S(2)}) %collective-permute-start.1) | collective-permute-done | bytes 73760 | tf_op jit(solution)/shard_map/ppermute | solution.py:630
  40.9 0.0 collective-permute-done.refs_1_.one_ref
  40.9 0.3 collective-permute-start.3
  41.2 0.0 copy-done.4
  41.3 0.0 copy-done.6
  41.3 0.0 copy-done.9
  41.3 3.3 %shard_map.143 = (f32[1152,128]{1,0:T(8,128)S(1)}, f32[72,128]{1,0:T(8,128)S(1)}) custom-call(s32[4,12]{1,0:T(4,128)S(1)} %bitcast.6, s32[4,12]{1,0:T(4,128)S(1)} %bitcast.9, s32[4,12]{1,0:T(4,128)S(1)} %bitcast.11, s32[48,8]{1,0:T(8,128)S(1)} %copy-done.6, f32[72,64]{1,0:T(8,128)S(1)} %copy-done.4, bf16[6,48,128]{2,1,0:T(8,128)(2,1)S(1)} %shard_map.141.own_ref, ...), custom_call_target="tpu_custom_call" | custom-call | tf_op jit(solution)/shard_map/pallas_call | solution.py:41
  44.6 0.0 collective-permute-done.3.other_ref
  44.6 0.2 shard_map.144
  44.8 0.0 copy-start.5
  44.8 16.3 %all_to_all.16.in_ref = bf16[32,72,128]{2,1,0:T(8,128)(2,1)S(1)} all-to-all(bf16[32,72,128]{2,1,0:T(8,128)(2,1)S(1)} %shard_map.144), channel_id=1, replica_groups=mesh['tile'=32,'sub'=4] {'tile'}, dimensions={0} | all-to-all | bytes 1179648 | tf_op jit(solution)/shard_map/all_to_all | solution.py:703
  61.1 0.1 shard_map.146.refs_0_
  61.2 0.1 collective-permute-start.4
  61.3 2.6 %collective-permute-done.4.refs_1_ = f32[40,128]{1,0:T(8,128)S(1)} collective-permute-done((f32[40,128]{1,0:T(8,128)S(1)}, f32[40,128]{1,0:T(8,128)S(1)}, u32[]{:S(2)}, u32[]{:S(2)}) %collective-permute-start.4) | collective-permute-done | bytes 20512 | tf_op jit(solution)/shard_map/ppermute | solution.py:630
  63.9 14.8 %all_to_all.17.own_ref = bf16[32,40,128]{2,1,0:T(8,128)(2,1)S(1)} all-to-all(bf16[32,40,128]{2,1,0:T(8,128)(2,1)S(1)} %shard_map.147), channel_id=1, replica_groups=mesh['tile'=32,'sub'=4] {'tile'}, dimensions={0} | all-to-all | bytes 655360 | tf_op jit(solution)/shard_map/all_to_all | solution.py:711
  78.7 3.5 %collective-permute-start.5 = (bf16[32,40,128]{2,1,0:T(8,128)(2,1)S(1)}, bf16[32,40,128]{2,1,0:T(8,128)(2,1)S(1)}, u32[]{:S(2)}, u32[]{:S(2)}) collective-permute-start(bf16[32,40,128]{2,1,0:T(8,128)(2,1)S(1)} %all_to_all.17.own_ref), channel_id=1, source_target_pairs={{0,1},{1,0},{2,3},{3,2},{4,5},{5,4},{6,7},{7,6},{8,9},{9,8},{10,11... | collective-permute-start | bytes 983048 | tf_op jit(solution)/shard_map/ppermute | solution.py:630
  82.2 0.0 copy-done.5
  82.2 1.5 %shard_map.145 = bf16[3,2,64,128]{3,2,1,0:T(8,128)(2,1)} custom-call(s32[4,12]{1,0:T(4,128)S(1)} %bitcast.7, s32[4,12]{1,0:T(4,128)S(1)} %bitcast.10, bf16[2,64,64]{2,1,0:T(8,128)(2,1)S(1)} %copy-done.5, bf16[32,72,128]{2,1,0:T(8,128)(2,1)S(1)} %all_to_all.16.in_ref), custom_call_target="tpu_custom_call" | custom-call | tf_op jit(solution)/shard_map/pallas_call | solution.py:41
  83.7 0.0 collective-permute-done.5.other_ref
  83.7 1.1 %shard_map.148 = (f32[1152,128]{1,0:T(8,128)}, f32[1152,128]{1,0:T(8,128)}) custom-call(bf16[32,40,128]{2,1,0:T(8,128)(2,1)S(1)} %all_to_all.17.own_ref, bf16[32,40,128]{2,1,0:T(8,128)(2,1)S(1)} %collective-permute-done.5.other_ref), custom_call_target="tpu_custom_call" | custom-call | tf_op jit(solution)/shard_map/pallas_call | solution.py:41
  (2 shorter events, 0.0 us)
Async XLA Ops:
  1.7 30.6 %copy-start.2 = (bf16[2,288,576]{2,1,0:T(8,128)(2,1)S(1)}, bf16[2,288,576]{2,1,0:T(8,128)(2,1)}, u32[]{:S(2)}) copy-start(bf16[2,288,576]{2,1,0:T(8,128)(2,1)} %constant.10.clone.sel_ref) | copy-start | bytes 1990660
  1.7 30.6 %copy-start.3 = (bf16[4,48,144]{2,1,0:T(8,128)(2,1)S(1)}, bf16[4,48,144]{2,1,0:T(8,128)(2,1)}, u32[]{:S(2)}) copy-start(bf16[4,48,144]{2,1,0:T(8,128)(2,1)} %constant.11.clone.ends_ref) | copy-start | bytes 165892
  1.8 30.6 %copy-start.7 = (s32[12,4]{0,1:T(4,128)S(1)}, s32[12,4]{0,1:T(4,128)}, u32[]{:S(2)}) copy-start(s32[12,4]{0,1:T(4,128)} %param.16) | copy-start | bytes 580
  1.8 30.6 %copy-start.8 = (s32[12,4]{0,1:T(4,128)S(1)}, s32[12,4]{0,1:T(4,128)}, u32[]{:S(2)}) copy-start(s32[12,4]{0,1:T(4,128)} %param.17) | copy-start | bytes 580
  32.3 4.9 %copy-start = (bf16[3,3,128,128]{3,2,1,0:T(8,128)(2,1)S(1)}, bf16[3,3,128,128]{3,2,1,0:T(8,128)(2,1)}, u32[]{:S(2)}) copy-start(bf16[3,3,128,128]{3,2,1,0:T(8,128)(2,1)} %w1_ref.3) | copy-start | bytes 884740
  32.3 4.9 %copy-start.1 = (bf16[3,3,128,128]{3,2,1,0:T(8,128)(2,1)S(1)}, bf16[3,3,128,128]{3,2,1,0:T(8,128)(2,1)}, u32[]{:S(2)}) copy-start(bf16[3,3,128,128]{3,2,1,0:T(8,128)(2,1)} %w2_ref.3) | copy-start | bytes 884740
  33.4 7.9 %copy-start.4 = (f32[72,64]{1,0:T(8,128)S(1)}, f32[72,64]{1,0:T(8,128)}, u32[]{:S(2)}) copy-start(f32[72,64]{1,0:T(8,128)} %constant.13.clone.sel_ref) | copy-start | bytes 55300
  33.4 7.8 %copy-start.6 = (s32[48,8]{1,0:T(8,128)S(1)}, s32[48,8]{1,0:T(8,128)}, u32[]{:S(2)}) copy-start(s32[48,8]{1,0:T(8,128)} %constant.12.clone.plan_ref) | copy-start | bytes 4612
  33.4 7.8 %copy-start.9 = (s32[12,4]{0,1:T(4,128)S(1)}, s32[12,4]{0,1:T(4,128)}, u32[]{:S(2)}) copy-start(s32[12,4]{0,1:T(4,128)} %param.18) | copy-start | bytes 580
  33.4 5.8 %collective-permute-start.2 = (bf16[6,48,128]{2,1,0:T(8,128)(2,1)S(1)}, bf16[6,48,128]{2,1,0:T(8,128)(2,1)S(1)}, u32[]{:S(2)}, u32[]{:S(2)}) collective-permute-start(bf16[6,48,128]{2,1,0:T(8,128)(2,1)S(1)} %shard_map.141.own_ref), channel_id=1, source_target_pairs={{0,3},{1,2},{2,1},{3,0},{4,7},{5,6},{6,5},{7,4},{8,11},{9,10},{10,... | collective-permute-start | bytes 221192 | tf_op jit(solution)/shard_map/ppermute | solution.py:630
  36.5 4.4 %collective-permute-start.1 = (bf16[6,48,128]{2,1,0:T(8,128)(2,1)S(1)}, bf16[6,48,128]{2,1,0:T(8,128)(2,1)S(1)}, u32[]{:S(2)}, u32[]{:S(2)}) collective-permute-start(bf16[6,48,128]{2,1,0:T(8,128)(2,1)S(1)} %shard_map.141.own_ref), channel_id=1, source_target_pairs={{0,2},{1,3},{2,0},{3,1},{4,6},{5,7},{6,4},{7,5},{8,10},{9,11},{10,... | collective-permute-start | bytes 221192 | tf_op jit(solution)/shard_map/ppermute | solution.py:630
  37.2 3.7 %collective-permute-start = (bf16[6,48,128]{2,1,0:T(8,128)(2,1)S(1)}, bf16[6,48,128]{2,1,0:T(8,128)(2,1)S(1)}, u32[]{:S(2)}, u32[]{:S(2)}) collective-permute-start(bf16[6,48,128]{2,1,0:T(8,128)(2,1)S(1)} %shard_map.141.own_ref), channel_id=1, source_target_pairs={{0,1},{1,0},{2,3},{3,2},{4,5},{5,4},{6,7},{7,6},{8,9},{9,8},{10,11... | collective-permute-start | bytes 221192 | tf_op jit(solution)/shard_map/ppermute | solution.py:630
  40.9 3.7 %collective-permute-start.3 = (bf16[1152,128]{1,0:T(8,128)(2,1)S(1)}, bf16[1152,128]{1,0:T(8,128)(2,1)S(1)}, u32[]{:S(2)}, u32[]{:S(2)}) collective-permute-start(bf16[1152,128]{1,0:T(8,128)(2,1)S(1)} %shard_map.142), channel_id=1, source_target_pairs={{0,1},{1,0},{2,3},{3,2},{4,5},{5,4},{6,7},{7,6},{8,9},{9,8},{10,11... | collective-permute-start | bytes 884744 | tf_op jit(solution)/shard_map/ppermute | solution.py:630
  44.8 37.4 %copy-start.5 = (bf16[2,64,64]{2,1,0:T(8,128)(2,1)S(1)}, bf16[2,64,64]{2,1,0:T(8,128)(2,1)}, u32[]{:S(2)}) copy-start(bf16[2,64,64]{2,1,0:T(8,128)(2,1)} %constant.14.clone.sel_ref) | copy-start | bytes 49156
  61.2 2.7 %collective-permute-start.4 = (f32[40,128]{1,0:T(8,128)S(1)}, f32[40,128]{1,0:T(8,128)S(1)}, u32[]{:S(2)}, u32[]{:S(2)}) collective-permute-start(f32[40,128]{1,0:T(8,128)S(1)} %shard_map.146.refs_0_), channel_id=1, source_target_pairs={{0,2},{1,3},{2,0},{3,1},{4,6},{5,7},{6,4},{7,5},{8,10},{9,11},{10,... | collective-permute-start | bytes 61448 | tf_op jit(solution)/shard_map/ppermute | solution.py:630
  78.7 5.0 %collective-permute-start.5 = (bf16[32,40,128]{2,1,0:T(8,128)(2,1)S(1)}, bf16[32,40,128]{2,1,0:T(8,128)(2,1)S(1)}, u32[]{:S(2)}, u32[]{:S(2)}) collective-permute-start(bf16[32,40,128]{2,1,0:T(8,128)(2,1)S(1)} %all_to_all.17.own_ref), channel_id=1, source_target_pairs={{0,1},{1,0},{2,3},{3,2},{4,5},{5,4},{6,7},{7,6},{8,9},{9,8},{10,11... | collective-permute-start | bytes 983048 | tf_op jit(solution)/shard_map/ppermute | solution.py:630

commit v7 on v6

--- a/solution.py
+++ b/solution.py
@@ -16,11 +16,11 @@
 WINDOW = 6
 ENDS = 48
 STRIP = 12 * WINDOW
-SLOT_ONE = 2 * STRIP
+UNIT = 48
+SLOT_ONE = UNIT + STRIP
 HALF = 9 * CH
 CHUNK = 36
-TAIL = 36
-SLOT_TWO = CHUNK + TAIL
+SLOT_TWO = 80
 SLOT_THREE = 40
 VMEM_BYTES = 48 * 1024 * 1024
 
@@ -72,11 +72,18 @@
     return jnp.where(4 * face + side > partner, rot >> 2, 0)
 
 
-def pack_lines(f_hbm, g_hbm, out_ref, buf, wide, ends, sems):
-    copies = [pltpu.make_async_copy(src, buf.at[k], sems.at[k]) for k, src in enumerate((f_hbm, g_hbm))]
+def unit_of(band):
+    unit = band - 4
+    strip = (unit * 43) >> 7
+    return strip, unit - 3 * strip
+
+
+def pack_lines(f_hbm, g_hbm, fn_hbm, rot_hbm, out_ref, buf, fn_ref, rot_ref, wide, ends, sems):
+    moves = ((f_hbm, buf.at[0]), (g_hbm, buf.at[1]), (fn_hbm, fn_ref), (rot_hbm, rot_ref))
+    copies = [pltpu.make_async_copy(src, dst, sems.at[k]) for k, (src, dst) in enumerate(moves)]
     for copy in copies:
         copy.start()
-    band, _ = here()
+    band, group = here()
     ends[ENDS:STRIP, :] = jnp.zeros((STRIP - ENDS, CH), F32)
     for fld in range(2):
         copies[fld].wait()
@@ -90,15 +97,25 @@
                         ends[place : place + 1, :] = block[col : col + 1, :]
     wide[0:24, :] = wide[SPAN * 12 : SPAN * 12 + 24, :]
     wide[SPAN * 12 + 24 : SPAN * 12 + 48, :] = wide[24:48, :]
+    for copy in copies[2:]:
+        copy.wait()
+    side = jnp.where(band == 0, 0, 1)
+    row = lax.broadcasted_iota(I32, (STRIP, CH), 0)
+    row = row - 3 * ((row * 43) >> 7)
+    flip = jnp.zeros((STRIP, CH), I32)
+    for face in range(3):
+        flip = jnp.where(row == face, is_mirrored(fn_ref, rot_ref, 3 * group + face, side), flip)
     outer = (band == 0) | (band == BANDS - 1)
     strips = [wide[24 * d : 24 * d + STRIP, :] for d in range(BANDS)]
     for d in range(BANDS):
-        rest = jnp.where(outer, strips[BANDS - 1 - d], ends[...])
-        out_ref[d] = jnp.concatenate([strips[d], rest], axis=0).astype(BF)
+        strip, face = unit_of(d)
+        unit = wide[pl.ds(96 * strip + face, UNIT, stride=3), :] if 4 <= d < 28 else ends[0:ENDS, :]
+        line = jnp.where(flip == 1, strips[BANDS - 1 - d], strips[d])
+        out_ref[d] = jnp.concatenate([unit, jnp.where(outer, line, ends[...])], axis=0).astype(BF)
 
 
 def line_selector():
-    select = np.zeros((2, WINDOW * ENDS, 4 * STRIP + 6 * ENDS), np.float32)
+    select = np.zeros((2, WINDOW * ENDS, 2 * STRIP + 6 * ENDS), np.float32)
     for mirrored in range(2):
         for j in range(WINDOW):
             part, parity = j // 2, j % 2
@@ -106,43 +123,23 @@
                 for depth in range(2):
                     for face in range(3):
                         base = j * ENDS + (fld * 2 + depth) * 12 + face
-                        column = STRIP * mirrored + (5 - j if mirrored else j) * 12 + fld * 6 + face
+                        column = (5 - j if mirrored else j) * 12 + fld * 6 + face
                         select[mirrored, base, column + depth * 3] = 1
-                        select[mirrored, base + 3, 2 * STRIP + column + (1 - depth) * 3] = 1
+                        select[mirrored, base + 3, STRIP + column + (1 - depth) * 3] = 1
                         for side in range(2):
-                            source = 4 * STRIP + (3 * mirrored + part) * ENDS + (1 - parity if mirrored else parity) * 24
+                            source = 2 * STRIP + (3 * mirrored + part) * ENDS + (1 - parity if mirrored else parity) * 24
                             select[mirrored, base + 6 + 3 * side, source + fld * 12 + side * 6 + depth * 3 + face] = 1
     return select
 
 
-def ends_selector():
-    select = np.zeros((4, ENDS, SLOT_ONE), np.float32)
-    for k, d in enumerate((0, 1, 30, 31)):
-        for row in range(2):
-            for fld in range(2):
-                for side in range(2):
-                    for depth in range(2):
-                        col = 63 - depth if side else depth
-                        at = (col - 2 * d + 2) % SPAN
-                        other = (col - 60 + 2 * d) % SPAN
-                        base = at * 12 if at < WINDOW else STRIP + other * 12
-                        for face in range(3):
-                            place = row * 24 + fld * 12 + side * 6 + depth * 3 + face
-                            select[k, place, base + fld * 6 + row * 3 + face] = 1
-    return select
-
-
-def gather_lines(fn_ref, rot_ref, sel_ref, ends_ref, in_ref, out_ref):
+def gather_lines(fn_ref, rot_ref, sel_ref, in_ref, out_ref):
     band, group = here()
-    first, last = in_ref[0], in_ref[BANDS - 1]
-    pick_ends = ends_ref[(band & 1) + 2 * (band >> 4)]
-    first_ends, last_ends = mm(pick_ends, first), mm(pick_ends, last)
-    ends = []
+    pieces = [in_ref[d].astype(F32)[UNIT:SLOT_ONE] for d in (0, BANDS - 1)]
     for source in [band + 31 + part for part in range(3)] + [64 - band - part for part in range(3)]:
         source = source & 31
-        block = in_ref[source].astype(F32)[STRIP : STRIP + ENDS]
-        ends.append(jnp.where(source == 0, first_ends, jnp.where(source == BANDS - 1, last_ends, block)))
-    pieces = jnp.concatenate([first.astype(F32), last.astype(F32)] + ends, axis=0).astype(BF)
+        outer = (source == 0) | (source == BANDS - 1)
+        pieces.append(jnp.where(outer, in_ref[source, 0:ENDS, :], in_ref[source, UNIT : UNIT + ENDS, :]).astype(F32))
+    pieces = jnp.concatenate(pieces, axis=0).astype(BF)
     place = lax.broadcasted_iota(I32, (WINDOW * ENDS, 1), 0)
     place = place - 12 * ((place * 171) >> 11)
     flip = jnp.zeros((WINDOW * ENDS, 1), I32)
@@ -174,16 +171,16 @@
     in_ref, w1_ref, w2_ref, own_ref, away_ref, sent, acc, done, w1t, w2t, f2, g2, wide
 ):
     band, group = here()
+    strip, _ = unit_of(band)
     transpose_weights(w1_ref, w1t)
     transpose_weights(w2_ref, w2t)
     for s in range(BANDS):
-        wide[s * STRIP : (s + 1) * STRIP, :] = in_ref[s].astype(F32)[0:STRIP]
-    for q in range(WINDOW):
+        wide[s * UNIT : (s + 1) * UNIT, :] = in_ref[s, 0:UNIT, :].astype(F32)
+    for q in range(12):
         for fld, target in enumerate((f2, g2)):
             for row in range(2):
-                for face in range(3):
-                    piece = wide[pl.ds(q * 12 + fld * 6 + row * 3 + face, BANDS, stride=STRIP), :]
-                    target[pl.ds(q * 192 + face * 64 + row, BANDS, stride=2), :] = piece
+                piece = wide[pl.ds(q * 4 + fld * 2 + row, BANDS, stride=UNIT), :]
+                target[pl.ds(q * 64 + row, BANDS, stride=2), :] = piece
 
     def conv_weights(ref):
         return jnp.concatenate([ref[a].reshape(3 * CH, CH) for a in range(3)], axis=1)
@@ -201,27 +198,26 @@
         return pltpu.roll(value, 1, 0)
 
     def three_columns(ref, first, count):
-        return jnp.concatenate([ref[first + 192 * b : first + 192 * b + count, :].astype(BF) for b in range(3)], axis=1)
-
-    y = mm(three_columns(f2, 0, 768), conv_weights(w1_ref))
+        return jnp.concatenate([ref[first + 64 * b : first + 64 * b + count, :].astype(BF) for b in range(3)], axis=1)
+
+    y = mm(three_columns(f2, 0, 640), conv_weights(w1_ref))
     pre = down_one(y[:, :CH]) + y[:, CH : 2 * CH] + up_one(y[:, 2 * CH :])
-    z = mm(three_columns(g2, 0, 768), back_weights(w2t))
+    z = mm(three_columns(g2, 0, 640), back_weights(w2t))
     back = up_one(z[:, :CH]) + z[:, CH : 2 * CH] + down_one(z[:, 2 * CH :])
     hidden, slope = silu_parts(pre)
-    index = lax.broadcasted_iota(I32, (768, CH), 0)
-    step = (index >= 192).astype(I32) + (index >= 384).astype(I32) + (index >= 576).astype(I32)
-    col = 2 * band - 1 + step
+    index = lax.broadcasted_iota(I32, (640, CH), 0)
+    col = 8 * strip - 1 + (index >> 6)
     row = index & 63
-    inner = (row >= 1) & (row <= 62) & (col >= 1) & (col <= 62)
+    inner = (row >= 1) & (row <= 62) & (col >= 1) & (col <= 62) & (band >= 4) & (band < 28)
     gpre = jnp.where(inner, back * slope, 0.0).astype(BF)
-    hid = jnp.where(inner, hidden, 0.0)[192:576].astype(BF)
-
-    gown = gpre[192:576].astype(F32)
-    gcat = jnp.concatenate([up_one(gown).astype(BF), gpre[192:576], down_one(gown).astype(BF)], axis=1)
-    first = mm_t(three_columns(f2, 192, 384), gcat)
+    hid = jnp.where(inner, hidden, 0.0)[64:576].astype(BF)
+
+    gown = gpre[64:576].astype(F32)
+    gcat = jnp.concatenate([up_one(gown).astype(BF), gpre[64:576], down_one(gown).astype(BF)], axis=1)
+    first = mm_t(three_columns(f2, 64, 512), gcat)
     hown = hid.astype(F32)
     hcat = jnp.concatenate([down_one(hown).astype(BF), hid, up_one(hown).astype(BF)], axis=1)
-    gback = jnp.concatenate([g2[start : start + 384, :].astype(BF) for start in (576, 384, 192)], axis=1)
+    gback = jnp.concatenate([g2[start : start + 512, :].astype(BF) for start in (192, 128, 64)], axis=1)
     second = mm_t(hcat, gback)
     for k, (a, b) in enumerate(TAPS):
         top, low = k * CH, 1152 + k * CH
@@ -231,15 +227,12 @@
     own_ref[...] = acc[pl.ds(pl.multiple_of(core * HALF, CH), HALF), :]
     away_ref[...] = acc[pl.ds(pl.multiple_of((1 - core) * HALF, CH), HALF), :].astype(BF)
 
-    gthree = jnp.concatenate([gpre[0:384], gpre[192:576], gpre[384:768]], axis=1)
+    gthree = jnp.concatenate([gpre[0:512], gpre[64:576], gpre[128:640]], axis=1)
     z = mm(gthree, back_weights(w1t))
-    done[...] = up_one(z[:, :CH]) + z[:, CH : 2 * CH] + down_one(z[:, 2 * CH :]) + g2[384:768, :]
-    sent[...] = jnp.zeros_like(sent)
-    for q in range(2):
-        for face in range(3):
-            for row in range(2):
-                piece = done[pl.ds(q * 192 + face * 64 + row, BANDS, stride=2), :]
-                sent[pl.ds((q * 3 + face) * 2 + row, BANDS, stride=16), :] = piece
+    done[...] = up_one(z[:, :CH]) + z[:, CH : 2 * CH] + down_one(z[:, 2 * CH :]) + g2[128:640, :]
+    for q in range(8):
+        for row in range(2):
+            sent[pl.ds(q * 2 + row, BANDS, stride=16), :] = done[pl.ds(q * 64 + row, BANDS, stride=2), :]
 
 
 def main_kernel(
@@ -543,7 +536,8 @@
     total[...] = own_ref[...] + other_ref[...].astype(F32) + line_ref[...]
     for i in range(BANDS):
         start = 0 if i == 0 else 24 if i == BANDS - 1 else 48
-        parts = [total[CHUNK * i : CHUNK * i + CHUNK, :], sent[i * 16 : i * 16 + 12, :], tail_ref[start : start + 24, :]]
+        parts = [total[CHUNK * i : CHUNK * i + CHUNK, :], sent[i * 16 : i * 16 + 16, :], tail_ref[start : start + 24, :]]
+        parts.append(jnp.zeros((4, CH), F32))
         out_ref[i] = jnp.concatenate(parts, axis=0).astype(BF)
 
 
@@ -582,13 +576,13 @@
 def grad_kernel(fn_ref, rot_ref, sel_ref, in_ref, out_ref, wide, total):
     band, group = here()
     for i in range(BANDS):
-        wide[i * 40 : i * 40 + 40, :] = in_ref[i].astype(F32)[32:SLOT_TWO]
-    for q in range(2):
-        for face in range(3):
-            for row in range(2):
-                piece = wide[pl.ds(4 + (q * 3 + face) * 2 + row, BANDS, stride=40), :]
-                total[row, face, pl.ds(q, BANDS, stride=2), :] = piece
-    tiles = [wide[pl.ds(pl.multiple_of(src * 40, 8), 40), :] for src in (band, BANDS - 1 - band)]
+        wide[i * 48 : i * 48 + 48, :] = in_ref[i, 32:SLOT_TWO, :].astype(F32)
+    for face in range(3):
+        for row in range(2):
+            for q in range(8):
+                piece = wide[pl.ds((4 + face) * 48 + 4 + q * 2 + row, 8, stride=144), :]
+                total[row, face, pl.ds(q, 8, stride=8), :] = piece
+    tiles = [wide[pl.ds(pl.multiple_of(src * 48, 16), 48), :] for src in (band, BANDS - 1 - band)]
     outer = (band == 0) | (band == BANDS - 1)
 
     @pl.when(~outer)
@@ -599,7 +593,7 @@
                 for row in range(2):
                     for depth in range(2):
                         column = depth if side == 0 else 63 - depth
-                        k, m = [16 + ((pos * 2 + side) * 2 + depth) * 3 + face for pos in (row, 1 - row)]
+                        k, m = [20 + ((pos * 2 + side) * 2 + depth) * 3 + face for pos in (row, 1 - row)]
                         extra = jnp.where(flip, tiles[1][m : m + 1, :], tiles[0][k : k + 1, :])
                         total[row, face, column : column + 1, :] += extra
 
@@ -612,12 +606,12 @@
         for face in range(3):
             order = sel_ref[is_mirrored(fn_ref, rot_ref, 3 * group + face, half)]
             for depth in range(2):
-                halves = [wide[pl.ds(16 + (pos * 2 + depth) * 3 + face, BANDS, stride=40), :] for pos in range(2)]
+                halves = [wide[pl.ds(20 + (pos * 2 + depth) * 3 + face, BANDS, stride=48), :] for pos in range(2)]
                 extra = mm(order, jnp.concatenate(halves, axis=0).astype(BF))
                 total[depth ^ half, face] += jnp.where(inner, extra, 0.0)
                 for side in range(2):
                     for col in range(2):
-                        k = 16 + ((side * 3 + face) * 2 + depth) * 2 + col
+                        k = 20 + ((side * 3 + face) * 2 + depth) * 2 + col
                         column = 63 - col if side else col
                         total[depth ^ half, face, column : column + 1, :] += patches[k : k + 1, :]
 
@@ -641,19 +635,21 @@
         jax.ShapeDtypeStruct((BANDS, SLOT_ONE, CH), BF),
         [
             pltpu.VMEM((2, 3, 2, SPAN, CH), BF),
+            pltpu.SMEM((4, 12), I32),
+            pltpu.SMEM((4, 12), I32),
             pltpu.VMEM(((SPAN + 4) * 12, CH), F32),
             pltpu.VMEM((STRIP, CH), F32),
-            pltpu.SemaphoreType.DMA((2,)),
+            pltpu.SemaphoreType.DMA((4,)),
         ],
-        tuple(pltpu.with_memory_space_constraint(value, pltpu.HBM) for value in (field_in, grad_out)),
-        {0: "h", 1: "h"},
+        tuple(pltpu.with_memory_space_constraint(value, pltpu.HBM) for value in (field_in, grad_out, *seams)),
+        dict.fromkeys(range(4), "h"),
     )
     strips = lax.all_to_all(slots, "tile", 0, 0, tiled=True)
     lines = call(
         gather_lines,
         jax.ShapeDtypeStruct((WINDOW, ENDS, CH), BF),
         [],
-        (*seams, jnp.asarray(line_selector(), BF), jnp.asarray(ends_selector(), BF), strips),
+        (*seams, jnp.asarray(line_selector(), BF), strips),
         in_smem,
     )
     lines = (lines, *[swapped(lines, step) for step in (1, 2, 3)])
@@ -663,12 +659,12 @@
         [share, jax.ShapeDtypeStruct((HALF, CH), BF), jax.ShapeDtypeStruct((BANDS * 16, CH), F32)],
         [
             pltpu.VMEM((2304, CH), F32),
-            pltpu.VMEM((384, CH), F32),
+            pltpu.VMEM((512, CH), F32),
             pltpu.VMEM((1152, CH), BF),
             pltpu.VMEM((1152, CH), BF),
-            pltpu.VMEM((1152, CH), F32),
-            pltpu.VMEM((1152, CH), F32),
-            pltpu.VMEM((BANDS * STRIP, CH), F32),
+            pltpu.VMEM((768, CH), F32),
+            pltpu.VMEM((768, CH), F32),
+            pltpu.VMEM((BANDS * UNIT, CH), F32),
         ],
         (strips, first_weight, second_weight),
     )
@@ -713,7 +709,7 @@
     grad_in = call(
         grad_kernel,
         jax.ShapeDtypeStruct((3, 2, SPAN, CH), BF),
-        [pltpu.VMEM((BANDS * 40, CH), F32), pltpu.VMEM((2, 3, SPAN, CH), F32)],
+        [pltpu.VMEM((BANDS * 48, CH), F32), pltpu.VMEM((2, 3, SPAN, CH), F32)],
         (*seams, jnp.asarray(order_selector(), BF), slots),
         in_smem,
     )

time: 85.1 us -> 83.4 us (0.980)
  blocking collectives: 61.6 us -> 58.6 us
  starting transfers between devices: 7.68 us -> 9.16 us
    all_to_all x1, blocking collectives: 30.5 us -> 26.7 us  [body(): strips = lax.all_to_all(slots, 'tile', 0, 0, tiled=True)]
    ppermute x6, starting transfers between devices: 7.68 us -> 9.16 us  [swapped(): return lax.ppermute(value, 'sub', [(i, i ^ step) for i in range(4)])]
  transfers between devices with their start and end apart: 6 -> 6, of which waited for: 2 -> 2; matrix products, arithmetic and copies ran while one was open for 0% -> 0% of each run, Pallas kernels for 8% -> 9%
where the time goes in v7:
time: 83.4 us; the launch traced here: 83 us
  blocking collectives  58.6 us (70%)
  Pallas kernels  10.6 us (13%)
  starting transfers between devices  9.16 us (11%)
  waiting for transfers between devices  3.45 us (4%)
    all_to_all x1, blocking collectives, body(): strips = lax.all_to_all(slots, 'tile', 0, 0, tiled=True)  26.7 us
    all_to_all x1, blocking collectives, body(): slots = lax.all_to_all(slots, 'tile', 0, 0, tiled=True)  17.1 us
    all_to_all x1, blocking collectives, body(): reduced = lax.all_to_all(reduced, 'tile', 0, 0, tiled=True)  14.9 us
    pallas_call x10, Pallas kernels, call(): pl.pallas_call(kernel, out_shape=outs, in_specs=[pl.BlockSpec(memory_spac...  10.6 us
    ppermute x6, starting transfers between devices, swapped(): return lax.ppermute(value, 'sub', [(i, i ^ step) for i in range(4)])  9.16 us
    ppermute x6, waiting for transfers between devices, swapped(): return lax.ppermute(value, 'sub', [(i, i ^ step) for i in range(4)])  3.45 us
  transfers between devices with their start and end apart: 6, of which 2 were waited for; matrix products, arithmetic and copies ran while one was open for 0% of the time, Pallas kernels for 9%

profile of v7, /device:TPU:1, one launch (start us, length us, event | category | flops | bytes accessed | tf_op | source)
XLA Modules:
  0.0 83.0 jit_solution(8703304269344418656)
XLA Ops:
  0.6 1.2 %shard_map.130 = bf16[32,120,128]{2,1,0:T(8,128)(2,1)S(1)} custom-call(bf16[3,2,64,128]{3,2,1,0:T(8,128)(2,1)} %f_hbm.1, bf16[3,2,64,128]{3,2,1,0:T(8,128)(2,1)} %g_hbm.1, s32[4,12]{1,0:T(4,128)} %bitcast.5, s32[4,12]{1,0:T(4,128)} %bitcast.9), custom_call_target="tpu_custom_call" | custom-call | tf_op jit(solution)/shard_map/pallas_call | solution.py:41
  1.8 0.0 copy-start.2
  1.8 0.0 copy-start.4
  1.8 0.0 copy-start.5
  1.8 26.7 %all_to_all.15.in_ref = bf16[32,120,128]{2,1,0:T(8,128)(2,1)S(1)} all-to-all(bf16[32,120,128]{2,1,0:T(8,128)(2,1)S(1)} %shard_map.130), channel_id=1, replica_groups=mesh['tile'=32,'sub'=4] {'tile'}, dimensions={0} | all-to-all | bytes 1966080 | tf_op jit(solution)/shard_map/all_to_all | solution.py:647
  28.5 0.0 copy-done.2
  28.5 0.0 copy-done.4
  28.5 0.0 copy-done.5
  28.5 0.0 copy-start
  28.5 0.0 copy-start.1
  28.6 0.9 %shard_map.132.own_ref = bf16[6,48,128]{2,1,0:T(8,128)(2,1)S(1)} custom-call(s32[4,12]{1,0:T(4,128)S(1)} %bitcast.6, s32[4,12]{1,0:T(4,128)S(1)} %bitcast.10, bf16[2,288,432]{2,1,0:T(8,128)(2,1)S(1)} %copy-done.2, bf16[32,120,128]{2,1,0:T(8,128)(2,1)S(1)} %all_to_all.15.in_ref), custom_call_target="tpu_custom_call" | custom-call | tf_op jit(solution)/shard_map/pallas_call | solution.py:41
  29.5 3.4 %collective-permute-start.2 = (bf16[6,48,128]{2,1,0:T(8,128)(2,1)S(1)}, bf16[6,48,128]{2,1,0:T(8,128)(2,1)S(1)}, u32[]{:S(2)}, u32[]{:S(2)}) collective-permute-start(bf16[6,48,128]{2,1,0:T(8,128)(2,1)S(1)} %shard_map.132.own_ref), channel_id=1, source_target_pairs={{0,3},{1,2},{2,1},{3,0},{4,7},{5,6},{6,5},{7,4},{8,11},{9,10},{10,... | collective-permute-start | bytes 221192 | tf_op jit(solution)/shard_map/ppermute | solution.py:624
  32.9 0.7 collective-permute-start.1
  33.6 0.0 collective-permute-start
  33.6 0.0 copy-done
  33.6 0.0 copy-done.1
  33.6 2.2 %shard_map.131 = (f32[1152,128]{1,0:T(8,128)S(1)}, bf16[1152,128]{1,0:T(8,128)(2,1)S(1)}, f32[512,128]{1,0:T(8,128)S(1)}) custom-call(bf16[32,120,128]{2,1,0:T(8,128)(2,1)S(1)} %all_to_all.15.in_ref, bf16[3,3,128,128]{3,2,1,0:T(8,128)(2,1)S(1)} %copy-done, bf16[3,3,128,128]{3,2,1,0:T(8,128)(2,1)S(1)} %copy-done.1), custom_call_target="tpu_custom_call" | custom-call | tf_op jit(solution)/shard_map/pallas_call | solution.py:41
  35.9 0.0 collective-permute-done.2.refs_3_.three_ref
  35.9 1.4 %collective-permute-done.1.refs_2_.two_ref = bf16[6,48,128]{2,1,0:T(8,128)(2,1)S(1)} collective-permute-done((bf16[6,48,128]{2,1,0:T(8,128)(2,1)S(1)}, bf16[6,48,128]{2,1,0:T(8,128)(2,1)S(1)}, u32[]{:S(2)}, u32[]{:S(2)}) %collective-permute-start.1) | collective-permute-done | bytes 73760 | tf_op jit(solution)/shard_map/ppermute | solution.py:624
  37.3 0.0 collective-permute-done.refs_1_.one_ref
  37.3 0.0 copy-start.3
  37.3 0.0 copy-start.7
  37.3 0.0 copy-start.8
  37.3 0.4 collective-permute-start.3
  37.8 0.3 copy-done.3
  38.1 0.0 copy-done.7
  38.1 0.0 copy-done.8
  38.1 3.3 %shard_map.134 = (f32[1152,128]{1,0:T(8,128)S(1)}, f32[72,128]{1,0:T(8,128)S(1)}) custom-call(s32[4,12]{1,0:T(4,128)S(1)} %bitcast.7, s32[4,12]{1,0:T(4,128)S(1)} %bitcast.11, s32[4,12]{1,0:T(4,128)S(1)} %bitcast.13, s32[48,8]{1,0:T(8,128)S(1)} %copy-done.7, f32[72,64]{1,0:T(8,128)S(1)} %copy-done.3, bf16[6,48,128]{2,1,0:T(8,128)(2,1)S(1)} %shard_map.132.own_ref, ...), custom_call_target="tpu_custom_call" | custom-call | tf_op jit(solution)/shard_map/pallas_call | solution.py:41
  41.4 0.0 collective-permute-done.3.other_ref
  41.5 0.2 shard_map.135
  41.7 17.1 %all_to_all.16.in_ref = bf16[32,80,128]{2,1,0:T(8,128)(2,1)S(1)} all-to-all(bf16[32,80,128]{2,1,0:T(8,128)(2,1)S(1)} %shard_map.135), channel_id=1, replica_groups=mesh['tile'=32,'sub'=4] {'tile'}, dimensions={0} | all-to-all | bytes 1310720 | tf_op jit(solution)/shard_map/all_to_all | solution.py:699
  58.7 0.1 shard_map.137.refs_0_
  58.8 0.7 collective-permute-start.4
  59.5 2.0 %collective-permute-done.4.refs_1_ = f32[40,128]{1,0:T(8,128)S(1)} collective-permute-done((f32[40,128]{1,0:T(8,128)S(1)}, f32[40,128]{1,0:T(8,128)S(1)}, u32[]{:S(2)}, u32[]{:S(2)}) %collective-permute-start.4) | collective-permute-done | bytes 20512 | tf_op jit(solution)/shard_map/ppermute | solution.py:624
  61.5 0.0 copy-start.6
  61.5 14.9 %all_to_all.17.own_ref = bf16[32,40,128]{2,1,0:T(8,128)(2,1)S(1)} all-to-all(bf16[32,40,128]{2,1,0:T(8,128)(2,1)S(1)} %shard_map.138), channel_id=1, replica_groups=mesh['tile'=32,'sub'=4] {'tile'}, dimensions={0} | all-to-all | bytes 655360 | tf_op jit(solution)/shard_map/all_to_all | solution.py:707
  76.4 3.9 %collective-permute-start.5 = (bf16[32,40,128]{2,1,0:T(8,128)(2,1)S(1)}, bf16[32,40,128]{2,1,0:T(8,128)(2,1)S(1)}, u32[]{:S(2)}, u32[]{:S(2)}) collective-permute-start(bf16[32,40,128]{2,1,0:T(8,128)(2,1)S(1)} %all_to_all.17.own_ref), channel_id=1, source_target_pairs={{0,1},{1,0},{2,3},{3,2},{4,5},{5,4},{6,7},{7,6},{8,9},{9,8},{10,11... | collective-permute-start | bytes 983048 | tf_op jit(solution)/shard_map/ppermute | solution.py:624
  80.3 0.0 copy-done.6
  80.3 1.6 %shard_map.136 = bf16[3,2,64,128]{3,2,1,0:T(8,128)(2,1)} custom-call(s32[4,12]{1,0:T(4,128)S(1)} %bitcast.8, s32[4,12]{1,0:T(4,128)S(1)} %bitcast.12, bf16[2,64,64]{2,1,0:T(8,128)(2,1)S(1)} %copy-done.6, bf16[32,80,128]{2,1,0:T(8,128)(2,1)S(1)} %all_to_all.16.in_ref), custom_call_target="tpu_custom_call" | custom-call | tf_op jit(solution)/shard_map/pallas_call | solution.py:41
  81.9 0.0 collective-permute-done.5.other_ref
  81.9 1.1 %shard_map.139 = (f32[1152,128]{1,0:T(8,128)}, f32[1152,128]{1,0:T(8,128)}) custom-call(bf16[32,40,128]{2,1,0:T(8,128)(2,1)S(1)} %all_to_all.17.own_ref, bf16[32,40,128]{2,1,0:T(8,128)(2,1)S(1)} %collective-permute-done.5.other_ref), custom_call_target="tpu_custom_call" | custom-call | tf_op jit(solution)/shard_map/pallas_call | solution.py:41
  (2 shorter events, 0.0 us)
Async XLA Ops:
  1.8 26.7 %copy-start.2 = (bf16[2,288,432]{2,1,0:T(8,128)(2,1)S(1)}, bf16[2,288,432]{2,1,0:T(8,128)(2,1)}, u32[]{:S(2)}) copy-start(bf16[2,288,432]{2,1,0:T(8,128)(2,1)} %constant.8.clone.sel_ref) | copy-start | bytes 1492996
  1.8 26.7 %copy-start.4 = (s32[12,4]{0,1:T(4,128)S(1)}, s32[12,4]{0,1:T(4,128)}, u32[]{:S(2)}) copy-start(s32[12,4]{0,1:T(4,128)} %param.15) | copy-start | bytes 580
  1.8 26.7 %copy-start.5 = (s32[12,4]{0,1:T(4,128)S(1)}, s32[12,4]{0,1:T(4,128)}, u32[]{:S(2)}) copy-start(s32[12,4]{0,1:T(4,128)} %param.16) | copy-start | bytes 580
  28.5 5.1 %copy-start = (bf16[3,3,128,128]{3,2,1,0:T(8,128)(2,1)S(1)}, bf16[3,3,128,128]{3,2,1,0:T(8,128)(2,1)}, u32[]{:S(2)}) copy-start(bf16[3,3,128,128]{3,2,1,0:T(8,128)(2,1)} %w1_ref.3) | copy-start | bytes 884740
  28.5 5.1 %copy-start.1 = (bf16[3,3,128,128]{3,2,1,0:T(8,128)(2,1)S(1)}, bf16[3,3,128,128]{3,2,1,0:T(8,128)(2,1)}, u32[]{:S(2)}) copy-start(bf16[3,3,128,128]{3,2,1,0:T(8,128)(2,1)} %w2_ref.3) | copy-start | bytes 884740
  29.5 6.4 %collective-permute-start.2 = (bf16[6,48,128]{2,1,0:T(8,128)(2,1)S(1)}, bf16[6,48,128]{2,1,0:T(8,128)(2,1)S(1)}, u32[]{:S(2)}, u32[]{:S(2)}) collective-permute-start(bf16[6,48,128]{2,1,0:T(8,128)(2,1)S(1)} %shard_map.132.own_ref), channel_id=1, source_target_pairs={{0,3},{1,2},{2,1},{3,0},{4,7},{5,6},{6,5},{7,4},{8,11},{9,10},{10,... | collective-permute-start | bytes 221192 | tf_op jit(solution)/shard_map/ppermute | solution.py:624
  32.9 4.4 %collective-permute-start.1 = (bf16[6,48,128]{2,1,0:T(8,128)(2,1)S(1)}, bf16[6,48,128]{2,1,0:T(8,128)(2,1)S(1)}, u32[]{:S(2)}, u32[]{:S(2)}) collective-permute-start(bf16[6,48,128]{2,1,0:T(8,128)(2,1)S(1)} %shard_map.132.own_ref), channel_id=1, source_target_pairs={{0,2},{1,3},{2,0},{3,1},{4,6},{5,7},{6,4},{7,5},{8,10},{9,11},{10,... | collective-permute-start | bytes 221192 | tf_op jit(solution)/shard_map/ppermute | solution.py:624
  33.6 3.7 %collective-permute-start = (bf16[6,48,128]{2,1,0:T(8,128)(2,1)S(1)}, bf16[6,48,128]{2,1,0:T(8,128)(2,1)S(1)}, u32[]{:S(2)}, u32[]{:S(2)}) collective-permute-start(bf16[6,48,128]{2,1,0:T(8,128)(2,1)S(1)} %shard_map.132.own_ref), channel_id=1, source_target_pairs={{0,1},{1,0},{2,3},{3,2},{4,5},{5,4},{6,7},{7,6},{8,9},{9,8},{10,11... | collective-permute-start | bytes 221192 | tf_op jit(solution)/shard_map/ppermute | solution.py:624
  37.3 0.8 copy-start.3
  37.3 0.8 copy-start.7
  37.3 0.8 copy-start.8
  37.3 4.1 %collective-permute-start.3 = (bf16[1152,128]{1,0:T(8,128)(2,1)S(1)}, bf16[1152,128]{1,0:T(8,128)(2,1)S(1)}, u32[]{:S(2)}, u32[]{:S(2)}) collective-permute-start(bf16[1152,128]{1,0:T(8,128)(2,1)S(1)} %shard_map.133), channel_id=1, source_target_pairs={{0,1},{1,0},{2,3},{3,2},{4,5},{5,4},{6,7},{7,6},{8,9},{9,8},{10,11... | collective-permute-start | bytes 884744 | tf_op jit(solution)/shard_map/ppermute | solution.py:624
  58.8 2.7 %collective-permute-start.4 = (f32[40,128]{1,0:T(8,128)S(1)}, f32[40,128]{1,0:T(8,128)S(1)}, u32[]{:S(2)}, u32[]{:S(2)}) collective-permute-start(f32[40,128]{1,0:T(8,128)S(1)} %shard_map.137.refs_0_), channel_id=1, source_target_pairs={{0,2},{1,3},{2,0},{3,1},{4,6},{5,7},{6,4},{7,5},{8,10},{9,11},{10,... | collective-permute-start | bytes 61448 | tf_op jit(solution)/shard_map/ppermute | solution.py:624
  61.5 18.8 %copy-start.6 = (bf16[2,64,64]{2,1,0:T(8,128)(2,1)S(1)}, bf16[2,64,64]{2,1,0:T(8,128)(2,1)}, u32[]{:S(2)}) copy-start(bf16[2,64,64]{2,1,0:T(8,128)(2,1)} %constant.11.clone.sel_ref) | copy-start | bytes 49156
  76.4 5.5 %collective-permute-start.5 = (bf16[32,40,128]{2,1,0:T(8,128)(2,1)S(1)}, bf16[32,40,128]{2,1,0:T(8,128)(2,1)S(1)}, u32[]{:S(2)}, u32[]{:S(2)}) collective-permute-start(bf16[32,40,128]{2,1,0:T(8,128)(2,1)S(1)} %all_to_all.17.own_ref), channel_id=1, source_target_pairs={{0,1},{1,0},{2,3},{3,2},{4,5},{5,4},{6,7},{7,6},{8,9},{9,8},{10,11... | collective-permute-start | bytes 983048 | tf_op jit(solution)/shard_map/ppermute | solution.py:624

commit v8 on v7

--- a/solution.py
+++ b/solution.py
@@ -20,8 +20,8 @@
 SLOT_ONE = UNIT + STRIP
 HALF = 9 * CH
 CHUNK = 36
-SLOT_TWO = 80
-SLOT_THREE = 40
+SLOT_TWO = 40
+SLOT_THREE = 80
 VMEM_BYTES = 48 * 1024 * 1024
 
 
@@ -168,7 +168,7 @@
 
 
 def interior_kernel(
-    in_ref, w1_ref, w2_ref, own_ref, away_ref, sent, acc, done, w1t, w2t, f2, g2, wide
+    _fill, _plan, _select, in_ref, w1_ref, w2_ref, own_ref, away_ref, sent, acc, done, w1t, w2t, f2, g2, wide
 ):
     band, group = here()
     strip, _ = unit_of(band)
@@ -532,13 +532,11 @@
     pass
 
 
-def share_kernel(own_ref, other_ref, line_ref, tail_ref, sent, out_ref, total):
+def share_kernel(own_ref, other_ref, line_ref, out_ref, total):
     total[...] = own_ref[...] + other_ref[...].astype(F32) + line_ref[...]
     for i in range(BANDS):
-        start = 0 if i == 0 else 24 if i == BANDS - 1 else 48
-        parts = [total[CHUNK * i : CHUNK * i + CHUNK, :], sent[i * 16 : i * 16 + 16, :], tail_ref[start : start + 24, :]]
-        parts.append(jnp.zeros((4, CH), F32))
-        out_ref[i] = jnp.concatenate(parts, axis=0).astype(BF)
+        rows = [total[CHUNK * i : CHUNK * i + CHUNK, :], jnp.zeros((SLOT_TWO - CHUNK, CH), F32)]
+        out_ref[i] = jnp.concatenate(rows, axis=0).astype(BF)
 
 
 def order_selector():
@@ -551,16 +549,23 @@
 
 
 def reduce_kernel(in_ref, out_ref):
-    total = in_ref[0, 0:48, :].astype(F32)
+    total = in_ref[0].astype(F32)
     for i in range(1, BANDS):
-        total = total + in_ref[i, 0:48, :].astype(F32)
-    out_ref[...] = total[0:SLOT_THREE]
-
-
-def spread_kernel(factor, own_ref, other_ref, out_ref):
-    total = ((own_ref[...] + other_ref[...]) * factor).astype(BF)
+        total = total + in_ref[i].astype(F32)
+    out_ref[...] = total
+
+
+def spread_kernel(factor, _order, own_ref, other_ref, tail_ref, sent, out_ref):
+    total = (own_ref[...] + other_ref[...]) * factor
     for i in range(BANDS):
-        out_ref[i] = total
+        start = 0 if i == 0 else 24 if i == BANDS - 1 else 48
+        parts = [total, sent[i * 16 : i * 16 + 16, :], tail_ref[start : start + 24, :]]
+        out_ref[i] = jnp.concatenate(parts, axis=0).astype(BF)
+
+
+def sums_kernel(in_ref, out_ref):
+    for i in range(BANDS):
+        out_ref[i] = in_ref[i, 0:48, :].astype(F32)[0:SLOT_TWO].astype(BF)
 
 
 def unpack_kernel(own_ref, other_ref, first_ref, second_ref):
@@ -576,11 +581,11 @@
 def grad_kernel(fn_ref, rot_ref, sel_ref, in_ref, out_ref, wide, total):
     band, group = here()
     for i in range(BANDS):
-        wide[i * 48 : i * 48 + 48, :] = in_ref[i, 32:SLOT_TWO, :].astype(F32)
+        wide[i * 48 : i * 48 + 48, :] = in_ref[i, 32:SLOT_THREE, :].astype(F32)
     for face in range(3):
         for row in range(2):
             for q in range(8):
-                piece = wide[pl.ds((4 + face) * 48 + 4 + q * 2 + row, 8, stride=144), :]
+                piece = wide[pl.ds((4 + face) * 48 + 8 + q * 2 + row, 8, stride=144), :]
                 total[row, face, pl.ds(q, 8, stride=8), :] = piece
     tiles = [wide[pl.ds(pl.multiple_of(src * 48, 16), 48), :] for src in (band, BANDS - 1 - band)]
     outer = (band == 0) | (band == BANDS - 1)
@@ -593,7 +598,7 @@
                 for row in range(2):
                     for depth in range(2):
                         column = depth if side == 0 else 63 - depth
-                        k, m = [20 + ((pos * 2 + side) * 2 + depth) * 3 + face for pos in (row, 1 - row)]
+                        k, m = [24 + ((pos * 2 + side) * 2 + depth) * 3 + face for pos in (row, 1 - row)]
                         extra = jnp.where(flip, tiles[1][m : m + 1, :], tiles[0][k : k + 1, :])
                         total[row, face, column : column + 1, :] += extra
 
@@ -606,12 +611,12 @@
         for face in range(3):
             order = sel_ref[is_mirrored(fn_ref, rot_ref, 3 * group + face, half)]
             for depth in range(2):
-                halves = [wide[pl.ds(20 + (pos * 2 + depth) * 3 + face, BANDS, stride=48), :] for pos in range(2)]
+                halves = [wide[pl.ds(24 + (pos * 2 + depth) * 3 + face, BANDS, stride=48), :] for pos in range(2)]
                 extra = mm(order, jnp.concatenate(halves, axis=0).astype(BF))
                 total[depth ^ half, face] += jnp.where(inner, extra, 0.0)
                 for side in range(2):
                     for col in range(2):
-                        k = 20 + ((side * 3 + face) * 2 + depth) * 2 + col
+                        k = 24 + ((side * 3 + face) * 2 + depth) * 2 + col
                         column = 63 - col if side else col
                         total[depth ^ half, face, column : column + 1, :] += patches[k : k + 1, :]
 
@@ -653,6 +658,7 @@
         in_smem,
     )
     lines = (lines, *[swapped(lines, step) for step in (1, 2, 3)])
+    tables = (corner_fill.T, jnp.asarray(plan), jnp.asarray(select, F32))
     share = jax.ShapeDtypeStruct((HALF, CH), F32)
     own, away, sent = call(
         interior_kernel,
@@ -666,7 +672,7 @@
             pltpu.VMEM((768, CH), F32),
             pltpu.VMEM((BANDS * UNIT, CH), F32),
         ],
-        (strips, first_weight, second_weight),
+        (*tables, strips, first_weight, second_weight),
     )
     away = call(after_kernel, jax.ShapeDtypeStruct((HALF, CH), BF), [], (away, *lines[1:]), dict.fromkeys((0, 1, 2, 3, "o0"), "a"), {0: 0})
     other = swapped(away, 1)
@@ -688,36 +694,38 @@
             pltpu.VMEM((5, 64, CH), BF),
             pltpu.VMEM((4, 64, CH), F32),
         ],
-        (*seams, corner_fill.T, jnp.asarray(plan), jnp.asarray(select, F32), *lines, first_weight, second_weight),
+        (*seams, *tables, *lines, first_weight, second_weight),
     )
     slots = call(
         share_kernel,
         jax.ShapeDtypeStruct((BANDS, SLOT_TWO, CH), BF),
         [pltpu.VMEM((HALF, CH), F32)],
-        (own, other, line, tails, sent),
+        (own, other, line),
     )
     slots = lax.all_to_all(slots, "tile", 0, 0, tiled=True)
-    part = call(reduce_kernel, jax.ShapeDtypeStruct((SLOT_THREE, CH), F32), [], (slots,))
+    order = jnp.asarray(order_selector(), BF)
+    part = call(reduce_kernel, jax.ShapeDtypeStruct((SLOT_TWO, CH), F32), [], (slots,))
     reduced = call(
         lambda *refs: spread_kernel(factor, *refs),
         jax.ShapeDtypeStruct((BANDS, SLOT_THREE, CH), BF),
         [],
-        (part, swapped(part, 2)),
+        (order, part, swapped(part, 2), tails, sent),
     )
     reduced = lax.all_to_all(reduced, "tile", 0, 0, tiled=True)
-    swap = swapped(reduced, 1)
+    sums = call(sums_kernel, jax.ShapeDtypeStruct((BANDS, SLOT_TWO, CH), BF), [], (reduced,))
+    swap = swapped(sums, 1)
     grad_in = call(
         grad_kernel,
         jax.ShapeDtypeStruct((3, 2, SPAN, CH), BF),
         [pltpu.VMEM((BANDS * 48, CH), F32), pltpu.VMEM((2, 3, SPAN, CH), F32)],
-        (*seams, jnp.asarray(order_selector(), BF), slots),
+        (*seams, order, reduced),
         in_smem,
     )
     first, second = call(
         unpack_kernel,
         [jax.ShapeDtypeStruct((1152, CH), F32), jax.ShapeDtypeStruct((1152, CH), F32)],
         [],
-        (reduced, swap),
+        (sums, swap),
     )
     return grad_in, first.reshape(3, 3, CH, CH), second.reshape(3, 3, CH, CH)
 

time: 83.4 us -> 81.2 us (0.974)
  blocking collectives: 58.6 us -> 56.6 us
    all_to_all x1, blocking collectives: 17.1 us -> 14.6 us  [body(): slots = lax.all_to_all(slots, 'tile', 0, 0, tiled=True)]
    pallas_call x10 -> x11, Pallas kernels: 10.6 us -> 10.7 us  [call(): pl.pallas_call(kernel, out_shape=outs, in_specs=[pl.BlockSpec(memory_spac...]
where the time goes in v8:
time: 81.2 us; the launch traced here: 81 us
  blocking collectives  56.6 us (70%)
  Pallas kernels  10.7 us (13%)
  starting transfers between devices  8.94 us (11%)
  waiting for transfers between devices  3.96 us (5%)
    all_to_all x1, blocking collectives, body(): strips = lax.all_to_all(slots, 'tile', 0, 0, tiled=True)  26.7 us
    all_to_all x1, blocking collectives, body(): reduced = lax.all_to_all(reduced, 'tile', 0, 0, tiled=True)  15.3 us
    all_to_all x1, blocking collectives, body(): slots = lax.all_to_all(slots, 'tile', 0, 0, tiled=True)  14.6 us
    pallas_call x11, Pallas kernels, call(): pl.pallas_call(kernel, out_shape=outs, in_specs=[pl.BlockSpec(memory_spac...  10.7 us
    ppermute x6, starting transfers between devices, swapped(): return lax.ppermute(value, 'sub', [(i, i ^ step) for i in range(4)])  8.94 us
    ppermute x6, waiting for transfers between devices, swapped(): return lax.ppermute(value, 'sub', [(i, i ^ step) for i in range(4)])  3.96 us
  transfers between devices with their start and end apart: 6, of which 2 were waited for; matrix products, arithmetic and copies ran while one was open for 0% of the time, Pallas kernels for 9%

profile of v8, /device:TPU:1, one launch (start us, length us, event | category | flops | bytes accessed | tf_op | source)
XLA Modules:
  0.0 81.0 jit_solution(12655175644616525746)
XLA Ops:
  0.6 1.2 %shard_map.130 = bf16[32,120,128]{2,1,0:T(8,128)(2,1)S(1)} custom-call(bf16[3,2,64,128]{3,2,1,0:T(8,128)(2,1)} %f_hbm.1, bf16[3,2,64,128]{3,2,1,0:T(8,128)(2,1)} %g_hbm.1, s32[4,12]{1,0:T(4,128)} %bitcast.5, s32[4,12]{1,0:T(4,128)} %bitcast.9), custom_call_target="tpu_custom_call" | custom-call | tf_op jit(solution)/shard_map/pallas_call | solution.py:41
  1.8 0.0 copy-start.2
  1.8 0.0 copy-start.6
  1.8 0.0 copy-start.7
  1.8 26.7 %all_to_all.15.in_ref = bf16[32,120,128]{2,1,0:T(8,128)(2,1)S(1)} all-to-all(bf16[32,120,128]{2,1,0:T(8,128)(2,1)S(1)} %shard_map.130), channel_id=1, replica_groups=mesh['tile'=32,'sub'=4] {'tile'}, dimensions={0} | all-to-all | bytes 1966080 | tf_op jit(solution)/shard_map/all_to_all | solution.py:652
  28.5 0.0 copy-done.2
  28.5 0.0 copy-done.6
  28.5 0.0 copy-done.7
  28.5 0.0 copy-start
  28.5 0.0 copy-start.1
  28.6 0.0 copy-start.3
  28.6 0.0 copy-start.5
  28.6 0.0 copy-start.8
  28.6 0.9 %shard_map.132.own_ref = bf16[6,48,128]{2,1,0:T(8,128)(2,1)S(1)} custom-call(s32[4,12]{1,0:T(4,128)S(1)} %bitcast.6, s32[4,12]{1,0:T(4,128)S(1)} %bitcast.10, bf16[2,288,432]{2,1,0:T(8,128)(2,1)S(1)} %copy-done.2, bf16[32,120,128]{2,1,0:T(8,128)(2,1)S(1)} %all_to_all.15.in_ref), custom_call_target="tpu_custom_call" | custom-call | tf_op jit(solution)/shard_map/pallas_call | solution.py:41
  29.5 2.8 %collective-permute-start = (bf16[6,48,128]{2,1,0:T(8,128)(2,1)S(1)}, bf16[6,48,128]{2,1,0:T(8,128)(2,1)S(1)}, u32[]{:S(2)}, u32[]{:S(2)}) collective-permute-start(bf16[6,48,128]{2,1,0:T(8,128)(2,1)S(1)} %shard_map.132.own_ref), channel_id=1, source_target_pairs={{0,1},{1,0},{2,3},{3,2},{4,5},{5,4},{6,7},{7,6},{8,9},{9,8},{10,11... | collective-permute-start | bytes 221192 | tf_op jit(solution)/shard_map/ppermute | solution.py:629
  32.3 0.8 collective-permute-start.1
  33.1 1.0 %collective-permute-start.2 = (bf16[6,48,128]{2,1,0:T(8,128)(2,1)S(1)}, bf16[6,48,128]{2,1,0:T(8,128)(2,1)S(1)}, u32[]{:S(2)}, u32[]{:S(2)}) collective-permute-start(bf16[6,48,128]{2,1,0:T(8,128)(2,1)S(1)} %shard_map.132.own_ref), channel_id=1, source_target_pairs={{0,3},{1,2},{2,1},{3,0},{4,7},{5,6},{6,5},{7,4},{8,11},{9,10},{10,... | collective-permute-start | bytes 221192 | tf_op jit(solution)/shard_map/ppermute | solution.py:629
  34.0 0.0 copy-done
  34.1 0.0 copy-done.1
  34.1 0.0 copy-done.3
  34.1 0.0 copy-done.5
  34.1 0.0 copy-done.8
  34.1 2.2 %shard_map.131 = (f32[1152,128]{1,0:T(8,128)S(1)}, bf16[1152,128]{1,0:T(8,128)(2,1)S(1)}, f32[512,128]{1,0:T(8,128)S(1)}) custom-call(s32[4,12]{1,0:T(4,128)S(1)} %bitcast.13, s32[48,8]{1,0:T(8,128)S(1)} %copy-done.5, f32[72,64]{1,0:T(8,128)S(1)} %copy-done.3, bf16[32,120,128]{2,1,0:T(8,128)(2,1)S(1)} %all_to_all.15.in_ref, ...), custom_call_target="tpu_custom_call" | custom-call | tf_op jit(solution)/shard_map/pallas_call | solution.py:41
  36.3 0.0 collective-permute-done.refs_1_.one_ref
  36.3 0.0 collective-permute-done.1.refs_2_.two_ref
  36.3 1.6 %collective-permute-done.2.refs_3_.three_ref = bf16[6,48,128]{2,1,0:T(8,128)(2,1)S(1)} collective-permute-done((bf16[6,48,128]{2,1,0:T(8,128)(2,1)S(1)}, bf16[6,48,128]{2,1,0:T(8,128)(2,1)S(1)}, u32[]{:S(2)}, u32[]{:S(2)}) %collective-permute-start.2) | collective-permute-done | bytes 73760 | tf_op jit(solution)/shard_map/ppermute | solution.py:629
  37.9 0.2 collective-permute-start.3
  38.1 3.3 %shard_map.134 = (f32[1152,128]{1,0:T(8,128)S(1)}, f32[72,128]{1,0:T(8,128)S(1)}) custom-call(s32[4,12]{1,0:T(4,128)S(1)} %bitcast.7, s32[4,12]{1,0:T(4,128)S(1)} %bitcast.11, s32[4,12]{1,0:T(4,128)S(1)} %bitcast.14, s32[48,8]{1,0:T(8,128)S(1)} %copy-done.5, f32[72,64]{1,0:T(8,128)S(1)} %copy-done.3, bf16[6,48,128]{2,1,0:T(8,128)(2,1)S(1)} %shard_map.132.own_ref, ...), custom_call_target="tpu_custom_call" | custom-call | tf_op jit(solution)/shard_map/pallas_call | solution.py:41
  41.5 0.0 collective-permute-done.3.other_ref
  41.5 0.2 shard_map.135
  41.7 14.6 %all_to_all.16.in_ref = bf16[32,40,128]{2,1,0:T(8,128)(2,1)S(1)} all-to-all(bf16[32,40,128]{2,1,0:T(8,128)(2,1)S(1)} %shard_map.135), channel_id=1, replica_groups=mesh['tile'=32,'sub'=4] {'tile'}, dimensions={0} | all-to-all | bytes 655360 | tf_op jit(solution)/shard_map/all_to_all | solution.py:705
  56.2 0.0 copy-start.4
  56.2 0.1 shard_map.136.refs_1_
  56.3 0.4 collective-permute-start.4
  56.6 2.4 %collective-permute-done.4.refs_2_ = f32[40,128]{1,0:T(8,128)S(1)} collective-permute-done((f32[40,128]{1,0:T(8,128)S(1)}, f32[40,128]{1,0:T(8,128)S(1)}, u32[]{:S(2)}, u32[]{:S(2)}) %collective-permute-start.4) | collective-permute-done | bytes 20512 | tf_op jit(solution)/shard_map/ppermute | solution.py:629
  59.0 0.0 copy-done.4
  59.1 15.3 %all_to_all.17.in_ref = bf16[32,80,128]{2,1,0:T(8,128)(2,1)S(1)} all-to-all(bf16[32,80,128]{2,1,0:T(8,128)(2,1)S(1)} %shard_map.137), channel_id=1, replica_groups=mesh['tile'=32,'sub'=4] {'tile'}, dimensions={0} | all-to-all | bytes 1310720 | tf_op jit(solution)/shard_map/all_to_all | solution.py:714
  74.4 0.1 shard_map.139.own_ref
  74.4 3.9 %collective-permute-start.5 = (bf16[32,40,128]{2,1,0:T(8,128)(2,1)S(1)}, bf16[32,40,128]{2,1,0:T(8,128)(2,1)S(1)}, u32[]{:S(2)}, u32[]{:S(2)}) collective-permute-start(bf16[32,40,128]{2,1,0:T(8,128)(2,1)S(1)} %shard_map.139.own_ref), channel_id=1, source_target_pairs={{0,1},{1,0},{2,3},{3,2},{4,5},{5,4},{6,7},{7,6},{8,9},{9,8},{10,11... | collective-permute-start | bytes 983048 | tf_op jit(solution)/shard_map/ppermute | solution.py:629
  78.3 1.6 %shard_map.138 = bf16[3,2,64,128]{3,2,1,0:T(8,128)(2,1)} custom-call(s32[4,12]{1,0:T(4,128)S(1)} %bitcast.8, s32[4,12]{1,0:T(4,128)S(1)} %bitcast.12, bf16[2,64,64]{2,1,0:T(8,128)(2,1)S(1)} %copy-done.4, bf16[32,80,128]{2,1,0:T(8,128)(2,1)S(1)} %all_to_all.17.in_ref), custom_call_target="tpu_custom_call" | custom-call | tf_op jit(solution)/shard_map/pallas_call | solution.py:41
  79.9 0.0 collective-permute-done.5.other_ref
  79.9 1.1 %shard_map.140 = (f32[1152,128]{1,0:T(8,128)}, f32[1152,128]{1,0:T(8,128)}) custom-call(bf16[32,40,128]{2,1,0:T(8,128)(2,1)S(1)} %shard_map.139.own_ref, bf16[32,40,128]{2,1,0:T(8,128)(2,1)S(1)} %collective-permute-done.5.other_ref), custom_call_target="tpu_custom_call" | custom-call | tf_op jit(solution)/shard_map/pallas_call | solution.py:41
  (2 shorter events, 0.1 us)
Async XLA Ops:
  1.8 26.7 %copy-start.2 = (bf16[2,288,432]{2,1,0:T(8,128)(2,1)S(1)}, bf16[2,288,432]{2,1,0:T(8,128)(2,1)}, u32[]{:S(2)}) copy-start(bf16[2,288,432]{2,1,0:T(8,128)(2,1)} %constant.8.clone.sel_ref) | copy-start | bytes 1492996
  1.8 26.7 %copy-start.6 = (s32[12,4]{0,1:T(4,128)S(1)}, s32[12,4]{0,1:T(4,128)}, u32[]{:S(2)}) copy-start(s32[12,4]{0,1:T(4,128)} %param.15) | copy-start | bytes 580
  1.8 26.7 %copy-start.7 = (s32[12,4]{0,1:T(4,128)S(1)}, s32[12,4]{0,1:T(4,128)}, u32[]{:S(2)}) copy-start(s32[12,4]{0,1:T(4,128)} %param.16) | copy-start | bytes 580
  28.5 5.5 %copy-start = (bf16[3,3,128,128]{3,2,1,0:T(8,128)(2,1)S(1)}, bf16[3,3,128,128]{3,2,1,0:T(8,128)(2,1)}, u32[]{:S(2)}) copy-start(bf16[3,3,128,128]{3,2,1,0:T(8,128)(2,1)} %w1_ref.3) | copy-start | bytes 884740
  28.5 5.5 %copy-start.1 = (bf16[3,3,128,128]{3,2,1,0:T(8,128)(2,1)S(1)}, bf16[3,3,128,128]{3,2,1,0:T(8,128)(2,1)}, u32[]{:S(2)}) copy-start(bf16[3,3,128,128]{3,2,1,0:T(8,128)(2,1)} %w2_ref.3) | copy-start | bytes 884740
  28.6 5.5 %copy-start.3 = (f32[72,64]{1,0:T(8,128)S(1)}, f32[72,64]{1,0:T(8,128)}, u32[]{:S(2)}) copy-start(f32[72,64]{1,0:T(8,128)} %constant.10.clone._select.sel_ref) | copy-start | bytes 55300
  28.6 5.5 %copy-start.5 = (s32[48,8]{1,0:T(8,128)S(1)}, s32[48,8]{1,0:T(8,128)}, u32[]{:S(2)}) copy-start(s32[48,8]{1,0:T(8,128)} %constant.9.clone._plan.plan_ref) | copy-start | bytes 4612
  28.6 5.5 %copy-start.8 = (s32[12,4]{0,1:T(4,128)S(1)}, s32[12,4]{0,1:T(4,128)}, u32[]{:S(2)}) copy-start(s32[12,4]{0,1:T(4,128)} %param.17) | copy-start | bytes 580
  29.5 6.8 %collective-permute-start = (bf16[6,48,128]{2,1,0:T(8,128)(2,1)S(1)}, bf16[6,48,128]{2,1,0:T(8,128)(2,1)S(1)}, u32[]{:S(2)}, u32[]{:S(2)}) collective-permute-start(bf16[6,48,128]{2,1,0:T(8,128)(2,1)S(1)} %shard_map.132.own_ref), channel_id=1, source_target_pairs={{0,1},{1,0},{2,3},{3,2},{4,5},{5,4},{6,7},{7,6},{8,9},{9,8},{10,11... | collective-permute-start | bytes 221192 | tf_op jit(solution)/shard_map/ppermute | solution.py:629
  32.3 4.0 %collective-permute-start.1 = (bf16[6,48,128]{2,1,0:T(8,128)(2,1)S(1)}, bf16[6,48,128]{2,1,0:T(8,128)(2,1)S(1)}, u32[]{:S(2)}, u32[]{:S(2)}) collective-permute-start(bf16[6,48,128]{2,1,0:T(8,128)(2,1)S(1)} %shard_map.132.own_ref), channel_id=1, source_target_pairs={{0,2},{1,3},{2,0},{3,1},{4,6},{5,7},{6,4},{7,5},{8,10},{9,11},{10,... | collective-permute-start | bytes 221192 | tf_op jit(solution)/shard_map/ppermute | solution.py:629
  33.1 4.8 %collective-permute-start.2 = (bf16[6,48,128]{2,1,0:T(8,128)(2,1)S(1)}, bf16[6,48,128]{2,1,0:T(8,128)(2,1)S(1)}, u32[]{:S(2)}, u32[]{:S(2)}) collective-permute-start(bf16[6,48,128]{2,1,0:T(8,128)(2,1)S(1)} %shard_map.132.own_ref), channel_id=1, source_target_pairs={{0,3},{1,2},{2,1},{3,0},{4,7},{5,6},{6,5},{7,4},{8,11},{9,10},{10,... | collective-permute-start | bytes 221192 | tf_op jit(solution)/shard_map/ppermute | solution.py:629
  37.9 3.6 %collective-permute-start.3 = (bf16[1152,128]{1,0:T(8,128)(2,1)S(1)}, bf16[1152,128]{1,0:T(8,128)(2,1)S(1)}, u32[]{:S(2)}, u32[]{:S(2)}) collective-permute-start(bf16[1152,128]{1,0:T(8,128)(2,1)S(1)} %shard_map.133), channel_id=1, source_target_pairs={{0,1},{1,0},{2,3},{3,2},{4,5},{5,4},{6,7},{7,6},{8,9},{9,8},{10,11... | collective-permute-start | bytes 884744 | tf_op jit(solution)/shard_map/ppermute | solution.py:629
  56.2 2.8 %copy-start.4 = (bf16[2,64,64]{2,1,0:T(8,128)(2,1)S(1)}, bf16[2,64,64]{2,1,0:T(8,128)(2,1)}, u32[]{:S(2)}) copy-start(bf16[2,64,64]{2,1,0:T(8,128)(2,1)} %constant.11.clone.refs_0_.sel_ref) | copy-start | bytes 49156
  56.3 2.7 %collective-permute-start.4 = (f32[40,128]{1,0:T(8,128)S(1)}, f32[40,128]{1,0:T(8,128)S(1)}, u32[]{:S(2)}, u32[]{:S(2)}) collective-permute-start(f32[40,128]{1,0:T(8,128)S(1)} %shard_map.136.refs_1_), channel_id=1, source_target_pairs={{0,2},{1,3},{2,0},{3,1},{4,6},{5,7},{6,4},{7,5},{8,10},{9,11},{10,... | collective-permute-start | bytes 61448 | tf_op jit(solution)/shard_map/ppermute | solution.py:629
  74.4 5.4 %collective-permute-start.5 = (bf16[32,40,128]{2,1,0:T(8,128)(2,1)S(1)}, bf16[32,40,128]{2,1,0:T(8,128)(2,1)S(1)}, u32[]{:S(2)}, u32[]{:S(2)}) collective-permute-start(bf16[32,40,128]{2,1,0:T(8,128)(2,1)S(1)} %shard_map.139.own_ref), channel_id=1, source_target_pairs={{0,1},{1,0},{2,3},{3,2},{4,5},{5,4},{6,7},{7,6},{8,9},{9,8},{10,11... | collective-permute-start | bytes 983048 | tf_op jit(solution)/shard_map/ppermute | solution.py:629

commit v9 on v8

--- a/solution.py
+++ b/solution.py
@@ -140,14 +140,20 @@
         outer = (source == 0) | (source == BANDS - 1)
         pieces.append(jnp.where(outer, in_ref[source, 0:ENDS, :], in_ref[source, UNIT : UNIT + ENDS, :]).astype(F32))
     pieces = jnp.concatenate(pieces, axis=0).astype(BF)
-    place = lax.broadcasted_iota(I32, (WINDOW * ENDS, 1), 0)
-    place = place - 12 * ((place * 171) >> 11)
-    flip = jnp.zeros((WINDOW * ENDS, 1), I32)
-    for side in range(4):
-        for face in range(3):
-            flip = jnp.where(place == side * 3 + face, is_mirrored(fn_ref, rot_ref, 3 * group + face, side), flip)
-    flip = jnp.broadcast_to(flip.astype(F32), sel_ref.shape[1:]).astype(BF)
-    picked = mm(sel_ref[0] * (1 - flip) + sel_ref[1] * flip, pieces).astype(BF)
+    place = lax.broadcasted_iota(I32, (24, CH), 0)
+    place = jnp.where(place < 12, place, place - 12)
+    flip = jnp.zeros((24, CH), I32)
+    lane = lax.broadcasted_iota(I32, (4, 12), 1)
+    rot = rot_ref[...]
+    partner = 4 * fn_ref[...] + (rot & 3)
+    table = jnp.where(4 * lane + lax.broadcasted_iota(I32, (4, 12), 0) > partner, rot >> 2, 0)
+    for face in range(3):
+        values = jnp.sum(jnp.where(lane == 3 * group + face, table, 0), axis=1, keepdims=True)
+        for side in range(4):
+            flip = jnp.where(place == side * 3 + face, jnp.broadcast_to(values[side : side + 1], (24, CH)), flip)
+    flip = jnp.concatenate([flip.astype(F32)] * (WINDOW * ENDS // 24), axis=0).astype(BF)
+    flip = jnp.concatenate([flip] * 4, axis=1)[:, 0 : sel_ref.shape[2]] > 0.5
+    picked = mm(jnp.where(flip, sel_ref[1], sel_ref[0]), pieces).astype(BF)
     for j in range(WINDOW):
         out_ref[j] = picked[j * ENDS : (j + 1) * ENDS]
 
@@ -594,7 +600,7 @@
     def _():
         for side in range(2):
             for face in range(3):
-                flip = is_mirrored(fn_ref, rot_ref, 3 * group + face, 2 + side) == 1
+                flip = mirrored_in(fn_ref, rot_ref, 3 * group + face, 2 + side) == 1
                 for row in range(2):
                     for depth in range(2):
                         column = depth if side == 0 else 63 - depth
@@ -609,7 +615,8 @@
         place = lax.broadcasted_iota(I32, (SPAN, CH), 0)
         inner = (place >= 2) & (place < SPAN - 2)
         for face in range(3):
-            order = sel_ref[is_mirrored(fn_ref, rot_ref, 3 * group + face, half)]
+            pair = [mirrored_in(fn_ref, rot_ref, 3 * group + face, side) for side in range(2)]
+            order = sel_ref[jnp.where(band == 0, pair[0], pair[1])]
             for depth in range(2):
                 halves = [wide[pl.ds(24 + (pos * 2 + depth) * 3 + face, BANDS, stride=48), :] for pos in range(2)]
                 extra = mm(order, jnp.concatenate(halves, axis=0).astype(BF))
@@ -632,7 +639,6 @@
 def body(field_in, grad_out, first_weight, second_weight, face_neighbour, seam_rotation, corner_fill):
     factor = (1.0 * 12 * SPAN * SPAN) ** -0.5
     seams = (face_neighbour.T, seam_rotation.T)
-    in_smem = {0: "s", 1: "s"}
     select, plan = tail_plan()
 
     slots = call(
@@ -655,7 +661,6 @@
         jax.ShapeDtypeStruct((WINDOW, ENDS, CH), BF),
         [],
         (*seams, jnp.asarray(line_selector(), BF), strips),
-        in_smem,
     )
     lines = (lines, *[swapped(lines, step) for step in (1, 2, 3)])
     tables = (corner_fill.T, jnp.asarray(plan), jnp.asarray(select, F32))
@@ -719,7 +724,6 @@
         jax.ShapeDtypeStruct((3, 2, SPAN, CH), BF),
         [pltpu.VMEM((BANDS * 48, CH), F32), pltpu.VMEM((2, 3, SPAN, CH), F32)],
         (*seams, order, reduced),
-        in_smem,
     )
     first, second = call(
         unpack_kernel,

time: 81.2 us -> 80.3 us (0.989)
  Pallas kernels: 10.7 us -> 9.57 us
    pallas_call x11, Pallas kernels: 10.7 us -> 9.57 us  [call(): pl.pallas_call(kernel, out_shape=outs, in_specs=[pl.BlockSpec(memory_spac...]
  transfers between devices with their start and end apart: 6 -> 6, of which waited for: 2 -> 3; matrix products, arithmetic and copies ran while one was open for 0% -> 0% of each run, Pallas kernels for 9% -> 8%
where the time goes in v9:
time: 80.3 us; the launch traced here: 80 us
  blocking collectives  56.6 us (70%)
  Pallas kernels  9.57 us (12%)
  starting transfers between devices  8.97 us (11%)
  waiting for transfers between devices  4.08 us (5%)
    all_to_all x1, blocking collectives, body(): strips = lax.all_to_all(slots, 'tile', 0, 0, tiled=True)  26.7 us
    all_to_all x1, blocking collectives, body(): reduced = lax.all_to_all(reduced, 'tile', 0, 0, tiled=True)  15.3 us
    all_to_all x1, blocking collectives, body(): slots = lax.all_to_all(slots, 'tile', 0, 0, tiled=True)  14.6 us
    pallas_call x11, Pallas kernels, call(): pl.pallas_call(kernel, out_shape=outs, in_specs=[pl.BlockSpec(memory_spac...  9.57 us
    ppermute x6, starting transfers between devices, swapped(): return lax.ppermute(value, 'sub', [(i, i ^ step) for i in range(4)])  8.97 us
    ppermute x6, waiting for transfers between devices, swapped(): return lax.ppermute(value, 'sub', [(i, i ^ step) for i in range(4)])  4.08 us
  transfers between devices with their start and end apart: 6, of which 3 were waited for; matrix products, arithmetic and copies ran while one was open for 0% of the time, Pallas kernels for 8%

profile of v9, /device:TPU:1, one launch (start us, length us, event | category | flops | bytes accessed | tf_op | source)
XLA Modules:
  0.0 80.0 jit_solution(14616404276358869926)
XLA Ops:
  0.6 1.2 %shard_map.130 = bf16[32,120,128]{2,1,0:T(8,128)(2,1)S(1)} custom-call(bf16[3,2,64,128]{3,2,1,0:T(8,128)(2,1)} %f_hbm.1, bf16[3,2,64,128]{3,2,1,0:T(8,128)(2,1)} %g_hbm.1, s32[4,12]{1,0:T(4,128)} %bitcast.5, s32[4,12]{1,0:T(4,128)} %bitcast.9), custom_call_target="tpu_custom_call" | custom-call | tf_op jit(solution)/shard_map/pallas_call | solution.py:41
  1.8 0.0 copy-start.2
  1.8 0.0 copy-start.6
  1.8 0.0 copy-start.7
  1.8 26.7 %all_to_all.15.in_ref = bf16[32,120,128]{2,1,0:T(8,128)(2,1)S(1)} all-to-all(bf16[32,120,128]{2,1,0:T(8,128)(2,1)S(1)} %shard_map.130), channel_id=1, replica_groups=mesh['tile'=32,'sub'=4] {'tile'}, dimensions={0} | all-to-all | bytes 1966080 | tf_op jit(solution)/shard_map/all_to_all | solution.py:658
  28.5 0.0 copy-done.2
  28.5 0.0 copy-done.6
  28.5 0.0 copy-done.7
  28.5 0.0 copy-start
  28.5 0.0 copy-start.1
  28.6 0.0 copy-start.3
  28.6 0.0 copy-start.5
  28.6 0.0 copy-start.8
  28.6 0.3 shard_map.132.own_ref
  28.9 2.8 %collective-permute-start = (bf16[6,48,128]{2,1,0:T(8,128)(2,1)S(1)}, bf16[6,48,128]{2,1,0:T(8,128)(2,1)S(1)}, u32[]{:S(2)}, u32[]{:S(2)}) collective-permute-start(bf16[6,48,128]{2,1,0:T(8,128)(2,1)S(1)} %shard_map.132.own_ref), channel_id=1, source_target_pairs={{0,1},{1,0},{2,3},{3,2},{4,5},{5,4},{6,7},{7,6},{8,9},{9,8},{10,11... | collective-permute-start | bytes 221192 | tf_op jit(solution)/shard_map/ppermute | solution.py:636
  31.7 0.8 collective-permute-start.1
  32.5 1.0 %collective-permute-start.2 = (bf16[6,48,128]{2,1,0:T(8,128)(2,1)S(1)}, bf16[6,48,128]{2,1,0:T(8,128)(2,1)S(1)}, u32[]{:S(2)}, u32[]{:S(2)}) collective-permute-start(bf16[6,48,128]{2,1,0:T(8,128)(2,1)S(1)} %shard_map.132.own_ref), channel_id=1, source_target_pairs={{0,3},{1,2},{2,1},{3,0},{4,7},{5,6},{6,5},{7,4},{8,11},{9,10},{10,... | collective-permute-start | bytes 221192 | tf_op jit(solution)/shard_map/ppermute | solution.py:636
  33.4 0.0 copy-done
  33.4 0.0 copy-done.1
  33.4 0.0 copy-done.3
  33.4 0.0 copy-done.5
  33.4 0.0 copy-done.8
  33.4 2.2 %shard_map.131 = (f32[1152,128]{1,0:T(8,128)S(1)}, bf16[1152,128]{1,0:T(8,128)(2,1)S(1)}, f32[512,128]{1,0:T(8,128)S(1)}) custom-call(s32[4,12]{1,0:T(4,128)S(1)} %bitcast.13, s32[48,8]{1,0:T(8,128)S(1)} %copy-done.5, f32[72,64]{1,0:T(8,128)S(1)} %copy-done.3, bf16[32,120,128]{2,1,0:T(8,128)(2,1)S(1)} %all_to_all.15.in_ref, ...), custom_call_target="tpu_custom_call" | custom-call | tf_op jit(solution)/shard_map/pallas_call | solution.py:41
  35.7 0.0 collective-permute-done.refs_1_.one_ref
  35.7 0.0 collective-permute-done.1.refs_2_.two_ref
  35.7 1.6 %collective-permute-done.2.refs_3_.three_ref = bf16[6,48,128]{2,1,0:T(8,128)(2,1)S(1)} collective-permute-done((bf16[6,48,128]{2,1,0:T(8,128)(2,1)S(1)}, bf16[6,48,128]{2,1,0:T(8,128)(2,1)S(1)}, u32[]{:S(2)}, u32[]{:S(2)}) %collective-permute-start.2) | collective-permute-done | bytes 73760 | tf_op jit(solution)/shard_map/ppermute | solution.py:636
  37.3 0.2 collective-permute-start.3
  37.5 3.3 %shard_map.134 = (f32[1152,128]{1,0:T(8,128)S(1)}, f32[72,128]{1,0:T(8,128)S(1)}) custom-call(s32[4,12]{1,0:T(4,128)S(1)} %bitcast.7, s32[4,12]{1,0:T(4,128)S(1)} %bitcast.11, s32[4,12]{1,0:T(4,128)S(1)} %bitcast.14, s32[48,8]{1,0:T(8,128)S(1)} %copy-done.5, f32[72,64]{1,0:T(8,128)S(1)} %copy-done.3, bf16[6,48,128]{2,1,0:T(8,128)(2,1)S(1)} %shard_map.132.own_ref, ...), custom_call_target="tpu_custom_call" | custom-call | tf_op jit(solution)/shard_map/pallas_call | solution.py:41
  40.8 0.0 collective-permute-done.3.other_ref
  40.9 0.2 shard_map.135
  41.0 14.6 %all_to_all.16.in_ref = bf16[32,40,128]{2,1,0:T(8,128)(2,1)S(1)} all-to-all(bf16[32,40,128]{2,1,0:T(8,128)(2,1)S(1)} %shard_map.135), channel_id=1, replica_groups=mesh['tile'=32,'sub'=4] {'tile'}, dimensions={0} | all-to-all | bytes 655360 | tf_op jit(solution)/shard_map/all_to_all | solution.py:710
  55.6 0.0 copy-start.4
  55.6 0.1 shard_map.136.refs_1_
  55.7 0.4 collective-permute-start.4
  56.1 2.3 %collective-permute-done.4.refs_2_ = f32[40,128]{1,0:T(8,128)S(1)} collective-permute-done((f32[40,128]{1,0:T(8,128)S(1)}, f32[40,128]{1,0:T(8,128)S(1)}, u32[]{:S(2)}, u32[]{:S(2)}) %collective-permute-start.4) | collective-permute-done | bytes 20512 | tf_op jit(solution)/shard_map/ppermute | solution.py:636
  58.4 0.0 copy-done.4
  58.4 15.3 %all_to_all.17.in_ref = bf16[32,80,128]{2,1,0:T(8,128)(2,1)S(1)} all-to-all(bf16[32,80,128]{2,1,0:T(8,128)(2,1)S(1)} %shard_map.137), channel_id=1, replica_groups=mesh['tile'=32,'sub'=4] {'tile'}, dimensions={0} | all-to-all | bytes 1310720 | tf_op jit(solution)/shard_map/all_to_all | solution.py:719
  73.7 0.1 shard_map.139.own_ref
  73.8 3.9 %collective-permute-start.5 = (bf16[32,40,128]{2,1,0:T(8,128)(2,1)S(1)}, bf16[32,40,128]{2,1,0:T(8,128)(2,1)S(1)}, u32[]{:S(2)}, u32[]{:S(2)}) collective-permute-start(bf16[32,40,128]{2,1,0:T(8,128)(2,1)S(1)} %shard_map.139.own_ref), channel_id=1, source_target_pairs={{0,1},{1,0},{2,3},{3,2},{4,5},{5,4},{6,7},{7,6},{8,9},{9,8},{10,11... | collective-permute-start | bytes 983048 | tf_op jit(solution)/shard_map/ppermute | solution.py:636
  77.7 1.1 %shard_map.138 = bf16[3,2,64,128]{3,2,1,0:T(8,128)(2,1)} custom-call(s32[4,12]{1,0:T(4,128)S(1)} %bitcast.8, s32[4,12]{1,0:T(4,128)S(1)} %bitcast.12, bf16[2,64,64]{2,1,0:T(8,128)(2,1)S(1)} %copy-done.4, bf16[32,80,128]{2,1,0:T(8,128)(2,1)S(1)} %all_to_all.17.in_ref), custom_call_target="tpu_custom_call" | custom-call | tf_op jit(solution)/shard_map/pallas_call | solution.py:41
  78.8 0.2 collective-permute-done.5.other_ref
  78.9 1.1 %shard_map.140 = (f32[1152,128]{1,0:T(8,128)}, f32[1152,128]{1,0:T(8,128)}) custom-call(bf16[32,40,128]{2,1,0:T(8,128)(2,1)S(1)} %shard_map.139.own_ref, bf16[32,40,128]{2,1,0:T(8,128)(2,1)S(1)} %collective-permute-done.5.other_ref), custom_call_target="tpu_custom_call" | custom-call | tf_op jit(solution)/shard_map/pallas_call | solution.py:41
  (2 shorter events, 0.0 us)
Async XLA Ops:
  1.8 26.7 %copy-start.2 = (bf16[2,288,432]{2,1,0:T(8,128)(2,1)S(1)}, bf16[2,288,432]{2,1,0:T(8,128)(2,1)}, u32[]{:S(2)}) copy-start(bf16[2,288,432]{2,1,0:T(8,128)(2,1)} %constant.8.clone.sel_ref) | copy-start | bytes 1492996
  1.8 26.7 %copy-start.6 = (s32[12,4]{0,1:T(4,128)S(1)}, s32[12,4]{0,1:T(4,128)}, u32[]{:S(2)}) copy-start(s32[12,4]{0,1:T(4,128)} %param.15) | copy-start | bytes 580
  1.8 26.7 %copy-start.7 = (s32[12,4]{0,1:T(4,128)S(1)}, s32[12,4]{0,1:T(4,128)}, u32[]{:S(2)}) copy-start(s32[12,4]{0,1:T(4,128)} %param.16) | copy-start | bytes 580
  28.5 4.9 %copy-start = (bf16[3,3,128,128]{3,2,1,0:T(8,128)(2,1)S(1)}, bf16[3,3,128,128]{3,2,1,0:T(8,128)(2,1)}, u32[]{:S(2)}) copy-start(bf16[3,3,128,128]{3,2,1,0:T(8,128)(2,1)} %w1_ref.3) | copy-start | bytes 884740
  28.5 4.9 %copy-start.1 = (bf16[3,3,128,128]{3,2,1,0:T(8,128)(2,1)S(1)}, bf16[3,3,128,128]{3,2,1,0:T(8,128)(2,1)}, u32[]{:S(2)}) copy-start(bf16[3,3,128,128]{3,2,1,0:T(8,128)(2,1)} %w2_ref.3) | copy-start | bytes 884740
  28.6 4.9 %copy-start.3 = (f32[72,64]{1,0:T(8,128)S(1)}, f32[72,64]{1,0:T(8,128)}, u32[]{:S(2)}) copy-start(f32[72,64]{1,0:T(8,128)} %constant.10.clone._select.sel_ref) | copy-start | bytes 55300
  28.6 4.9 %copy-start.5 = (s32[48,8]{1,0:T(8,128)S(1)}, s32[48,8]{1,0:T(8,128)}, u32[]{:S(2)}) copy-start(s32[48,8]{1,0:T(8,128)} %constant.9.clone._plan.plan_ref) | copy-start | bytes 4612
  28.6 4.9 %copy-start.8 = (s32[12,4]{0,1:T(4,128)S(1)}, s32[12,4]{0,1:T(4,128)}, u32[]{:S(2)}) copy-start(s32[12,4]{0,1:T(4,128)} %param.17) | copy-start | bytes 580
  28.9 6.8 %collective-permute-start = (bf16[6,48,128]{2,1,0:T(8,128)(2,1)S(1)}, bf16[6,48,128]{2,1,0:T(8,128)(2,1)S(1)}, u32[]{:S(2)}, u32[]{:S(2)}) collective-permute-start(bf16[6,48,128]{2,1,0:T(8,128)(2,1)S(1)} %shard_map.132.own_ref), channel_id=1, source_target_pairs={{0,1},{1,0},{2,3},{3,2},{4,5},{5,4},{6,7},{7,6},{8,9},{9,8},{10,11... | collective-permute-start | bytes 221192 | tf_op jit(solution)/shard_map/ppermute | solution.py:636
  31.7 4.0 %collective-permute-start.1 = (bf16[6,48,128]{2,1,0:T(8,128)(2,1)S(1)}, bf16[6,48,128]{2,1,0:T(8,128)(2,1)S(1)}, u32[]{:S(2)}, u32[]{:S(2)}) collective-permute-start(bf16[6,48,128]{2,1,0:T(8,128)(2,1)S(1)} %shard_map.132.own_ref), channel_id=1, source_target_pairs={{0,2},{1,3},{2,0},{3,1},{4,6},{5,7},{6,4},{7,5},{8,10},{9,11},{10,... | collective-permute-start | bytes 221192 | tf_op jit(solution)/shard_map/ppermute | solution.py:636
  32.5 4.8 %collective-permute-start.2 = (bf16[6,48,128]{2,1,0:T(8,128)(2,1)S(1)}, bf16[6,48,128]{2,1,0:T(8,128)(2,1)S(1)}, u32[]{:S(2)}, u32[]{:S(2)}) collective-permute-start(bf16[6,48,128]{2,1,0:T(8,128)(2,1)S(1)} %shard_map.132.own_ref), channel_id=1, source_target_pairs={{0,3},{1,2},{2,1},{3,0},{4,7},{5,6},{6,5},{7,4},{8,11},{9,10},{10,... | collective-permute-start | bytes 221192 | tf_op jit(solution)/shard_map/ppermute | solution.py:636
  37.3 3.6 %collective-permute-start.3 = (bf16[1152,128]{1,0:T(8,128)(2,1)S(1)}, bf16[1152,128]{1,0:T(8,128)(2,1)S(1)}, u32[]{:S(2)}, u32[]{:S(2)}) collective-permute-start(bf16[1152,128]{1,0:T(8,128)(2,1)S(1)} %shard_map.133), channel_id=1, source_target_pairs={{0,1},{1,0},{2,3},{3,2},{4,5},{5,4},{6,7},{7,6},{8,9},{9,8},{10,11... | collective-permute-start | bytes 884744 | tf_op jit(solution)/shard_map/ppermute | solution.py:636
  55.6 2.8 %copy-start.4 = (bf16[2,64,64]{2,1,0:T(8,128)(2,1)S(1)}, bf16[2,64,64]{2,1,0:T(8,128)(2,1)}, u32[]{:S(2)}) copy-start(bf16[2,64,64]{2,1,0:T(8,128)(2,1)} %constant.11.clone.refs_0_.sel_ref) | copy-start | bytes 49156
  55.7 2.7 %collective-permute-start.4 = (f32[40,128]{1,0:T(8,128)S(1)}, f32[40,128]{1,0:T(8,128)S(1)}, u32[]{:S(2)}, u32[]{:S(2)}) collective-permute-start(f32[40,128]{1,0:T(8,128)S(1)} %shard_map.136.refs_1_), channel_id=1, source_target_pairs={{0,2},{1,3},{2,0},{3,1},{4,6},{5,7},{6,4},{7,5},{8,10},{9,11},{10,... | collective-permute-start | bytes 61448 | tf_op jit(solution)/shard_map/ppermute | solution.py:636
  73.8 5.1 %collective-permute-start.5 = (bf16[32,40,128]{2,1,0:T(8,128)(2,1)S(1)}, bf16[32,40,128]{2,1,0:T(8,128)(2,1)S(1)}, u32[]{:S(2)}, u32[]{:S(2)}) collective-permute-start(bf16[32,40,128]{2,1,0:T(8,128)(2,1)S(1)} %shard_map.139.own_ref), channel_id=1, source_target_pairs={{0,1},{1,0},{2,3},{3,2},{4,5},{5,4},{6,7},{7,6},{8,9},{9,8},{10,11... | collective-permute-start | bytes 983048 | tf_op jit(solution)/shard_map/ppermute | solution.py:636

commit v10 on v9

--- a/solution.py
+++ b/solution.py
@@ -495,9 +495,14 @@
     tile = jnp.concatenate([owe[k, pl.ds(pl.multiple_of(group * 16, 16), 16), :] for k in range(4)], axis=0)
     plan = [plan_ref[:, k : k + 1] for k in range(8)]
     flips = [jnp.zeros((48, 1), I32) for _ in range(2)]
-    for which in range(4):
-        for face_index in range(3):
-            value = mirrored_in(fn_ref, rot_ref, 3 * group + face_index, which)
+    table_lane = lax.broadcasted_iota(I32, (4, 12), 1)
+    rotations = rot_ref[...]
+    partners = 4 * fn_ref[...] + (rotations & 3)
+    table = jnp.where(4 * table_lane + lax.broadcasted_iota(I32, (4, 12), 0) > partners, rotations >> 2, 0)
+    for face_index in range(3):
+        values = jnp.sum(jnp.where(table_lane == 3 * group + face_index, table, 0), axis=1, keepdims=True)
+        for which in range(4):
+            value = jnp.broadcast_to(values[which : which + 1], (48, 1))
             for k in range(2):
                 flips[k] = jnp.where(plan[6 + k] == which * 3 + face_index, value, flips[k])
     last = jnp.where(at_last, 1, 0)
@@ -662,7 +667,7 @@
         [],
         (*seams, jnp.asarray(line_selector(), BF), strips),
     )
-    lines = (lines, *[swapped(lines, step) for step in (1, 2, 3)])
+    beyond, beside = swapped(lines, 2), swapped(lines, 1)
     tables = (corner_fill.T, jnp.asarray(plan), jnp.asarray(select, F32))
     share = jax.ShapeDtypeStruct((HALF, CH), F32)
     own, away, sent = call(
@@ -679,6 +684,8 @@
         ],
         (*tables, strips, first_weight, second_weight),
     )
+    beyond = call(after_kernel, jax.ShapeDtypeStruct((WINDOW, ENDS, CH), BF), [], (beyond, own), dict.fromkeys((0, 1, "o0"), "a"), {0: 0})
+    lines = (lines, beside, beyond, swapped(beyond, 1))
     away = call(after_kernel, jax.ShapeDtypeStruct((HALF, CH), BF), [], (away, *lines[1:]), dict.fromkeys((0, 1, 2, 3, "o0"), "a"), {0: 0})
     other = swapped(away, 1)
 

time: 80.3 us -> 79.9 us (level)
  waiting for transfers between devices: 4.08 us -> 2.97 us
  starting transfers between devices: 8.97 us -> 9.9 us
    ppermute x6, waiting for transfers between devices: 4.08 us -> 2.97 us  [swapped(): return lax.ppermute(value, 'sub', [(i, i ^ step) for i in range(4)])]
    ppermute x6, starting transfers between devices: 8.97 us -> 9.9 us  [swapped(): return lax.ppermute(value, 'sub', [(i, i ^ step) for i in range(4)])]
    pallas_call x11 -> x12, Pallas kernels: 9.57 us -> 9.56 us  [call(): pl.pallas_call(kernel, out_shape=outs, in_specs=[pl.BlockSpec(memory_spac...]
where the time goes in v10:
time: 79.9 us; the launch traced here: 79.7 us
  blocking collectives  56.4 us (71%)
  starting transfers between devices  9.9 us (12%)
  Pallas kernels  9.56 us (12%)
  waiting for transfers between devices  2.97 us (4%)
    all_to_all x1, blocking collectives, body(): strips = lax.all_to_all(slots, 'tile', 0, 0, tiled=True)  26.7 us
    all_to_all x1, blocking collectives, body(): reduced = lax.all_to_all(reduced, 'tile', 0, 0, tiled=True)  15.3 us
    all_to_all x1, blocking collectives, body(): slots = lax.all_to_all(slots, 'tile', 0, 0, tiled=True)  14.4 us
    ppermute x6, starting transfers between devices, swapped(): return lax.ppermute(value, 'sub', [(i, i ^ step) for i in range(4)])  9.9 us
    pallas_call x12, Pallas kernels, call(): pl.pallas_call(kernel, out_shape=outs, in_specs=[pl.BlockSpec(memory_spac...  9.56 us
    ppermute x6, waiting for transfers between devices, swapped(): return lax.ppermute(value, 'sub', [(i, i ^ step) for i in range(4)])  2.97 us
  transfers between devices with their start and end apart: 6, of which 3 were waited for; matrix products, arithmetic and copies ran while one was open for 0% of the time, Pallas kernels for 8%

profile of v10, /device:TPU:1, one launch (start us, length us, event | category | flops | bytes accessed | tf_op | source)
XLA Modules:
  0.0 79.7 jit_solution(9011985919853650061)
XLA Ops:
  0.6 1.2 %shard_map.130 = bf16[32,120,128]{2,1,0:T(8,128)(2,1)S(1)} custom-call(bf16[3,2,64,128]{3,2,1,0:T(8,128)(2,1)} %f_hbm.1, bf16[3,2,64,128]{3,2,1,0:T(8,128)(2,1)} %g_hbm.1, s32[4,12]{1,0:T(4,128)} %bitcast.5, s32[4,12]{1,0:T(4,128)} %bitcast.9), custom_call_target="tpu_custom_call" | custom-call | tf_op jit(solution)/shard_map/pallas_call | solution.py:41
  1.8 0.0 copy-start.2
  1.8 0.0 copy-start.6
  1.8 0.0 copy-start.7
  1.8 26.7 %all_to_all.15.in_ref = bf16[32,120,128]{2,1,0:T(8,128)(2,1)S(1)} all-to-all(bf16[32,120,128]{2,1,0:T(8,128)(2,1)S(1)} %shard_map.130), channel_id=1, replica_groups=mesh['tile'=32,'sub'=4] {'tile'}, dimensions={0} | all-to-all | bytes 1966080 | tf_op jit(solution)/shard_map/all_to_all | solution.py:663
  28.5 0.0 copy-done.2
  28.5 0.0 copy-done.6
  28.5 0.0 copy-done.7
  28.5 0.0 copy-start
  28.5 0.0 copy-start.1
  28.6 0.0 copy-start.3
  28.6 0.0 copy-start.5
  28.6 0.0 copy-start.8
  28.6 0.3 shard_map.132.own_ref
  28.9 0.8 %collective-permute-start.1 = (bf16[6,48,128]{2,1,0:T(8,128)(2,1)S(1)}, bf16[6,48,128]{2,1,0:T(8,128)(2,1)S(1)}, u32[]{:S(2)}, u32[]{:S(2)}) collective-permute-start(bf16[6,48,128]{2,1,0:T(8,128)(2,1)S(1)} %shard_map.132.own_ref), channel_id=1, source_target_pairs={{0,2},{1,3},{2,0},{3,1},{4,6},{5,7},{6,4},{7,5},{8,10},{9,11},{10,... | collective-permute-start | bytes 221192 | tf_op jit(solution)/shard_map/ppermute | solution.py:641
  29.7 3.1 %collective-permute-start = (bf16[6,48,128]{2,1,0:T(8,128)(2,1)S(1)}, bf16[6,48,128]{2,1,0:T(8,128)(2,1)S(1)}, u32[]{:S(2)}, u32[]{:S(2)}) collective-permute-start(bf16[6,48,128]{2,1,0:T(8,128)(2,1)S(1)} %shard_map.132.own_ref), channel_id=1, source_target_pairs={{0,1},{1,0},{2,3},{3,2},{4,5},{5,4},{6,7},{7,6},{8,9},{9,8},{10,11... | collective-permute-start | bytes 221192 | tf_op jit(solution)/shard_map/ppermute | solution.py:641
  32.8 0.0 copy-done
  32.8 0.0 copy-done.1
  32.8 0.0 copy-done.3
  32.8 0.0 copy-done.5
  32.8 0.0 copy-done.8
  32.9 2.2 %shard_map.131 = (f32[1152,128]{1,0:T(8,128)S(1)}, bf16[1152,128]{1,0:T(8,128)(2,1)S(1)}, f32[512,128]{1,0:T(8,128)S(1)}) custom-call(s32[4,12]{1,0:T(4,128)S(1)} %bitcast.13, s32[48,8]{1,0:T(8,128)S(1)} %copy-done.5, f32[72,64]{1,0:T(8,128)S(1)} %copy-done.3, bf16[32,120,128]{2,1,0:T(8,128)(2,1)S(1)} %all_to_all.15.in_ref, ...), custom_call_target="tpu_custom_call" | custom-call | tf_op jit(solution)/shard_map/pallas_call | solution.py:41
  35.1 0.0 collective-permute-done.1.refs_0_
  35.1 0.9 %collective-permute-start.2 = (bf16[6,48,128]{2,1,0:T(8,128)(2,1)S(1)}, bf16[6,48,128]{2,1,0:T(8,128)(2,1)S(1)}, u32[]{:S(2)}, u32[]{:S(2)}) collective-permute-start(bf16[6,48,128]{2,1,0:T(8,128)(2,1)S(1)} %shard_map.133.refs_2_.two_ref), channel_id=1, source_target_pairs={{0,1},{1,0},{2,3},{3,2},{4,5},{5,4},{6,7},{7,6},{8,9},{9,8},{10,11... | collective-permute-start | bytes 221192 | tf_op jit(solution)/shard_map/ppermute | solution.py:641
  36.0 0.0 collective-permute-done.refs_1_.one_ref
  36.0 0.9 %collective-permute-done.2.refs_3_.three_ref = bf16[6,48,128]{2,1,0:T(8,128)(2,1)S(1)} collective-permute-done((bf16[6,48,128]{2,1,0:T(8,128)(2,1)S(1)}, bf16[6,48,128]{2,1,0:T(8,128)(2,1)S(1)}, u32[]{:S(2)}, u32[]{:S(2)}) %collective-permute-start.2) | collective-permute-done | bytes 73760 | tf_op jit(solution)/shard_map/ppermute | solution.py:641
  37.0 0.4 collective-permute-start.3
  37.3 3.3 %shard_map.135 = (f32[1152,128]{1,0:T(8,128)S(1)}, f32[72,128]{1,0:T(8,128)S(1)}) custom-call(s32[4,12]{1,0:T(4,128)S(1)} %bitcast.7, s32[4,12]{1,0:T(4,128)S(1)} %bitcast.11, s32[4,12]{1,0:T(4,128)S(1)} %bitcast.14, s32[48,8]{1,0:T(8,128)S(1)} %copy-done.5, f32[72,64]{1,0:T(8,128)S(1)} %copy-done.3, bf16[6,48,128]{2,1,0:T(8,128)(2,1)S(1)} %shard_map.132.own_ref, ...), custom_call_target="tpu_custom_call" | custom-call | tf_op jit(solution)/shard_map/pallas_call | solution.py:41
  40.7 0.0 collective-permute-done.3.other_ref
  40.7 0.1 shard_map.136
  40.8 14.4 %all_to_all.16.in_ref = bf16[32,40,128]{2,1,0:T(8,128)(2,1)S(1)} all-to-all(bf16[32,40,128]{2,1,0:T(8,128)(2,1)S(1)} %shard_map.136), channel_id=1, replica_groups=mesh['tile'=32,'sub'=4] {'tile'}, dimensions={0} | all-to-all | bytes 655360 | tf_op jit(solution)/shard_map/all_to_all | solution.py:717
  55.3 0.0 copy-start.4
  55.3 0.1 shard_map.137.refs_1_
  55.3 0.8 %collective-permute-start.4 = (f32[40,128]{1,0:T(8,128)S(1)}, f32[40,128]{1,0:T(8,128)S(1)}, u32[]{:S(2)}, u32[]{:S(2)}) collective-permute-start(f32[40,128]{1,0:T(8,128)S(1)} %shard_map.137.refs_1_), channel_id=1, source_target_pairs={{0,2},{1,3},{2,0},{3,1},{4,6},{5,7},{6,4},{7,5},{8,10},{9,11},{10,... | collective-permute-start | bytes 61448 | tf_op jit(solution)/shard_map/ppermute | solution.py:641
  56.1 1.9 %collective-permute-done.4.refs_2_ = f32[40,128]{1,0:T(8,128)S(1)} collective-permute-done((f32[40,128]{1,0:T(8,128)S(1)}, f32[40,128]{1,0:T(8,128)S(1)}, u32[]{:S(2)}, u32[]{:S(2)}) %collective-permute-start.4) | collective-permute-done | bytes 20512 | tf_op jit(solution)/shard_map/ppermute | solution.py:641
  58.0 0.0 copy-done.4
  58.1 15.3 %all_to_all.17.in_ref = bf16[32,80,128]{2,1,0:T(8,128)(2,1)S(1)} all-to-all(bf16[32,80,128]{2,1,0:T(8,128)(2,1)S(1)} %shard_map.138), channel_id=1, replica_groups=mesh['tile'=32,'sub'=4] {'tile'}, dimensions={0} | all-to-all | bytes 1310720 | tf_op jit(solution)/shard_map/all_to_all | solution.py:726
  73.4 0.1 shard_map.140.own_ref
  73.5 3.9 %collective-permute-start.5 = (bf16[32,40,128]{2,1,0:T(8,128)(2,1)S(1)}, bf16[32,40,128]{2,1,0:T(8,128)(2,1)S(1)}, u32[]{:S(2)}, u32[]{:S(2)}) collective-permute-start(bf16[32,40,128]{2,1,0:T(8,128)(2,1)S(1)} %shard_map.140.own_ref), channel_id=1, source_target_pairs={{0,1},{1,0},{2,3},{3,2},{4,5},{5,4},{6,7},{7,6},{8,9},{9,8},{10,11... | collective-permute-start | bytes 983048 | tf_op jit(solution)/shard_map/ppermute | solution.py:641
  77.3 1.1 %shard_map.139 = bf16[3,2,64,128]{3,2,1,0:T(8,128)(2,1)} custom-call(s32[4,12]{1,0:T(4,128)S(1)} %bitcast.8, s32[4,12]{1,0:T(4,128)S(1)} %bitcast.12, bf16[2,64,64]{2,1,0:T(8,128)(2,1)S(1)} %copy-done.4, bf16[32,80,128]{2,1,0:T(8,128)(2,1)S(1)} %all_to_all.17.in_ref), custom_call_target="tpu_custom_call" | custom-call | tf_op jit(solution)/shard_map/pallas_call | solution.py:41
  78.4 0.2 collective-permute-done.5.other_ref
  78.6 1.1 %shard_map.141 = (f32[1152,128]{1,0:T(8,128)}, f32[1152,128]{1,0:T(8,128)}) custom-call(bf16[32,40,128]{2,1,0:T(8,128)(2,1)S(1)} %shard_map.140.own_ref, bf16[32,40,128]{2,1,0:T(8,128)(2,1)S(1)} %collective-permute-done.5.other_ref), custom_call_target="tpu_custom_call" | custom-call | tf_op jit(solution)/shard_map/pallas_call | solution.py:41
  (3 shorter events, 0.1 us)
Async XLA Ops:
  1.8 26.7 %copy-start.2 = (bf16[2,288,432]{2,1,0:T(8,128)(2,1)S(1)}, bf16[2,288,432]{2,1,0:T(8,128)(2,1)}, u32[]{:S(2)}) copy-start(bf16[2,288,432]{2,1,0:T(8,128)(2,1)} %constant.8.clone.sel_ref) | copy-start | bytes 1492996
  1.8 26.7 %copy-start.6 = (s32[12,4]{0,1:T(4,128)S(1)}, s32[12,4]{0,1:T(4,128)}, u32[]{:S(2)}) copy-start(s32[12,4]{0,1:T(4,128)} %param.15) | copy-start | bytes 580
  1.8 26.7 %copy-start.7 = (s32[12,4]{0,1:T(4,128)S(1)}, s32[12,4]{0,1:T(4,128)}, u32[]{:S(2)}) copy-start(s32[12,4]{0,1:T(4,128)} %param.16) | copy-start | bytes 580
  28.5 4.3 %copy-start = (bf16[3,3,128,128]{3,2,1,0:T(8,128)(2,1)S(1)}, bf16[3,3,128,128]{3,2,1,0:T(8,128)(2,1)}, u32[]{:S(2)}) copy-start(bf16[3,3,128,128]{3,2,1,0:T(8,128)(2,1)} %w1_ref.3) | copy-start | bytes 884740
  28.5 4.3 %copy-start.1 = (bf16[3,3,128,128]{3,2,1,0:T(8,128)(2,1)S(1)}, bf16[3,3,128,128]{3,2,1,0:T(8,128)(2,1)}, u32[]{:S(2)}) copy-start(bf16[3,3,128,128]{3,2,1,0:T(8,128)(2,1)} %w2_ref.3) | copy-start | bytes 884740
  28.6 4.3 %copy-start.3 = (f32[72,64]{1,0:T(8,128)S(1)}, f32[72,64]{1,0:T(8,128)}, u32[]{:S(2)}) copy-start(f32[72,64]{1,0:T(8,128)} %constant.10.clone._select.sel_ref) | copy-start | bytes 55300
  28.6 4.3 %copy-start.5 = (s32[48,8]{1,0:T(8,128)S(1)}, s32[48,8]{1,0:T(8,128)}, u32[]{:S(2)}) copy-start(s32[48,8]{1,0:T(8,128)} %constant.9.clone._plan.plan_ref) | copy-start | bytes 4612
  28.6 4.3 %copy-start.8 = (s32[12,4]{0,1:T(4,128)S(1)}, s32[12,4]{0,1:T(4,128)}, u32[]{:S(2)}) copy-start(s32[12,4]{0,1:T(4,128)} %param.17) | copy-start | bytes 580
  28.9 6.2 %collective-permute-start.1 = (bf16[6,48,128]{2,1,0:T(8,128)(2,1)S(1)}, bf16[6,48,128]{2,1,0:T(8,128)(2,1)S(1)}, u32[]{:S(2)}, u32[]{:S(2)}) collective-permute-start(bf16[6,48,128]{2,1,0:T(8,128)(2,1)S(1)} %shard_map.132.own_ref), channel_id=1, source_target_pairs={{0,2},{1,3},{2,0},{3,1},{4,6},{5,7},{6,4},{7,5},{8,10},{9,11},{10,... | collective-permute-start | bytes 221192 | tf_op jit(solution)/shard_map/ppermute | solution.py:641
  29.7 6.3 %collective-permute-start = (bf16[6,48,128]{2,1,0:T(8,128)(2,1)S(1)}, bf16[6,48,128]{2,1,0:T(8,128)(2,1)S(1)}, u32[]{:S(2)}, u32[]{:S(2)}) collective-permute-start(bf16[6,48,128]{2,1,0:T(8,128)(2,1)S(1)} %shard_map.132.own_ref), channel_id=1, source_target_pairs={{0,1},{1,0},{2,3},{3,2},{4,5},{5,4},{6,7},{7,6},{8,9},{9,8},{10,11... | collective-permute-start | bytes 221192 | tf_op jit(solution)/shard_map/ppermute | solution.py:641
  35.1 1.9 %collective-permute-start.2 = (bf16[6,48,128]{2,1,0:T(8,128)(2,1)S(1)}, bf16[6,48,128]{2,1,0:T(8,128)(2,1)S(1)}, u32[]{:S(2)}, u32[]{:S(2)}) collective-permute-start(bf16[6,48,128]{2,1,0:T(8,128)(2,1)S(1)} %shard_map.133.refs_2_.two_ref), channel_id=1, source_target_pairs={{0,1},{1,0},{2,3},{3,2},{4,5},{5,4},{6,7},{7,6},{8,9},{9,8},{10,11... | collective-permute-start | bytes 221192 | tf_op jit(solution)/shard_map/ppermute | solution.py:641
  37.0 3.7 %collective-permute-start.3 = (bf16[1152,128]{1,0:T(8,128)(2,1)S(1)}, bf16[1152,128]{1,0:T(8,128)(2,1)S(1)}, u32[]{:S(2)}, u32[]{:S(2)}) collective-permute-start(bf16[1152,128]{1,0:T(8,128)(2,1)S(1)} %shard_map.134), channel_id=1, source_target_pairs={{0,1},{1,0},{2,3},{3,2},{4,5},{5,4},{6,7},{7,6},{8,9},{9,8},{10,11... | collective-permute-start | bytes 884744 | tf_op jit(solution)/shard_map/ppermute | solution.py:641
  55.3 2.8 %copy-start.4 = (bf16[2,64,64]{2,1,0:T(8,128)(2,1)S(1)}, bf16[2,64,64]{2,1,0:T(8,128)(2,1)}, u32[]{:S(2)}) copy-start(bf16[2,64,64]{2,1,0:T(8,128)(2,1)} %constant.11.clone.refs_0_.sel_ref) | copy-start | bytes 49156
  55.3 2.7 %collective-permute-start.4 = (f32[40,128]{1,0:T(8,128)S(1)}, f32[40,128]{1,0:T(8,128)S(1)}, u32[]{:S(2)}, u32[]{:S(2)}) collective-permute-start(f32[40,128]{1,0:T(8,128)S(1)} %shard_map.137.refs_1_), channel_id=1, source_target_pairs={{0,2},{1,3},{2,0},{3,1},{4,6},{5,7},{6,4},{7,5},{8,10},{9,11},{10,... | collective-permute-start | bytes 61448 | tf_op jit(solution)/shard_map/ppermute | solution.py:641
  73.5 5.1 %collective-permute-start.5 = (bf16[32,40,128]{2,1,0:T(8,128)(2,1)S(1)}, bf16[32,40,128]{2,1,0:T(8,128)(2,1)S(1)}, u32[]{:S(2)}, u32[]{:S(2)}) collective-permute-start(bf16[32,40,128]{2,1,0:T(8,128)(2,1)S(1)} %shard_map.140.own_ref), channel_id=1, source_target_pairs={{0,1},{1,0},{2,3},{3,2},{4,5},{5,4},{6,7},{7,6},{8,9},{9,8},{10,11... | collective-permute-start | bytes 983048 | tf_op jit(solution)/shard_map/ppermute | solution.py:641

commit v11 on v10

--- a/solution.py
+++ b/solution.py
@@ -686,7 +686,7 @@
     )
     beyond = call(after_kernel, jax.ShapeDtypeStruct((WINDOW, ENDS, CH), BF), [], (beyond, own), dict.fromkeys((0, 1, "o0"), "a"), {0: 0})
     lines = (lines, beside, beyond, swapped(beyond, 1))
-    away = call(after_kernel, jax.ShapeDtypeStruct((HALF, CH), BF), [], (away, *lines[1:]), dict.fromkeys((0, 1, 2, 3, "o0"), "a"), {0: 0})
+    away = call(after_kernel, jax.ShapeDtypeStruct((HALF, CH), BF), [], (away, *lines[1:3]), dict.fromkeys((0, 1, 2, "o0"), "a"), {0: 0})
     other = swapped(away, 1)
 
     line, tails = call(

time: 79.9 us -> 79.8 us (level)
  no operation moved by 1% of the time
where the time goes in v11:
time: 79.8 us; the launch traced here: 79.6 us
  blocking collectives  56.2 us (70%)
  starting transfers between devices  9.67 us (12%)
  Pallas kernels  9.57 us (12%)
  waiting for transfers between devices  3.3 us (4%)
  between operations  0.8 us (1%)
    all_to_all x1, blocking collectives, body(): strips = lax.all_to_all(slots, 'tile', 0, 0, tiled=True)  26.7 us
    all_to_all x1, blocking collectives, body(): reduced = lax.all_to_all(reduced, 'tile', 0, 0, tiled=True)  15.5 us
    all_to_all x1, blocking collectives, body(): slots = lax.all_to_all(slots, 'tile', 0, 0, tiled=True)  14 us
    ppermute x6, starting transfers between devices, swapped(): return lax.ppermute(value, 'sub', [(i, i ^ step) for i in range(4)])  9.67 us
    pallas_call x12, Pallas kernels, call(): pl.pallas_call(kernel, out_shape=outs, in_specs=[pl.BlockSpec(memory_spac...  9.57 us
    ppermute x6, waiting for transfers between devices, swapped(): return lax.ppermute(value, 'sub', [(i, i ^ step) for i in range(4)])  3.3 us
  transfers between devices with their start and end apart: 6, of which 3 were waited for; matrix products, arithmetic and copies ran while one was open for 0% of the time, Pallas kernels for 8%

profile of v11, /device:TPU:1, one launch (start us, length us, event | category | flops | bytes accessed | tf_op | source)
XLA Modules:
  0.0 79.6 jit_solution(7685125034272890159)
XLA Ops:
  0.6 1.2 %shard_map.130 = bf16[32,120,128]{2,1,0:T(8,128)(2,1)S(1)} custom-call(bf16[3,2,64,128]{3,2,1,0:T(8,128)(2,1)} %f_hbm.1, bf16[3,2,64,128]{3,2,1,0:T(8,128)(2,1)} %g_hbm.1, s32[4,12]{1,0:T(4,128)} %bitcast.5, s32[4,12]{1,0:T(4,128)} %bitcast.9), custom_call_target="tpu_custom_call" | custom-call | tf_op jit(solution)/shard_map/pallas_call | solution.py:41
  1.8 0.0 copy-start.2
  1.8 0.0 copy-start.6
  1.8 0.0 copy-start.7
  1.8 26.7 %all_to_all.15.in_ref = bf16[32,120,128]{2,1,0:T(8,128)(2,1)S(1)} all-to-all(bf16[32,120,128]{2,1,0:T(8,128)(2,1)S(1)} %shard_map.130), channel_id=1, replica_groups=mesh['tile'=32,'sub'=4] {'tile'}, dimensions={0} | all-to-all | bytes 1966080 | tf_op jit(solution)/shard_map/all_to_all | solution.py:663
  28.5 0.0 copy-done.2
  28.5 0.0 copy-done.6
  28.5 0.0 copy-done.7
  28.5 0.0 copy-start
  28.5 0.0 copy-start.1
  28.6 0.0 copy-start.3
  28.6 0.0 copy-start.5
  28.6 0.0 copy-start.8
  28.6 0.3 shard_map.132.own_ref
  28.9 0.8 %collective-permute-start.1 = (bf16[6,48,128]{2,1,0:T(8,128)(2,1)S(1)}, bf16[6,48,128]{2,1,0:T(8,128)(2,1)S(1)}, u32[]{:S(2)}, u32[]{:S(2)}) collective-permute-start(bf16[6,48,128]{2,1,0:T(8,128)(2,1)S(1)} %shard_map.132.own_ref), channel_id=1, source_target_pairs={{0,2},{1,3},{2,0},{3,1},{4,6},{5,7},{6,4},{7,5},{8,10},{9,11},{10,... | collective-permute-start | bytes 221192 | tf_op jit(solution)/shard_map/ppermute | solution.py:641
  29.7 3.1 %collective-permute-start = (bf16[6,48,128]{2,1,0:T(8,128)(2,1)S(1)}, bf16[6,48,128]{2,1,0:T(8,128)(2,1)S(1)}, u32[]{:S(2)}, u32[]{:S(2)}) collective-permute-start(bf16[6,48,128]{2,1,0:T(8,128)(2,1)S(1)} %shard_map.132.own_ref), channel_id=1, source_target_pairs={{0,1},{1,0},{2,3},{3,2},{4,5},{5,4},{6,7},{7,6},{8,9},{9,8},{10,11... | collective-permute-start | bytes 221192 | tf_op jit(solution)/shard_map/ppermute | solution.py:641
  32.8 0.0 copy-done
  32.8 0.0 copy-done.1
  32.8 0.0 copy-done.3
  32.8 0.0 copy-done.5
  32.8 0.0 copy-done.8
  32.9 2.2 %shard_map.131 = (f32[1152,128]{1,0:T(8,128)S(1)}, bf16[1152,128]{1,0:T(8,128)(2,1)S(1)}, f32[512,128]{1,0:T(8,128)S(1)}) custom-call(s32[4,12]{1,0:T(4,128)S(1)} %bitcast.13, s32[48,8]{1,0:T(8,128)S(1)} %copy-done.5, f32[72,64]{1,0:T(8,128)S(1)} %copy-done.3, bf16[32,120,128]{2,1,0:T(8,128)(2,1)S(1)} %all_to_all.15.in_ref, ...), custom_call_target="tpu_custom_call" | custom-call | tf_op jit(solution)/shard_map/pallas_call | solution.py:41
  35.1 0.0 collective-permute-done.1.refs_0_
  35.1 0.0 collective-permute-done.refs_1_.one_ref
  35.1 0.9 %collective-permute-start.2 = (bf16[1152,128]{1,0:T(8,128)(2,1)S(1)}, bf16[1152,128]{1,0:T(8,128)(2,1)S(1)}, u32[]{:S(2)}, u32[]{:S(2)}) collective-permute-start(bf16[1152,128]{1,0:T(8,128)(2,1)S(1)} %shard_map.134), channel_id=1, source_target_pairs={{0,1},{1,0},{2,3},{3,2},{4,5},{5,4},{6,7},{7,6},{8,9},{9,8},{10,11... | collective-permute-start | bytes 884744 | tf_op jit(solution)/shard_map/ppermute | solution.py:641
  36.0 0.1 collective-permute-start.3
  36.1 1.2 %collective-permute-done.3.three_ref = bf16[6,48,128]{2,1,0:T(8,128)(2,1)S(1)} collective-permute-done((bf16[6,48,128]{2,1,0:T(8,128)(2,1)S(1)}, bf16[6,48,128]{2,1,0:T(8,128)(2,1)S(1)}, u32[]{:S(2)}, u32[]{:S(2)}) %collective-permute-start.3) | collective-permute-done | bytes 73760 | tf_op jit(solution)/shard_map/ppermute | solution.py:641
  37.4 3.4 %shard_map.135 = (f32[1152,128]{1,0:T(8,128)S(1)}, f32[72,128]{1,0:T(8,128)S(1)}) custom-call(s32[4,12]{1,0:T(4,128)S(1)} %bitcast.7, s32[4,12]{1,0:T(4,128)S(1)} %bitcast.11, s32[4,12]{1,0:T(4,128)S(1)} %bitcast.14, s32[48,8]{1,0:T(8,128)S(1)} %copy-done.5, f32[72,64]{1,0:T(8,128)S(1)} %copy-done.3, bf16[6,48,128]{2,1,0:T(8,128)(2,1)S(1)} %shard_map.132.own_ref, ...), custom_call_target="tpu_custom_call" | custom-call | tf_op jit(solution)/shard_map/pallas_call | solution.py:41
  40.7 0.0 collective-permute-done.2.other_ref
  40.7 0.1 shard_map.136
  40.9 14.0 %all_to_all.16.in_ref = bf16[32,40,128]{2,1,0:T(8,128)(2,1)S(1)} all-to-all(bf16[32,40,128]{2,1,0:T(8,128)(2,1)S(1)} %shard_map.136), channel_id=1, replica_groups=mesh['tile'=32,'sub'=4] {'tile'}, dimensions={0} | all-to-all | bytes 655360 | tf_op jit(solution)/shard_map/all_to_all | solution.py:717
  54.9 0.0 copy-start.4
  54.9 0.1 shard_map.137.refs_1_
  55.0 0.8 %collective-permute-start.4 = (f32[40,128]{1,0:T(8,128)S(1)}, f32[40,128]{1,0:T(8,128)S(1)}, u32[]{:S(2)}, u32[]{:S(2)}) collective-permute-start(f32[40,128]{1,0:T(8,128)S(1)} %shard_map.137.refs_1_), channel_id=1, source_target_pairs={{0,2},{1,3},{2,0},{3,1},{4,6},{5,7},{6,4},{7,5},{8,10},{9,11},{10,... | collective-permute-start | bytes 61448 | tf_op jit(solution)/shard_map/ppermute | solution.py:641
  55.8 1.9 %collective-permute-done.4.refs_2_ = f32[40,128]{1,0:T(8,128)S(1)} collective-permute-done((f32[40,128]{1,0:T(8,128)S(1)}, f32[40,128]{1,0:T(8,128)S(1)}, u32[]{:S(2)}, u32[]{:S(2)}) %collective-permute-start.4) | collective-permute-done | bytes 20512 | tf_op jit(solution)/shard_map/ppermute | solution.py:641
  57.7 0.0 copy-done.4
  57.7 0.1 shard_map.138
  57.7 15.5 %all_to_all.17.in_ref = bf16[32,80,128]{2,1,0:T(8,128)(2,1)S(1)} all-to-all(bf16[32,80,128]{2,1,0:T(8,128)(2,1)S(1)} %shard_map.138), channel_id=1, replica_groups=mesh['tile'=32,'sub'=4] {'tile'}, dimensions={0} | all-to-all | bytes 1310720 | tf_op jit(solution)/shard_map/all_to_all | solution.py:726
  73.2 0.1 shard_map.140.own_ref
  73.3 3.9 %collective-permute-start.5 = (bf16[32,40,128]{2,1,0:T(8,128)(2,1)S(1)}, bf16[32,40,128]{2,1,0:T(8,128)(2,1)S(1)}, u32[]{:S(2)}, u32[]{:S(2)}) collective-permute-start(bf16[32,40,128]{2,1,0:T(8,128)(2,1)S(1)} %shard_map.140.own_ref), channel_id=1, source_target_pairs={{0,1},{1,0},{2,3},{3,2},{4,5},{5,4},{6,7},{7,6},{8,9},{9,8},{10,11... | collective-permute-start | bytes 983048 | tf_op jit(solution)/shard_map/ppermute | solution.py:641
  77.2 1.1 %shard_map.139 = bf16[3,2,64,128]{3,2,1,0:T(8,128)(2,1)} custom-call(s32[4,12]{1,0:T(4,128)S(1)} %bitcast.8, s32[4,12]{1,0:T(4,128)S(1)} %bitcast.12, bf16[2,64,64]{2,1,0:T(8,128)(2,1)S(1)} %copy-done.4, bf16[32,80,128]{2,1,0:T(8,128)(2,1)S(1)} %all_to_all.17.in_ref), custom_call_target="tpu_custom_call" | custom-call | tf_op jit(solution)/shard_map/pallas_call | solution.py:41
  78.3 0.2 collective-permute-done.5.other_ref
  78.5 1.1 %shard_map.141 = (f32[1152,128]{1,0:T(8,128)}, f32[1152,128]{1,0:T(8,128)}) custom-call(bf16[32,40,128]{2,1,0:T(8,128)(2,1)S(1)} %shard_map.140.own_ref, bf16[32,40,128]{2,1,0:T(8,128)(2,1)S(1)} %collective-permute-done.5.other_ref), custom_call_target="tpu_custom_call" | custom-call | tf_op jit(solution)/shard_map/pallas_call | solution.py:41
  (2 shorter events, 0.0 us)
Async XLA Ops:
  1.8 26.7 %copy-start.2 = (bf16[2,288,432]{2,1,0:T(8,128)(2,1)S(1)}, bf16[2,288,432]{2,1,0:T(8,128)(2,1)}, u32[]{:S(2)}) copy-start(bf16[2,288,432]{2,1,0:T(8,128)(2,1)} %constant.8.clone.sel_ref) | copy-start | bytes 1492996
  1.8 26.7 %copy-start.6 = (s32[12,4]{0,1:T(4,128)S(1)}, s32[12,4]{0,1:T(4,128)}, u32[]{:S(2)}) copy-start(s32[12,4]{0,1:T(4,128)} %param.15) | copy-start | bytes 580
  1.8 26.7 %copy-start.7 = (s32[12,4]{0,1:T(4,128)S(1)}, s32[12,4]{0,1:T(4,128)}, u32[]{:S(2)}) copy-start(s32[12,4]{0,1:T(4,128)} %param.16) | copy-start | bytes 580
  28.5 4.3 %copy-start = (bf16[3,3,128,128]{3,2,1,0:T(8,128)(2,1)S(1)}, bf16[3,3,128,128]{3,2,1,0:T(8,128)(2,1)}, u32[]{:S(2)}) copy-start(bf16[3,3,128,128]{3,2,1,0:T(8,128)(2,1)} %w1_ref.3) | copy-start | bytes 884740
  28.5 4.3 %copy-start.1 = (bf16[3,3,128,128]{3,2,1,0:T(8,128)(2,1)S(1)}, bf16[3,3,128,128]{3,2,1,0:T(8,128)(2,1)}, u32[]{:S(2)}) copy-start(bf16[3,3,128,128]{3,2,1,0:T(8,128)(2,1)} %w2_ref.3) | copy-start | bytes 884740
  28.6 4.3 %copy-start.3 = (f32[72,64]{1,0:T(8,128)S(1)}, f32[72,64]{1,0:T(8,128)}, u32[]{:S(2)}) copy-start(f32[72,64]{1,0:T(8,128)} %constant.10.clone._select.sel_ref) | copy-start | bytes 55300
  28.6 4.3 %copy-start.5 = (s32[48,8]{1,0:T(8,128)S(1)}, s32[48,8]{1,0:T(8,128)}, u32[]{:S(2)}) copy-start(s32[48,8]{1,0:T(8,128)} %constant.9.clone._plan.plan_ref) | copy-start | bytes 4612
  28.6 4.3 %copy-start.8 = (s32[12,4]{0,1:T(4,128)S(1)}, s32[12,4]{0,1:T(4,128)}, u32[]{:S(2)}) copy-start(s32[12,4]{0,1:T(4,128)} %param.17) | copy-start | bytes 580
  28.9 6.2 %collective-permute-start.1 = (bf16[6,48,128]{2,1,0:T(8,128)(2,1)S(1)}, bf16[6,48,128]{2,1,0:T(8,128)(2,1)S(1)}, u32[]{:S(2)}, u32[]{:S(2)}) collective-permute-start(bf16[6,48,128]{2,1,0:T(8,128)(2,1)S(1)} %shard_map.132.own_ref), channel_id=1, source_target_pairs={{0,2},{1,3},{2,0},{3,1},{4,6},{5,7},{6,4},{7,5},{8,10},{9,11},{10,... | collective-permute-start | bytes 221192 | tf_op jit(solution)/shard_map/ppermute | solution.py:641
  29.7 5.4 %collective-permute-start = (bf16[6,48,128]{2,1,0:T(8,128)(2,1)S(1)}, bf16[6,48,128]{2,1,0:T(8,128)(2,1)S(1)}, u32[]{:S(2)}, u32[]{:S(2)}) collective-permute-start(bf16[6,48,128]{2,1,0:T(8,128)(2,1)S(1)} %shard_map.132.own_ref), channel_id=1, source_target_pairs={{0,1},{1,0},{2,3},{3,2},{4,5},{5,4},{6,7},{7,6},{8,9},{9,8},{10,11... | collective-permute-start | bytes 221192 | tf_op jit(solution)/shard_map/ppermute | solution.py:641
  35.1 5.6 %collective-permute-start.2 = (bf16[1152,128]{1,0:T(8,128)(2,1)S(1)}, bf16[1152,128]{1,0:T(8,128)(2,1)S(1)}, u32[]{:S(2)}, u32[]{:S(2)}) collective-permute-start(bf16[1152,128]{1,0:T(8,128)(2,1)S(1)} %shard_map.134), channel_id=1, source_target_pairs={{0,1},{1,0},{2,3},{3,2},{4,5},{5,4},{6,7},{7,6},{8,9},{9,8},{10,11... | collective-permute-start | bytes 884744 | tf_op jit(solution)/shard_map/ppermute | solution.py:641
  36.0 1.3 %collective-permute-start.3 = (bf16[6,48,128]{2,1,0:T(8,128)(2,1)S(1)}, bf16[6,48,128]{2,1,0:T(8,128)(2,1)S(1)}, u32[]{:S(2)}, u32[]{:S(2)}) collective-permute-start(bf16[6,48,128]{2,1,0:T(8,128)(2,1)S(1)} %shard_map.133.refs_2_.two_ref), channel_id=1, source_target_pairs={{0,1},{1,0},{2,3},{3,2},{4,5},{5,4},{6,7},{7,6},{8,9},{9,8},{10,11... | collective-permute-start | bytes 221192 | tf_op jit(solution)/shard_map/ppermute | solution.py:641
  54.9 2.8 %copy-start.4 = (bf16[2,64,64]{2,1,0:T(8,128)(2,1)S(1)}, bf16[2,64,64]{2,1,0:T(8,128)(2,1)}, u32[]{:S(2)}) copy-start(bf16[2,64,64]{2,1,0:T(8,128)(2,1)} %constant.11.clone.refs_0_.sel_ref) | copy-start | bytes 49156
  55.0 2.7 %collective-permute-start.4 = (f32[40,128]{1,0:T(8,128)S(1)}, f32[40,128]{1,0:T(8,128)S(1)}, u32[]{:S(2)}, u32[]{:S(2)}) collective-permute-start(f32[40,128]{1,0:T(8,128)S(1)} %shard_map.137.refs_1_), channel_id=1, source_target_pairs={{0,2},{1,3},{2,0},{3,1},{4,6},{5,7},{6,4},{7,5},{8,10},{9,11},{10,... | collective-permute-start | bytes 61448 | tf_op jit(solution)/shard_map/ppermute | solution.py:641
  73.3 5.2 %collective-permute-start.5 = (bf16[32,40,128]{2,1,0:T(8,128)(2,1)S(1)}, bf16[32,40,128]{2,1,0:T(8,128)(2,1)S(1)}, u32[]{:S(2)}, u32[]{:S(2)}) collective-permute-start(bf16[32,40,128]{2,1,0:T(8,128)(2,1)S(1)} %shard_map.140.own_ref), channel_id=1, source_target_pairs={{0,1},{1,0},{2,3},{3,2},{4,5},{5,4},{6,7},{7,6},{8,9},{9,8},{10,11... | collective-permute-start | bytes 983048 | tf_op jit(solution)/shard_map/ppermute | solution.py:641

commit v12 on v10

--- a/solution.py
+++ b/solution.py
@@ -174,7 +174,7 @@
 
 
 def interior_kernel(
-    _fill, _plan, _select, in_ref, w1_ref, w2_ref, own_ref, away_ref, sent, acc, done, w1t, w2t, f2, g2, wide
+    _fill, _plan, _select, in_ref, w1_ref, w2_ref, own_ref, away_ref, sent, w1t, w2t, acc, done, f2, g2, wide
 ):
     band, group = here()
     strip, _ = unit_of(band)
@@ -242,13 +242,11 @@
 
 
 def main_kernel(
-    fn_ref, rot_ref, fill_ref, plan_ref, sel_ref, own_ref, one_ref, two_ref, three_ref, w1_ref, w2_ref,
+    fn_ref, rot_ref, fill_ref, plan_ref, sel_ref, own_ref, one_ref, two_ref, three_ref, w1_ref, w1t, w2t,
     share_ref, tail_ref,
-    w1t, w2t, xs, hal, nb, lp, lg, lc, ss, gp, gpu, owe,
+    xs, hal, nb, lp, lg, lc, ss, gp, gpu, owe,
 ):
     band, group = here()
-    transpose_weights(w1_ref, w1t)
-    transpose_weights(w2_ref, w2t)
 
     line = lax.broadcasted_iota(I32, (64, 1), 0)
     place = line & 15
@@ -670,14 +668,13 @@
     beyond, beside = swapped(lines, 2), swapped(lines, 1)
     tables = (corner_fill.T, jnp.asarray(plan), jnp.asarray(select, F32))
     share = jax.ShapeDtypeStruct((HALF, CH), F32)
-    own, away, sent = call(
+    turned = jax.ShapeDtypeStruct((HALF, CH), BF)
+    own, away, sent, first_turned, second_turned = call(
         interior_kernel,
-        [share, jax.ShapeDtypeStruct((HALF, CH), BF), jax.ShapeDtypeStruct((BANDS * 16, CH), F32)],
+        [share, jax.ShapeDtypeStruct((HALF, CH), BF), jax.ShapeDtypeStruct((BANDS * 16, CH), F32), turned, turned],
         [
             pltpu.VMEM((2304, CH), F32),
             pltpu.VMEM((512, CH), F32),
-            pltpu.VMEM((1152, CH), BF),
-            pltpu.VMEM((1152, CH), BF),
             pltpu.VMEM((768, CH), F32),
             pltpu.VMEM((768, CH), F32),
             pltpu.VMEM((BANDS * UNIT, CH), F32),
@@ -693,8 +690,6 @@
         main_kernel,
         [share, jax.ShapeDtypeStruct((72, CH), F32)],
         [
-            pltpu.VMEM((1152, CH), BF),
-            pltpu.VMEM((1152, CH), BF),
             pltpu.VMEM((4, WINDOW, 64, CH), BF),
             pltpu.VMEM((WINDOW, 64, CH), BF),
             pltpu.VMEM((2, 5, 5, 64, CH), BF),
@@ -706,7 +701,7 @@
             pltpu.VMEM((5, 64, CH), BF),
             pltpu.VMEM((4, 64, CH), F32),
         ],
-        (*seams, *tables, *lines, first_weight, second_weight),
+        (*seams, *tables, *lines, first_weight, first_turned, second_turned),
     )
     slots = call(
         share_kernel,

time: 79.9 us -> 79.9 us (level)
  no operation moved by 1% of the time
where the time goes in v12:
time: 79.9 us; the launch traced here: 79.7 us
  blocking collectives  56.4 us (71%)
  starting transfers between devices  9.84 us (12%)
  Pallas kernels  9.58 us (12%)
  waiting for transfers between devices  2.97 us (4%)
    all_to_all x1, blocking collectives, body(): strips = lax.all_to_all(slots, 'tile', 0, 0, tiled=True)  26.7 us
    all_to_all x1, blocking collectives, body(): reduced = lax.all_to_all(reduced, 'tile', 0, 0, tiled=True)  15.3 us
    all_to_all x1, blocking collectives, body(): slots = lax.all_to_all(slots, 'tile', 0, 0, tiled=True)  14.4 us
    ppermute x6, starting transfers between devices, swapped(): return lax.ppermute(value, 'sub', [(i, i ^ step) for i in range(4)])  9.84 us
    pallas_call x12, Pallas kernels, call(): pl.pallas_call(kernel, out_shape=outs, in_specs=[pl.BlockSpec(memory_spac...  9.58 us
    ppermute x6, waiting for transfers between devices, swapped(): return lax.ppermute(value, 'sub', [(i, i ^ step) for i in range(4)])  2.97 us
  transfers between devices with their start and end apart: 6, of which 3 were waited for; matrix products, arithmetic and copies ran while one was open for 0% of the time, Pallas kernels for 8%

profile of v12, /device:TPU:1, one launch (start us, length us, event | category | flops | bytes accessed | tf_op | source)
XLA Modules:
  0.0 79.7 jit_solution(18420551489827797194)
XLA Ops:
  0.6 1.2 %shard_map.130 = bf16[32,120,128]{2,1,0:T(8,128)(2,1)S(1)} custom-call(bf16[3,2,64,128]{3,2,1,0:T(8,128)(2,1)} %f_hbm.1, bf16[3,2,64,128]{3,2,1,0:T(8,128)(2,1)} %g_hbm.1, s32[4,12]{1,0:T(4,128)} %bitcast.5, s32[4,12]{1,0:T(4,128)} %bitcast.9), custom_call_target="tpu_custom_call" | custom-call | tf_op jit(solution)/shard_map/pallas_call | solution.py:41
  1.8 0.0 copy-start.1
  1.8 0.0 copy-start.6
  1.8 0.0 copy-start.7
  1.8 26.7 %all_to_all.15.in_ref = bf16[32,120,128]{2,1,0:T(8,128)(2,1)S(1)} all-to-all(bf16[32,120,128]{2,1,0:T(8,128)(2,1)S(1)} %shard_map.130), channel_id=1, replica_groups=mesh['tile'=32,'sub'=4] {'tile'}, dimensions={0} | all-to-all | bytes 1966080 | tf_op jit(solution)/shard_map/all_to_all | solution.py:661
  28.5 0.0 copy-done.1
  28.5 0.0 copy-done.6
  28.5 0.0 copy-done.7
  28.5 0.0 copy-start
  28.5 0.0 copy-start.2
  28.6 0.0 copy-start.3
  28.6 0.0 copy-start.5
  28.6 0.0 copy-start.8
  28.6 0.3 shard_map.132.own_ref
  28.9 0.8 %collective-permute-start.1 = (bf16[6,48,128]{2,1,0:T(8,128)(2,1)S(1)}, bf16[6,48,128]{2,1,0:T(8,128)(2,1)S(1)}, u32[]{:S(2)}, u32[]{:S(2)}) collective-permute-start(bf16[6,48,128]{2,1,0:T(8,128)(2,1)S(1)} %shard_map.132.own_ref), channel_id=1, source_target_pairs={{0,2},{1,3},{2,0},{3,1},{4,6},{5,7},{6,4},{7,5},{8,10},{9,11},{10,... | collective-permute-start | bytes 221192 | tf_op jit(solution)/shard_map/ppermute | solution.py:639
  29.7 3.1 %collective-permute-start = (bf16[6,48,128]{2,1,0:T(8,128)(2,1)S(1)}, bf16[6,48,128]{2,1,0:T(8,128)(2,1)S(1)}, u32[]{:S(2)}, u32[]{:S(2)}) collective-permute-start(bf16[6,48,128]{2,1,0:T(8,128)(2,1)S(1)} %shard_map.132.own_ref), channel_id=1, source_target_pairs={{0,1},{1,0},{2,3},{3,2},{4,5},{5,4},{6,7},{7,6},{8,9},{9,8},{10,11... | collective-permute-start | bytes 221192 | tf_op jit(solution)/shard_map/ppermute | solution.py:639
  32.8 0.0 copy-done
  32.8 0.0 copy-done.2
  32.8 0.0 copy-done.3
  32.8 0.0 copy-done.5
  32.8 0.0 copy-done.8
  32.9 2.3 %shard_map.131 = (f32[1152,128]{1,0:T(8,128)S(1)}, bf16[1152,128]{1,0:T(8,128)(2,1)S(1)}, f32[512,128]{1,0:T(8,128)S(1)}, bf16[1152,128]{1,0:T(8,128)(2,1)S(1)}, bf16[1152,128]{1,0:T(8,128)(2,1)S(1)}) custom-call(s32[4,12]{1,0:T(4,128)S(1)} %bitcast.13, s32[48,8]{1,0:T(8,128)S(1)} %copy-done.5, f32[72,64]{1,0:T(8,128)S(1)} %copy-done.3, ...), custom_call_target="tpu_custom_call" | custom-call | tf_op jit(solution)/shard_map/pallas_call | solution.py:41
  35.1 0.0 collective-permute-done.1.refs_0_
  35.1 0.9 %collective-permute-start.2 = (bf16[6,48,128]{2,1,0:T(8,128)(2,1)S(1)}, bf16[6,48,128]{2,1,0:T(8,128)(2,1)S(1)}, u32[]{:S(2)}, u32[]{:S(2)}) collective-permute-start(bf16[6,48,128]{2,1,0:T(8,128)(2,1)S(1)} %shard_map.133.refs_2_.two_ref), channel_id=1, source_target_pairs={{0,1},{1,0},{2,3},{3,2},{4,5},{5,4},{6,7},{7,6},{8,9},{9,8},{10,11... | collective-permute-start | bytes 221192 | tf_op jit(solution)/shard_map/ppermute | solution.py:639
  36.0 0.0 collective-permute-done.refs_1_.one_ref
  36.0 0.9 %collective-permute-done.2.refs_3_.three_ref = bf16[6,48,128]{2,1,0:T(8,128)(2,1)S(1)} collective-permute-done((bf16[6,48,128]{2,1,0:T(8,128)(2,1)S(1)}, bf16[6,48,128]{2,1,0:T(8,128)(2,1)S(1)}, u32[]{:S(2)}, u32[]{:S(2)}) %collective-permute-start.2) | collective-permute-done | bytes 73760 | tf_op jit(solution)/shard_map/ppermute | solution.py:639
  37.0 0.4 collective-permute-start.3
  37.3 3.3 %shard_map.135 = (f32[1152,128]{1,0:T(8,128)S(1)}, f32[72,128]{1,0:T(8,128)S(1)}) custom-call(s32[4,12]{1,0:T(4,128)S(1)} %bitcast.7, s32[4,12]{1,0:T(4,128)S(1)} %bitcast.11, s32[4,12]{1,0:T(4,128)S(1)} %bitcast.14, s32[48,8]{1,0:T(8,128)S(1)} %copy-done.5, f32[72,64]{1,0:T(8,128)S(1)} %copy-done.3, bf16[6,48,128]{2,1,0:T(8,128)(2,1)S(1)} %shard_map.132.own_ref, ...), custom_call_target="tpu_custom_call" | custom-call | tf_op jit(solution)/shard_map/pallas_call | solution.py:41
  40.6 0.0 collective-permute-done.3.other_ref
  40.6 0.2 shard_map.136
  40.8 14.4 %all_to_all.16.in_ref = bf16[32,40,128]{2,1,0:T(8,128)(2,1)S(1)} all-to-all(bf16[32,40,128]{2,1,0:T(8,128)(2,1)S(1)} %shard_map.136), channel_id=1, replica_groups=mesh['tile'=32,'sub'=4] {'tile'}, dimensions={0} | all-to-all | bytes 655360 | tf_op jit(solution)/shard_map/all_to_all | solution.py:712
  55.3 0.0 copy-start.4
  55.3 0.1 shard_map.137.refs_1_
  55.3 0.8 %collective-permute-start.4 = (f32[40,128]{1,0:T(8,128)S(1)}, f32[40,128]{1,0:T(8,128)S(1)}, u32[]{:S(2)}, u32[]{:S(2)}) collective-permute-start(f32[40,128]{1,0:T(8,128)S(1)} %shard_map.137.refs_1_), channel_id=1, source_target_pairs={{0,2},{1,3},{2,0},{3,1},{4,6},{5,7},{6,4},{7,5},{8,10},{9,11},{10,... | collective-permute-start | bytes 61448 | tf_op jit(solution)/shard_map/ppermute | solution.py:639
  56.1 1.9 %collective-permute-done.4.refs_2_ = f32[40,128]{1,0:T(8,128)S(1)} collective-permute-done((f32[40,128]{1,0:T(8,128)S(1)}, f32[40,128]{1,0:T(8,128)S(1)}, u32[]{:S(2)}, u32[]{:S(2)}) %collective-permute-start.4) | collective-permute-done | bytes 20512 | tf_op jit(solution)/shard_map/ppermute | solution.py:639
  58.0 0.0 copy-done.4
  58.1 15.3 %all_to_all.17.in_ref = bf16[32,80,128]{2,1,0:T(8,128)(2,1)S(1)} all-to-all(bf16[32,80,128]{2,1,0:T(8,128)(2,1)S(1)} %shard_map.138), channel_id=1, replica_groups=mesh['tile'=32,'sub'=4] {'tile'}, dimensions={0} | all-to-all | bytes 1310720 | tf_op jit(solution)/shard_map/all_to_all | solution.py:721
  73.4 0.1 shard_map.140.own_ref
  73.4 3.9 %collective-permute-start.5 = (bf16[32,40,128]{2,1,0:T(8,128)(2,1)S(1)}, bf16[32,40,128]{2,1,0:T(8,128)(2,1)S(1)}, u32[]{:S(2)}, u32[]{:S(2)}) collective-permute-start(bf16[32,40,128]{2,1,0:T(8,128)(2,1)S(1)} %shard_map.140.own_ref), channel_id=1, source_target_pairs={{0,1},{1,0},{2,3},{3,2},{4,5},{5,4},{6,7},{7,6},{8,9},{9,8},{10,11... | collective-permute-start | bytes 983048 | tf_op jit(solution)/shard_map/ppermute | solution.py:639
  77.3 1.1 %shard_map.139 = bf16[3,2,64,128]{3,2,1,0:T(8,128)(2,1)} custom-call(s32[4,12]{1,0:T(4,128)S(1)} %bitcast.8, s32[4,12]{1,0:T(4,128)S(1)} %bitcast.12, bf16[2,64,64]{2,1,0:T(8,128)(2,1)S(1)} %copy-done.4, bf16[32,80,128]{2,1,0:T(8,128)(2,1)S(1)} %all_to_all.17.in_ref), custom_call_target="tpu_custom_call" | custom-call | tf_op jit(solution)/shard_map/pallas_call | solution.py:41
  78.4 0.2 collective-permute-done.5.other_ref
  78.5 1.1 %shard_map.141 = (f32[1152,128]{1,0:T(8,128)}, f32[1152,128]{1,0:T(8,128)}) custom-call(bf16[32,40,128]{2,1,0:T(8,128)(2,1)S(1)} %shard_map.140.own_ref, bf16[32,40,128]{2,1,0:T(8,128)(2,1)S(1)} %collective-permute-done.5.other_ref), custom_call_target="tpu_custom_call" | custom-call | tf_op jit(solution)/shard_map/pallas_call | solution.py:41
  (3 shorter events, 0.1 us)
Async XLA Ops:
  1.8 26.7 %copy-start.1 = (bf16[2,288,432]{2,1,0:T(8,128)(2,1)S(1)}, bf16[2,288,432]{2,1,0:T(8,128)(2,1)}, u32[]{:S(2)}) copy-start(bf16[2,288,432]{2,1,0:T(8,128)(2,1)} %constant.8.clone.sel_ref) | copy-start | bytes 1492996
  1.8 26.7 %copy-start.6 = (s32[12,4]{0,1:T(4,128)S(1)}, s32[12,4]{0,1:T(4,128)}, u32[]{:S(2)}) copy-start(s32[12,4]{0,1:T(4,128)} %param.15) | copy-start | bytes 580
  1.8 26.7 %copy-start.7 = (s32[12,4]{0,1:T(4,128)S(1)}, s32[12,4]{0,1:T(4,128)}, u32[]{:S(2)}) copy-start(s32[12,4]{0,1:T(4,128)} %param.16) | copy-start | bytes 580
  28.5 4.3 %copy-start = (bf16[3,3,128,128]{3,2,1,0:T(8,128)(2,1)S(1)}, bf16[3,3,128,128]{3,2,1,0:T(8,128)(2,1)}, u32[]{:S(2)}) copy-start(bf16[3,3,128,128]{3,2,1,0:T(8,128)(2,1)} %w1_ref.3) | copy-start | bytes 884740
  28.5 4.3 %copy-start.2 = (bf16[3,3,128,128]{3,2,1,0:T(8,128)(2,1)S(1)}, bf16[3,3,128,128]{3,2,1,0:T(8,128)(2,1)}, u32[]{:S(2)}) copy-start(bf16[3,3,128,128]{3,2,1,0:T(8,128)(2,1)} %w2_ref.1) | copy-start | bytes 884740
  28.6 4.3 %copy-start.3 = (f32[72,64]{1,0:T(8,128)S(1)}, f32[72,64]{1,0:T(8,128)}, u32[]{:S(2)}) copy-start(f32[72,64]{1,0:T(8,128)} %constant.10.clone._select.sel_ref) | copy-start | bytes 55300
  28.6 4.3 %copy-start.5 = (s32[48,8]{1,0:T(8,128)S(1)}, s32[48,8]{1,0:T(8,128)}, u32[]{:S(2)}) copy-start(s32[48,8]{1,0:T(8,128)} %constant.9.clone._plan.plan_ref) | copy-start | bytes 4612
  28.6 4.3 %copy-start.8 = (s32[12,4]{0,1:T(4,128)S(1)}, s32[12,4]{0,1:T(4,128)}, u32[]{:S(2)}) copy-start(s32[12,4]{0,1:T(4,128)} %param.17) | copy-start | bytes 580
  28.9 6.2 %collective-permute-start.1 = (bf16[6,48,128]{2,1,0:T(8,128)(2,1)S(1)}, bf16[6,48,128]{2,1,0:T(8,128)(2,1)S(1)}, u32[]{:S(2)}, u32[]{:S(2)}) collective-permute-start(bf16[6,48,128]{2,1,0:T(8,128)(2,1)S(1)} %shard_map.132.own_ref), channel_id=1, source_target_pairs={{0,2},{1,3},{2,0},{3,1},{4,6},{5,7},{6,4},{7,5},{8,10},{9,11},{10,... | collective-permute-start | bytes 221192 | tf_op jit(solution)/shard_map/ppermute | solution.py:639
  29.7 6.3 %collective-permute-start = (bf16[6,48,128]{2,1,0:T(8,128)(2,1)S(1)}, bf16[6,48,128]{2,1,0:T(8,128)(2,1)S(1)}, u32[]{:S(2)}, u32[]{:S(2)}) collective-permute-start(bf16[6,48,128]{2,1,0:T(8,128)(2,1)S(1)} %shard_map.132.own_ref), channel_id=1, source_target_pairs={{0,1},{1,0},{2,3},{3,2},{4,5},{5,4},{6,7},{7,6},{8,9},{9,8},{10,11... | collective-permute-start | bytes 221192 | tf_op jit(solution)/shard_map/ppermute | solution.py:639
  35.1 1.8 %collective-permute-start.2 = (bf16[6,48,128]{2,1,0:T(8,128)(2,1)S(1)}, bf16[6,48,128]{2,1,0:T(8,128)(2,1)S(1)}, u32[]{:S(2)}, u32[]{:S(2)}) collective-permute-start(bf16[6,48,128]{2,1,0:T(8,128)(2,1)S(1)} %shard_map.133.refs_2_.two_ref), channel_id=1, source_target_pairs={{0,1},{1,0},{2,3},{3,2},{4,5},{5,4},{6,7},{7,6},{8,9},{9,8},{10,11... | collective-permute-start | bytes 221192 | tf_op jit(solution)/shard_map/ppermute | solution.py:639
  37.0 3.7 %collective-permute-start.3 = (bf16[1152,128]{1,0:T(8,128)(2,1)S(1)}, bf16[1152,128]{1,0:T(8,128)(2,1)S(1)}, u32[]{:S(2)}, u32[]{:S(2)}) collective-permute-start(bf16[1152,128]{1,0:T(8,128)(2,1)S(1)} %shard_map.134), channel_id=1, source_target_pairs={{0,1},{1,0},{2,3},{3,2},{4,5},{5,4},{6,7},{7,6},{8,9},{9,8},{10,11... | collective-permute-start | bytes 884744 | tf_op jit(solution)/shard_map/ppermute | solution.py:639
  55.3 2.8 %copy-start.4 = (bf16[2,64,64]{2,1,0:T(8,128)(2,1)S(1)}, bf16[2,64,64]{2,1,0:T(8,128)(2,1)}, u32[]{:S(2)}) copy-start(bf16[2,64,64]{2,1,0:T(8,128)(2,1)} %constant.11.clone.refs_0_.sel_ref) | copy-start | bytes 49156
  55.3 2.7 %collective-permute-start.4 = (f32[40,128]{1,0:T(8,128)S(1)}, f32[40,128]{1,0:T(8,128)S(1)}, u32[]{:S(2)}, u32[]{:S(2)}) collective-permute-start(f32[40,128]{1,0:T(8,128)S(1)} %shard_map.137.refs_1_), channel_id=1, source_target_pairs={{0,2},{1,3},{2,0},{3,1},{4,6},{5,7},{6,4},{7,5},{8,10},{9,11},{10,... | collective-permute-start | bytes 61448 | tf_op jit(solution)/shard_map/ppermute | solution.py:639
  73.4 5.1 %collective-permute-start.5 = (bf16[32,40,128]{2,1,0:T(8,128)(2,1)S(1)}, bf16[32,40,128]{2,1,0:T(8,128)(2,1)S(1)}, u32[]{:S(2)}, u32[]{:S(2)}) collective-permute-start(bf16[32,40,128]{2,1,0:T(8,128)(2,1)S(1)} %shard_map.140.own_ref), channel_id=1, source_target_pairs={{0,1},{1,0},{2,3},{3,2},{4,5},{5,4},{6,7},{7,6},{8,9},{9,8},{10,11... | collective-permute-start | bytes 983048 | tf_op jit(solution)/shard_map/ppermute | solution.py:639
